TPU v7x, 32 devices: a whole 2x2x4 slice. The times are simulated.
32 devices in a mesh: section: 2 (over core), ctx: 4 (over y, x), mp: 4 (over z).
Axes of the slice: x: 2, y: 2, z: 4, core: 2. Of those that a mesh axis runs over, the one named last changes fastest.
Arguments:
- section_input: bfloat16 [2, 2048, 2048], P(None, ('ctx', 'mp')), may hold values from -6 to 6
- cotangent: float32 [2, 2048, 2048], P(None, ('ctx', 'mp')), may hold values from -6 to 6
- pair_owner: int32 [2, 2, 4], replicated, may hold values from 0 to 3, each once within a row
- attn_gain: bfloat16 [2, 2048], P('section'), may hold values from 0.5 to 1.5
- w_query: bfloat16 [2, 2048, 2048], P('section', None, 'mp'), may hold values from -0.125 to 0.125
- w_key: bfloat16 [2, 2048, 1024], P('section', None, 'mp'), may hold values from -0.125 to 0.125
- w_value: bfloat16 [2, 2048, 1024], P('section', None, 'mp'), may hold values from -0.125 to 0.125
- query_gain: bfloat16 [2, 128], P('section'), may hold values from 0.099609375 to 1.8984375
- key_gain: bfloat16 [2, 128], P('section'), may hold values from 0.099609375 to 1.8984375
- w_output: bfloat16 [2, 2048, 2048], P('section', 'mp'), may hold values from -0.75 to 0.75
- mlp_gain: bfloat16 [2, 2048], P('section'), may hold values from 0.5 to 1.5
- w_gate: bfloat16 [2, 2048, 6144], P('section', None, 'mp'), may hold values from -0.125 to 0.125
- w_up: bfloat16 [2, 2048, 6144], P('section', None, 'mp'), may hold values from -0.125 to 0.125
- w_down: bfloat16 [2, 6144, 2048], P('section', 'mp'), may hold values from -0.078125 to 0.078125
Outputs:
- section_outputs: float32 [2, 2, 2048, 2048], P('section', None, ('ctx', 'mp'))
- input_grads: float32 [2, 2, 2048, 2048], P('section', None, ('ctx', 'mp'))
- attn_gain_grad: float32 [2, 2048], P('section')
- w_query_grad: float32 [2, 2048, 2048], P('section', None, 'mp')
- w_key_grad: float32 [2, 2048, 1024], P('section', None, 'mp')
- w_value_grad: float32 [2, 2048, 1024], P('section', None, 'mp')
- query_gain_grad: float32 [2, 128], P('section')
- key_gain_grad: float32 [2, 128], P('section')
- w_output_grad: float32 [2, 2048, 2048], P('section', 'mp')
- mlp_gain_grad: float32 [2, 2048], P('section')
- w_gate_grad: float32 [2, 2048, 6144], P('section', None, 'mp')
- w_up_grad: float32 [2, 2048, 6144], P('section', None, 'mp')
- w_down_grad: float32 [2, 6144, 2048], P('section', 'mp')
Inputs may be any that keep to these rules, and one draw needn't show every extreme that they name: `pair_owner`: for each micro-batch and sequence, every ctx index appears once.
All inputs are finite; a program needn't handle non-finite values.
Results may differ from a plain program's by a relative error of at most 0.04.
Values may be sent and summed in bfloat16 or wider, within the bound.
No kernel may reach another device: no remote copies, remote signals or barrier semaphores. Data moves between devices by JAX's collectives and lax.ppermute only.
A program may use at most 320 MiB of HBM per device.

v0:
```python
import jax
import jax.numpy as jnp
from jax import lax
from jax.sharding import PartitionSpec as P

D = 2048
HD = 128
MB = 2
SEQS = 2
TOK_CTX = 512
STRETCH = 128


EPSILON = 1e-06
ROPE_BASE = 1000000.0
MASKED_SCORE = -1e30


def from_partner(block, axis, distance):
    count = lax.axis_size(axis)
    route = []
    for low in range(count):
        high = low | 1 << distance
        if high != low and high < count:
            route += [(low, high), (high, low)]
    return lax.ppermute(block, axis, route)


def row_norm(token_rows, gain_vec):
    scaling = lax.rsqrt(jnp.mean(token_rows * token_rows, axis=-1, keepdims=True) + EPSILON)
    return token_rows * scaling * gain_vec


def rotate(head_split, cosine, sine):
    half_width = head_split.shape[-1] // 2
    front_half = head_split[..., :half_width]
    back_half = head_split[..., half_width:]
    return jnp.concatenate(
        [front_half * cosine - back_half * sine, back_half * cosine + front_half * sine], axis=-1
    )


def head_prep(flat_rows, gain_vec, cosine, sine):
    row_count = flat_rows.shape[0]
    head_split = flat_rows.reshape(row_count, flat_rows.shape[1] // HD, HD)
    normed = row_norm(head_split, gain_vec)
    return rotate(normed, cosine[:, None, :], sine[:, None, :]).reshape(
        row_count, flat_rows.shape[1]
    )


def rope_tables(positions):
    inv_freq = ROPE_BASE ** (-jnp.arange(0, HD, 2).astype(jnp.float32) / HD)
    angles = positions.astype(jnp.float32)[:, None] * inv_freq[None, :]
    return (jnp.cos(angles), jnp.sin(angles))


def block_positions(stretch_owner, devices, n_ctx):
    matches = devices[:, None] == jnp.arange(n_ctx, dtype=jnp.int32)[None, :]
    held_block = jnp.sum(jnp.where(matches[:, None, :], stretch_owner[None, :, :], 0), axis=-1)
    offsets = jnp.arange(STRETCH, dtype=jnp.int32)
    lower_pos = held_block[:, :, None] * STRETCH + offsets[None, None, :]
    upper_pos = (2 * n_ctx - 1 - held_block)[:, :, None] * STRETCH + offsets[None, None, :]
    return jnp.concatenate([lower_pos, upper_pos], axis=-1)


def key_positions(stretch_owner, first_device, blocks, n_ctx):
    devices = first_device + jnp.arange(blocks, dtype=jnp.int32)
    places = block_positions(stretch_owner, devices, n_ctx)
    return jnp.transpose(places, (1, 0, 2)).reshape(SEQS, blocks * 2 * STRETCH)


def other_section(token_rows):
    return from_partner(token_rows.astype(jnp.bfloat16), "section", 0).astype(token_rows.dtype)


def spread_rows(token_rows):
    return lax.all_gather(token_rows, "mp", axis=0, tiled=True)


def gather_grads(token_rows):
    return lax.all_gather(token_rows, "mp", axis=0, tiled=True)


def row_sums(left_side, weight, weight_dim):
    return lax.psum_scatter(
        lax.dot_general(
            left_side, weight, (((1,), (weight_dim,)), ((), ())), preferred_element_type=jnp.float32
        ).astype(jnp.bfloat16),
        "mp",
        scatter_dimension=0,
        tiled=True,
    ).astype(jnp.float32)


def attend_fold(carry, piece, start, queries, query_pos, stretch_owner, n_ctx):
    run_top, totals, running = carry
    key_rows, value_rows = piece
    blocks = key_rows.shape[0] // TOK_CTX
    kv_local = key_rows.shape[1] // HD
    groups = queries.shape[3]
    block_span = 2 * STRETCH
    keys_five = key_rows.reshape(blocks, SEQS, block_span, kv_local, HD)
    values_five = value_rows.reshape(blocks, SEQS, block_span, kv_local, HD)
    key_pos = key_positions(stretch_owner, start // TOK_CTX, blocks, n_ctx)
    scores = jnp.einsum(
        "sqhgd,nsjhd->shgqnj", queries, keys_five, preferred_element_type=jnp.float32
    )
    scores = scores.reshape(SEQS, kv_local, groups, block_span, blocks * block_span) * HD ** (-0.5)
    allowed = key_pos[:, None, None, None, :] <= query_pos[:, None, None, :, None]
    masked = jnp.where(allowed, scores, MASKED_SCORE)
    new_top = jnp.maximum(run_top, jnp.max(masked, axis=-1))
    weights = jnp.where(allowed, jnp.exp(masked - new_top[..., None]), 0.0)
    totals = jnp.sum(weights, axis=-1)
    weights_low = weights.astype(jnp.bfloat16).reshape(
        SEQS, kv_local, groups, block_span, blocks, block_span
    )
    running = jnp.einsum(
        "shgqnj,nsjhd->shgqd", weights_low, values_five, preferred_element_type=jnp.float32
    )
    return (new_top, totals, running)


def attend_back(
    queries,
    key_rows,
    value_rows,
    query_pos,
    stretch_owner,
    n_ctx,
    log_total,
    attended,
    grad_attended,
):
    blocks = key_rows.shape[0] // TOK_CTX
    kv_local = key_rows.shape[1] // HD
    groups = queries.shape[3]
    block_span = 2 * STRETCH
    scaling = HD ** (-0.5)
    keys_five = key_rows.reshape(blocks, SEQS, block_span, kv_local, HD)
    values_five = value_rows.reshape(blocks, SEQS, block_span, kv_local, HD)
    key_pos = key_positions(stretch_owner, 0, blocks, n_ctx)
    shape_full = (SEQS, kv_local, groups, block_span, blocks * block_span)
    split_shape = (SEQS, kv_local, groups, block_span, blocks, block_span)
    scores = (
        jnp.einsum(
            "sqhgd,nsjhd->shgqnj", queries, keys_five, preferred_element_type=jnp.float32
        ).reshape(shape_full)
        * scaling
    )
    allowed = key_pos[:, None, None, None, :] <= query_pos[:, None, None, :, None]
    probs = jnp.exp(jnp.where(allowed, scores - log_total[..., None], MASKED_SCORE))
    grad_five = grad_attended.reshape(SEQS, block_span, kv_local, groups, HD)
    grad_probs = jnp.einsum(
        "sqhgd,nsjhd->shgqnj", grad_five, values_five, preferred_element_type=jnp.float32
    ).reshape(shape_full)
    attended_five = attended.reshape(SEQS, block_span, kv_local, groups, HD)
    row_delta = jnp.transpose(
        jnp.sum(grad_five.astype(jnp.float32) * attended_five, axis=-1), (0, 2, 3, 1)
    )
    grad_scores = (
        (probs * (grad_probs - row_delta[..., None])).astype(jnp.bfloat16).reshape(split_shape)
    )
    probs_low = probs.astype(jnp.bfloat16).reshape(split_shape)
    grad_queries = (
        jnp.einsum(
            "shgqnj,nsjhd->sqhgd", grad_scores, keys_five, preferred_element_type=jnp.float32
        )
        * scaling
    )
    grad_keys = (
        jnp.einsum("shgqnj,sqhgd->nsjhd", grad_scores, queries, preferred_element_type=jnp.float32)
        * scaling
    )
    grad_values = jnp.einsum(
        "shgqnj,sqhgd->nsjhd", probs_low, grad_five, preferred_element_type=jnp.float32
    )
    rows_all = blocks * TOK_CTX
    key_terms = jnp.concatenate(
        [grad_keys.reshape(rows_all, kv_local * HD), grad_values.reshape(rows_all, kv_local * HD)],
        axis=1,
    )
    return (grad_queries.reshape(TOK_CTX, kv_local * groups * HD), key_terms)


def section_forward(token_rows, stretch_owner, params, n_ctx):
    attn_gain, w_qkv, query_gain, key_gain, w_out, mlp_gain, w_gate_up, w_down = params
    q_width = w_out.shape[0]
    kv_width = (w_qkv.shape[1] - q_width) // 2
    kv_local = kv_width // HD
    groups = q_width // kv_width
    block_span = 2 * STRETCH
    ctx_place = jnp.reshape(lax.axis_index("ctx"), (1,))
    query_pos = block_positions(stretch_owner, ctx_place, n_ctx)[0]
    cosine, sine = rope_tables(query_pos.reshape(TOK_CTX))
    attn_in = spread_rows(row_norm(token_rows, attn_gain.astype(jnp.float32)).astype(jnp.bfloat16))
    mixed_proj = jnp.dot(attn_in, w_qkv, preferred_element_type=jnp.float32)
    q_proj = mixed_proj[:, :q_width]
    k_proj = mixed_proj[:, q_width : q_width + kv_width]
    values = mixed_proj[:, q_width + kv_width :].astype(jnp.bfloat16)
    queries = head_prep(q_proj, query_gain.astype(jnp.float32), cosine, sine).astype(jnp.bfloat16)
    key_rows = head_prep(k_proj, key_gain.astype(jnp.float32), cosine, sine).astype(jnp.bfloat16)
    queries_five = queries.reshape(SEQS, block_span, kv_local, groups, HD)
    state_shape = (SEQS, kv_local, groups, block_span)
    init_carry = (
        jnp.full(state_shape, MASKED_SCORE, jnp.float32),
        jnp.zeros(state_shape, jnp.float32),
        jnp.zeros(state_shape + (HD,), jnp.float32),
    )
    kept_state = {}
    run_top, totals, running = attend_fold(
        init_carry,
        (
            lax.all_gather(key_rows, "ctx", axis=0, tiled=True),
            lax.all_gather(values, "ctx", axis=0, tiled=True),
        ),
        jnp.int32(0),
        queries_five,
        query_pos,
        stretch_owner,
        n_ctx,
    )
    attended = jnp.transpose(running / totals[..., None], (0, 3, 1, 2, 4)).reshape(TOK_CTX, q_width)
    log_total = run_top + jnp.log(totals)
    attended_low = attended.astype(jnp.bfloat16)
    mid_rows = token_rows + row_sums(attended_low, w_out, 0)
    mlp_in = spread_rows(row_norm(mid_rows, mlp_gain.astype(jnp.float32)).astype(jnp.bfloat16))
    gate_up = jnp.dot(mlp_in, w_gate_up, preferred_element_type=jnp.float32)
    ff_local = w_down.shape[0]
    gate_pre = gate_up[:, :ff_local]
    up_pre = gate_up[:, ff_local:]
    hidden = (jax.nn.silu(gate_pre) * up_pre).astype(jnp.bfloat16)
    result = mid_rows + row_sums(hidden, w_down, 0)
    kept_state["token_rows"] = token_rows
    kept_state["mid_rows"] = mid_rows
    kept_state["attn_in"] = attn_in
    kept_state["q_proj"] = q_proj
    kept_state["k_proj"] = k_proj
    kept_state["queries"] = queries
    kept_state["key_rows"] = key_rows
    kept_state["values"] = values
    kept_state["attended"] = attended
    kept_state["attended_low"] = attended_low
    kept_state["log_total"] = log_total
    kept_state["mlp_in"] = mlp_in
    kept_state["gate_pre"] = gate_pre
    kept_state["up_pre"] = up_pre
    kept_state["hidden"] = hidden
    kept_state["stretch_owner"] = stretch_owner
    kept_state["query_pos"] = query_pos
    kept_state["cosine"] = cosine
    kept_state["sine"] = sine
    return (result, kept_state)


def section_backward(grad_out, kept_state, params, n_ctx):
    attn_gain, w_qkv, query_gain, key_gain, w_out, mlp_gain, w_gate_up, w_down = params
    q_width = w_out.shape[0]
    kv_width = (w_qkv.shape[1] - q_width) // 2
    kv_local = kv_width // HD
    groups = q_width // kv_width
    block_span = 2 * STRETCH
    contract_rows = (((0,), (0,)), ((), ()))
    contract_cols = (((1,), (1,)), ((), ()))
    branch_whole = gather_grads(grad_out.astype(jnp.bfloat16))
    grad_hidden = lax.dot_general(
        branch_whole, w_down, contract_cols, preferred_element_type=jnp.float32
    )
    grad_down = lax.dot_general(
        kept_state["hidden"], branch_whole, contract_rows, preferred_element_type=jnp.float32
    )
    gate_pre = kept_state["gate_pre"]
    sigmoid_gate = jax.nn.sigmoid(gate_pre)
    grad_gate = (
        grad_hidden * kept_state["up_pre"] * sigmoid_gate * (1.0 + gate_pre * (1.0 - sigmoid_gate))
    )
    grad_up = grad_hidden * gate_pre * sigmoid_gate
    grad_both = jnp.concatenate([grad_gate, grad_up], axis=1).astype(jnp.bfloat16)
    grad_gate_up = lax.dot_general(
        kept_state["mlp_in"], grad_both, contract_rows, preferred_element_type=jnp.float32
    )
    grad_mlp_in = row_sums(grad_both, w_gate_up, 1)
    unused_mlp, pull_mlp = jax.vjp(row_norm, kept_state["mid_rows"], mlp_gain.astype(jnp.float32))
    grad_mid_norm, grad_mlp_gain = pull_mlp(grad_mlp_in)
    grad_mid = grad_out + grad_mid_norm
    attn_whole = gather_grads(grad_mid.astype(jnp.bfloat16))
    grad_attended = lax.dot_general(
        attn_whole, w_out, contract_cols, preferred_element_type=jnp.float32
    ).astype(jnp.bfloat16)
    grad_output = lax.dot_general(
        kept_state["attended_low"], attn_whole, contract_rows, preferred_element_type=jnp.float32
    )
    keys_all, values_all = (
        lax.all_gather(kept_state["key_rows"], "ctx", axis=0, tiled=True),
        lax.all_gather(kept_state["values"], "ctx", axis=0, tiled=True),
    )
    queries_five = kept_state["queries"].reshape(SEQS, block_span, kv_local, groups, HD)
    grad_queries, key_terms = attend_back(
        queries_five,
        keys_all,
        values_all,
        kept_state["query_pos"],
        kept_state["stretch_owner"],
        n_ctx,
        kept_state["log_total"],
        kept_state["attended"],
        grad_attended,
    )
    key_grads = lax.psum_scatter(
        key_terms.astype(jnp.bfloat16), "ctx", scatter_dimension=0, tiled=True
    ).astype(jnp.float32)
    grad_keys = key_grads[:, :kv_width]
    grad_values = key_grads[:, kv_width:]
    cosine = kept_state["cosine"]
    sine = kept_state["sine"]

    def prep_local(flat_rows, gain_vec):
        return head_prep(flat_rows, gain_vec, cosine, sine)

    unused_query, pull_query = jax.vjp(
        prep_local, kept_state["q_proj"], query_gain.astype(jnp.float32)
    )
    grad_q_proj, grad_query_gain = pull_query(grad_queries)
    unused_key, pull_key = jax.vjp(prep_local, kept_state["k_proj"], key_gain.astype(jnp.float32))
    grad_k_proj, grad_key_gain = pull_key(grad_keys)
    grad_mixed = jnp.concatenate([grad_q_proj, grad_k_proj, grad_values], axis=1).astype(
        jnp.bfloat16
    )
    grad_qkv = lax.dot_general(
        kept_state["attn_in"], grad_mixed, contract_rows, preferred_element_type=jnp.float32
    )
    grad_attn_in = row_sums(grad_mixed, w_qkv, 1)
    unused_attn, pull_attn = jax.vjp(
        row_norm, kept_state["token_rows"], attn_gain.astype(jnp.float32)
    )
    grad_rows_norm, grad_attn_gain = pull_attn(grad_attn_in)
    grad_in = grad_mid + grad_rows_norm
    return (
        grad_in,
        (grad_qkv, grad_output, grad_gate_up, grad_down),
        (grad_attn_gain, grad_query_gain, grad_key_gain, grad_mlp_gain),
    )


def shards(
    section_input,
    cotangent,
    pair_owner,
    attn_gain,
    w_query,
    w_key,
    w_value,
    query_gain,
    key_gain,
    w_output,
    mlp_gain,
    w_gate,
    w_up,
    w_down,
):
    n_ctx = lax.axis_size("ctx")
    is_first = lax.axis_index("section") == 0
    params = (
        attn_gain[0],
        jnp.concatenate([w_query[0], w_key[0], w_value[0]], axis=1),
        query_gain[0],
        key_gain[0],
        w_output[0],
        mlp_gain[0],
        jnp.concatenate([w_gate[0], w_up[0]], axis=1),
        w_down[0],
    )
    rows_here = section_input.shape[1]
    incoming = jnp.zeros((rows_here, D), jnp.float32)
    results = []
    kept_ticks = []
    for step_index in range(MB + 1):
        own_input = section_input[min(step_index, MB - 1)].astype(jnp.float32)
        stretch_owner = jnp.where(
            is_first, pair_owner[min(step_index, MB - 1)], pair_owner[max(step_index - 1, 0)]
        )
        token_rows = jnp.where(is_first, own_input, incoming)
        result, kept_state = section_forward(token_rows, stretch_owner, params, n_ctx)
        results.append(result)
        kept_ticks.append(kept_state)
        if step_index < MB:
            incoming = other_section(result)
    section_outputs = jnp.stack(
        [
            jnp.where(is_first, results[micro_index], results[micro_index + 1])
            for micro_index in range(MB)
        ]
    )[None]
    grad_back = jnp.zeros((rows_here, D), jnp.float32)
    grads_in = []
    matrix_sums = None
    gain_sums = None
    for step_index in range(MB + 1):
        kept_state = jax.tree.map(
            lambda early_one, later_one: jnp.where(is_first, early_one, later_one),
            kept_ticks[max(step_index - 1, 0)],
            kept_ticks[min(step_index + 1, MB)],
        )
        grad_out = jnp.where(is_first, grad_back, cotangent[min(step_index, MB - 1)])
        live_flag = jnp.where(is_first, step_index >= 1, step_index < MB).astype(jnp.float32)
        grad_in, matrices, gains = section_backward(grad_out, kept_state, params, n_ctx)
        grad_qkv, grad_output, grad_gate_up, grad_down = tuple(
            (live_flag * matrix for matrix in matrices)
        )
        gains = tuple((live_flag * gain_vec for gain_vec in gains))
        matrices = (grad_qkv, grad_output, grad_gate_up, grad_down)
        if step_index == 0:
            matrix_sums = matrices
            gain_sums = gains
        else:
            matrix_sums = tuple((summed + added for summed, added in zip(matrix_sums, matrices)))
            gain_sums = tuple((summed + added for summed, added in zip(gain_sums, gains)))
        grads_in.append(grad_in)
        if step_index < MB:
            grad_back = other_section(grad_in)
    input_grads = jnp.stack(
        [
            jnp.where(is_first, grads_in[micro_index + 1], grads_in[micro_index])
            for micro_index in range(MB)
        ]
    )[None]
    sum_qkv, sum_output, sum_gate_up, sum_down = matrix_sums
    sum_qkv, sum_output, sum_gate_up, sum_down = (
        lax.psum(sum_qkv.astype(jnp.bfloat16), "ctx").astype(jnp.float32),
        lax.psum(sum_output.astype(jnp.bfloat16), "ctx").astype(jnp.float32),
        lax.psum(sum_gate_up.astype(jnp.bfloat16), "ctx").astype(jnp.float32),
        lax.psum(sum_down.astype(jnp.bfloat16), "ctx").astype(jnp.float32),
    )
    gain_attn, gain_query, gain_key, gain_mlp = gain_sums
    gain_attn, gain_query, gain_key, gain_mlp = lax.psum(
        (gain_attn, gain_query, gain_key, gain_mlp), ("ctx", "mp")
    )
    q_width = w_query.shape[2]
    kv_width = w_key.shape[2]
    ff_local = w_gate.shape[2]
    return (
        section_outputs,
        input_grads,
        gain_attn[None],
        sum_qkv[:, :q_width][None],
        sum_qkv[:, q_width : q_width + kv_width][None],
        sum_qkv[:, q_width + kv_width :][None],
        gain_query[None],
        gain_key[None],
        sum_output[None],
        gain_mlp[None],
        sum_gate_up[:, :ff_local][None],
        sum_gate_up[:, ff_local:][None],
        sum_down[None],
    )


def solution(mesh):
    in_specs = (
        P(None, ("ctx", "mp"), None),
        P(None, ("ctx", "mp"), None),
        P(),
        P("section", None),
        P("section", None, "mp"),
        P("section", None, "mp"),
        P("section", None, "mp"),
        P("section", None),
        P("section", None),
        P("section", "mp", None),
        P("section", None),
        P("section", None, "mp"),
        P("section", None, "mp"),
        P("section", "mp", None),
    )
    out_specs = (
        P("section", None, ("ctx", "mp"), None),
        P("section", None, ("ctx", "mp"), None),
        P("section", None),
        P("section", None, "mp"),
        P("section", None, "mp"),
        P("section", None, "mp"),
        P("section", None),
        P("section", None),
        P("section", "mp", None),
        P("section", None),
        P("section", None, "mp"),
        P("section", None, "mp"),
        P("section", "mp", None),
    )
    return jax.shard_map(shards, mesh=mesh, in_specs=in_specs, out_specs=out_specs, check_vma=False)
```

profile of v0, /device:TPU:0, one launch (start us, length us, event | category | flops | bytes accessed | tf_op | source)
XLA Modules:
  0.0 2434.2 jit_solution(5191637729796308873)
XLA Ops:
  20.7 39.4 %all-gather.25.cloned.1.call-done = bf16[512,2048]{1,0:T(8,128)(2,1)} async-done(((bf16[128,2048]{1,0:T(8,128)(2,1)}), bf16[512,2048]{1,0:T(8,128)(2,1)}) %all-gather.25.cloned.1.call-update) | async-done | bytes 2097168 | tf_op jit(solution)/shard_map/all_gather | solution.py:78
  87.8 10.7 all-gather.27.cloned.1.call-done
  106.8 20.3 all-gather.29.cloned.1.call-done
  138.7 43.9 %reduce-scatter.16.cloned.1.call-done = bf16[128,2048]{1,0:T(8,128)(2,1)} async-done(((bf16[512,2048]{1,0:T(8,128)(2,1)}), bf16[128,2048]{1,0:T(8,128)(2,1)}) %reduce-scatter.16.cloned.1.call-update) | async-done | bytes 524304 | tf_op jit(solution)/shard_map/reduce_scatter | solution.py:86
  186.1 45.4 %all-gather.31.cloned.1.call-done = bf16[512,2048]{1,0:T(8,128)(2,1)} async-done(((bf16[128,2048]{1,0:T(8,128)(2,1)}), bf16[512,2048]{1,0:T(8,128)(2,1)}) %all-gather.31.cloned.1.call-update) | async-done | bytes 2097168 | tf_op jit(solution)/shard_map/all_gather | solution.py:78
  231.5 10.5 fusion.321
  253.7 42.4 %reduce-scatter.18.cloned.1.call-done = bf16[128,2048]{1,0:T(8,128)(2,1)} async-done(((bf16[512,2048]{1,0:T(8,128)(2,1)}), bf16[128,2048]{1,0:T(8,128)(2,1)}) %reduce-scatter.18.cloned.1.call-update) | async-done | bytes 524304 | tf_op jit(solution)/shard_map/reduce_scatter | solution.py:86
  302.6 45.2 %all-gather.33.cloned.1.call-done = bf16[512,2048]{1,0:T(8,128)(2,1)} async-done(((bf16[128,2048]{1,0:T(8,128)(2,1)}), bf16[512,2048]{1,0:T(8,128)(2,1)}) %all-gather.33.cloned.1.call-update) | async-done | bytes 2097168 | tf_op jit(solution)/shard_map/all_gather | solution.py:78
  398.7 19.7 all-gather.37.cloned.1.call-done
  433.0 44.0 %reduce-scatter.20.cloned.1.call-done = bf16[128,2048]{1,0:T(8,128)(2,1)} async-done(((bf16[512,2048]{1,0:T(8,128)(2,1)}), bf16[128,2048]{1,0:T(8,128)(2,1)}) %reduce-scatter.20.cloned.1.call-update) | async-done | bytes 524304 | tf_op jit(solution)/shard_map/reduce_scatter | solution.py:86
  484.1 43.0 %all-gather.39.cloned.1.call-done = bf16[512,2048]{1,0:T(8,128)(2,1)} async-done(((bf16[128,2048]{1,0:T(8,128)(2,1)}), bf16[512,2048]{1,0:T(8,128)(2,1)}) %all-gather.39.cloned.1.call-update) | async-done | bytes 2097168 | tf_op jit(solution)/shard_map/all_gather | solution.py:78
  527.1 14.6 fusion.320
  541.7 32.2 %all-gather.49.cloned.1.call-done = bf16[512,2048]{1,0:T(8,128)(2,1)} async-done(((bf16[128,2048]{1,0:T(8,128)(2,1)}), bf16[512,2048]{1,0:T(8,128)(2,1)}) %all-gather.49.cloned.1.call-update) | async-done | bytes 2097168 | tf_op jit(solution)/shard_map/all_gather | solution.py:82
  573.8 11.7 multiply_convert_fusion.5
  594.4 42.7 %reduce-scatter.22.cloned.1.call-done = bf16[128,2048]{1,0:T(8,128)(2,1)} async-done(((bf16[512,2048]{1,0:T(8,128)(2,1)}), bf16[128,2048]{1,0:T(8,128)(2,1)}) %reduce-scatter.22.cloned.1.call-update) | async-done | bytes 524304 | tf_op jit(solution)/shard_map/reduce_scatter | solution.py:86
  642.8 45.2 %all-gather.41.cloned.1.call-done = bf16[512,2048]{1,0:T(8,128)(2,1)} async-done(((bf16[128,2048]{1,0:T(8,128)(2,1)}), bf16[512,2048]{1,0:T(8,128)(2,1)}) %all-gather.41.cloned.1.call-update) | async-done | bytes 2097168 | tf_op jit(solution)/shard_map/all_gather | solution.py:78
  708.6 11.7 convolution_convert_fusion.2
  739.0 21.2 all-gather.45.cloned.1.call-done
  780.5 26.4 %reduce-scatter.28.cloned.1.call-done = bf16[128,2048]{1,0:T(8,128)(2,1)} async-done(((bf16[512,2048]{1,0:T(8,128)(2,1)}), bf16[128,2048]{1,0:T(8,128)(2,1)}) %reduce-scatter.28.cloned.1.call-update) | async-done | bytes 524304 | tf_op jit(solution)/shard_map/reduce_scatter | solution.py:86
  809.2 43.7 %reduce-scatter.24.cloned.1.call-done = bf16[128,2048]{1,0:T(8,128)(2,1)} async-done(((bf16[512,2048]{1,0:T(8,128)(2,1)}), bf16[128,2048]{1,0:T(8,128)(2,1)}) %reduce-scatter.24.cloned.1.call-update) | async-done | bytes 524304 | tf_op jit(solution)/shard_map/reduce_scatter | solution.py:86
  866.4 14.3 all-gather.53.cloned.1.call-done
  882.8 26.8 %all-gather.51.cloned.1.call-done = bf16[2048,256]{1,0:T(8,128)(2,1)} async-done(((bf16[512,256]{1,0:T(8,128)(2,1)}), bf16[2048,256]{1,0:T(8,128)(2,1)}) %all-gather.51.cloned.1.call-update) | async-done | bytes 1048592 | tf_op jit(solution)/shard_map/all_gather | solution.py:294
  922.0 35.1 %all-gather.55.cloned.1.call-done = bf16[512,2048]{1,0:T(8,128)(2,1)} async-done(((bf16[128,2048]{1,0:T(8,128)(2,1)}), bf16[512,2048]{1,0:T(8,128)(2,1)}) %all-gather.55.cloned.1.call-update) | async-done | bytes 2097168 | tf_op jit(solution)/shard_map/all_gather | solution.py:82
  1055.3 43.4 %reduce-scatter.32.cloned.1.call-done = bf16[128,2048]{1,0:T(8,128)(2,1)} async-done(((bf16[512,2048]{1,0:T(8,128)(2,1)}), bf16[128,2048]{1,0:T(8,128)(2,1)}) %reduce-scatter.32.cloned.1.call-update) | async-done | bytes 524304 | tf_op jit(solution)/shard_map/reduce_scatter | solution.py:86
  1108.3 37.2 %all-gather.47.cloned.1.call-done = bf16[512,2048]{1,0:T(8,128)(2,1)} async-done(((bf16[128,2048]{1,0:T(8,128)(2,1)}), bf16[512,2048]{1,0:T(8,128)(2,1)}) %all-gather.47.cloned.1.call-update) | async-done | bytes 2097168 | tf_op jit(solution)/shard_map/all_gather | solution.py:78
  1145.4 14.5 fusion.319
  1159.9 32.4 %all-gather.57.cloned.1.call-done = bf16[512,2048]{1,0:T(8,128)(2,1)} async-done(((bf16[128,2048]{1,0:T(8,128)(2,1)}), bf16[512,2048]{1,0:T(8,128)(2,1)}) %all-gather.57.cloned.1.call-update) | async-done | bytes 2097168 | tf_op jit(solution)/shard_map/all_gather | solution.py:82
  1192.2 11.4 multiply_convert_fusion.3
  1205.3 10.7 convolution_convert_fusion.1
  1218.6 40.2 %reduce-scatter.34.cloned.1.call-done = bf16[128,2048]{1,0:T(8,128)(2,1)} async-done(((bf16[512,2048]{1,0:T(8,128)(2,1)}), bf16[128,2048]{1,0:T(8,128)(2,1)}) %reduce-scatter.34.cloned.1.call-update) | async-done | bytes 524304 | tf_op jit(solution)/shard_map/reduce_scatter | solution.py:86
  1268.5 18.2 all-gather.59.cloned.1.call-done
  1292.5 23.4 all-gather.61.cloned.1.call-done
  1324.1 39.4 %all-gather.63.cloned.1.call-done = bf16[512,2048]{1,0:T(8,128)(2,1)} async-done(((bf16[128,2048]{1,0:T(8,128)(2,1)}), bf16[512,2048]{1,0:T(8,128)(2,1)}) %all-gather.63.cloned.1.call-update) | async-done | bytes 2097168 | tf_op jit(solution)/shard_map/all_gather | solution.py:82
  1460.9 43.9 %reduce-scatter.38.cloned.1.call-done = bf16[128,2048]{1,0:T(8,128)(2,1)} async-done(((bf16[512,2048]{1,0:T(8,128)(2,1)}), bf16[128,2048]{1,0:T(8,128)(2,1)}) %reduce-scatter.38.cloned.1.call-update) | async-done | bytes 524304 | tf_op jit(solution)/shard_map/reduce_scatter | solution.py:86
  1517.5 45.4 %all-gather.65.cloned.1.call-done = bf16[512,2048]{1,0:T(8,128)(2,1)} async-done(((bf16[128,2048]{1,0:T(8,128)(2,1)}), bf16[512,2048]{1,0:T(8,128)(2,1)}) %all-gather.65.cloned.1.call-update) | async-done | bytes 2097168 | tf_op jit(solution)/shard_map/all_gather | solution.py:82
  1562.9 11.8 multiply_convert_fusion.1
  1576.4 10.7 convolution_convert_fusion
  1593.9 35.9 %reduce-scatter.40.cloned.1.call-done = bf16[128,2048]{1,0:T(8,128)(2,1)} async-done(((bf16[512,2048]{1,0:T(8,128)(2,1)}), bf16[128,2048]{1,0:T(8,128)(2,1)}) %reduce-scatter.40.cloned.1.call-update) | async-done | bytes 524304 | tf_op jit(solution)/shard_map/reduce_scatter | solution.py:86
  1634.9 10.5 fusion.114
  1645.5 12.3 fusion.92
  1675.0 11.2 all-gather.69.cloned.1.call-done
  1694.3 39.8 %all-gather.71.cloned.1.call-done = bf16[512,2048]{1,0:T(8,128)(2,1)} async-done(((bf16[128,2048]{1,0:T(8,128)(2,1)}), bf16[512,2048]{1,0:T(8,128)(2,1)}) %all-gather.71.cloned.1.call-update) | async-done | bytes 2097168 | tf_op jit(solution)/shard_map/all_gather | solution.py:82
  1793.9 12.3 fusion.90
  1830.7 16.4 fusion.15
  1885.6 26.0 %add_convert_fusion = bf16[2048,3072]{1,0:T(8,128)(2,1)} fusion(f32[2048,3072]{1,0:T(8,128)} %fusion.90, f32[2048,3072]{1,0:T(8,128)} %fusion.92, f32[]{:T(128)S(6)} %convert_element_type.478, f32[]{:T(128)S(6)} %convert_element_type.477, bf16[512,2048]{1,0:T(8,128)(2,1)} %all-gather.39.cloned.1.call-done, ...), kind=kOutput, calls=%fused_computation | convolution fusion | flops 6481248256 | bytes 70254600 | tf_op jit(solution)/shard_map/dot_general | solution.py:279
  1935.4 76.8 %all-reduce.12 = (f32[1,2048]{1,0:T(1,128)}, f32[1,128]{1,0:T(1,128)}, f32[1,128]{1,0:T(1,128)}, f32[1,2048]{1,0:T(1,128)}) all-reduce(f32[1,2048]{1,0:T(1,128)S(1)} %bitcast.719, f32[1,128]{1,0:T(1,128)S(1)} %add_bitcast_fusion.7, f32[1,128]{1,0:T(1,128)S(1)} %add_bitcast_fusion.6, ...), channel_id=1, replica_groups=mesh['section'=2,'ctx'=4,'mp'=4] {'ctx','mp'}, use_global_device_ids=true, to_apply=%region_72.73 | all-reduce | flops 4352 | bytes 34816 | tf_op jit(solution)/shard_map/psum | solution.py:435
  2016.0 364.7 %all-reduce.16.cloned.1.call-done = (bf16[2048,1024]{1,0:T(8,128)(2,1)}, bf16[1,512,2048]{2,1,0:T(8,128)(2,1)}, bf16[2048,3072]{1,0:T(8,128)(2,1)}, bf16[1,1536,2048]{2,1,0:T(8,128)(2,1)}) async-done(((bf16[2048,1024]{1,0:T(8,128)(2,1)}, bf16[1,512,2048]{2,1,0:T(8,128)(2,1)}, bf16[2048,3072]{1,0:T(8,128)(2,1)}, bf16[1,1536,2048]{2,1,0:T(8,128)(2,1)}), (bf16[2048,1024]{1,0:T(8,128)(2,1)}, ...) | async-done | bytes 25165840 | tf_op jit(solution)/shard_map/psum | solution.py:429
  2402.0 18.6 slice_bitcast_fusion
  (733 shorter events, 720.1 us)
Async XLA Ops:
  7.2 127.7 %copy-start = (bf16[1,512,2048]{2,1,0:T(8,128)(2,1)S(1)}, bf16[1,512,2048]{2,1,0:T(8,128)(2,1)}, u32[]{:S(2)}) copy-start(bf16[1,512,2048]{2,1,0:T(8,128)(2,1)} %param.23) | copy-start | bytes 6291460
  7.2 52.9 %all-gather.25.cloned.1.call-start = ((), (), s32[]{:S(2)}) async-start(), calls=%async_computation.15 | async-start | bytes 2621440 | tf_op jit(solution)/shard_map/all_gather | solution.py:78
  8.1 1499.9 %copy-start.83 = (f32[1,2048]{1,0:T(1,128)}, f32[1,2048]{1,0:T(1,128)S(1)}, u32[]{:S(2)}) copy-start(f32[1,2048]{1,0:T(1,128)S(1)} %mul.1992) | copy-start | bytes 24580
  11.4 87.1 %all-gather.27.cloned.1.call-start = ((), (), s32[]{:S(2)}) async-start(), calls=%async_computation.16 | async-start | bytes 1310720 | tf_op jit(solution)/shard_map/all_gather | solution.py:214
  16.0 1405.8 %copy-start.88 = (f32[128]{0:T(128)}, f32[128]{0:T(128)S(1)}, u32[]{:S(2)}) copy-start(f32[128]{0:T(128)S(1)} %bitcast_convert_fusion.4) | copy-start | bytes 1540
  16.6 1432.5 %copy-start.86 = (f32[128]{0:T(128)}, f32[128]{0:T(128)S(1)}, u32[]{:S(2)}) copy-start(f32[128]{0:T(128)S(1)} %bitcast_convert_fusion.5) | copy-start | bytes 1540
  73.0 54.1 %all-gather.29.cloned.1.call-start = ((), (), s32[]{:S(2)}) async-start(), calls=%async_computation.17 | async-start | bytes 1310720 | tf_op jit(solution)/shard_map/all_gather | solution.py:215
  86.5 96.1 %reduce-scatter.16.cloned.1.call-start = ((), (), s32[]{:S(2)}) async-start(), calls=%async_computation.18 | async-start | bytes 2621440 | tf_op jit(solution)/shard_map/reduce_scatter | solution.py:86
  138.6 92.9 %all-gather.31.cloned.1.call-start = ((), (), s32[]{:S(2)}) async-start(), calls=%async_computation.19 | async-start | bytes 2621440 | tf_op jit(solution)/shard_map/all_gather | solution.py:78
  186.1 110.1 %reduce-scatter.18.cloned.1.call-start = ((), (), s32[]{:S(2)}) async-start(), calls=%async_computation.20 | async-start | bytes 2621440 | tf_op jit(solution)/shard_map/reduce_scatter | solution.py:86
  253.4 94.3 %all-gather.33.cloned.1.call-start = ((), (), s32[]{:S(2)}) async-start(), calls=%async_computation.21 | async-start | bytes 2621440 | tf_op jit(solution)/shard_map/all_gather | solution.py:78
  297.6 2.0 collective-permute-start
  302.4 87.5 %all-gather.35.cloned.1.call-start = ((), (), s32[]{:S(2)}) async-start(), calls=%async_computation.22 | async-start | bytes 1310720 | tf_op jit(solution)/shard_map/all_gather | solution.py:214
  364.4 54.0 %all-gather.37.cloned.1.call-start = ((), (), s32[]{:S(2)}) async-start(), calls=%async_computation.23 | async-start | bytes 1310720 | tf_op jit(solution)/shard_map/all_gather | solution.py:215
  379.8 97.2 %reduce-scatter.20.cloned.1.call-start = ((), (), s32[]{:S(2)}) async-start(), calls=%async_computation.24 | async-start | bytes 2621440 | tf_op jit(solution)/shard_map/reduce_scatter | solution.py:86
  433.0 94.1 %all-gather.39.cloned.1.call-start = ((), (), s32[]{:S(2)}) async-start(), calls=%async_computation.25 | async-start | bytes 2621440 | tf_op jit(solution)/shard_map/all_gather | solution.py:78
  481.7 92.2 %all-gather.49.cloned.1.call-start = ((), (), s32[]{:S(2)}) async-start(), calls=%async_computation.33 | async-start | bytes 2621440 | tf_op jit(solution)/shard_map/all_gather | solution.py:82
  483.8 153.3 %reduce-scatter.22.cloned.1.call-start = ((), (), s32[]{:S(2)}) async-start(), calls=%async_computation.26 | async-start | bytes 2621440 | tf_op jit(solution)/shard_map/reduce_scatter | solution.py:86
  594.3 93.6 %all-gather.41.cloned.1.call-start = ((), (), s32[]{:S(2)}) async-start(), calls=%async_computation.27 | async-start | bytes 2621440 | tf_op jit(solution)/shard_map/all_gather | solution.py:78
  638.6 2.0 collective-permute-start.1
  642.5 94.3 %all-gather.43.cloned.1.call-start = ((), (), s32[]{:S(2)}) async-start(), calls=%async_computation.28 | async-start | bytes 1310720 | tf_op jit(solution)/shard_map/all_gather | solution.py:214
  706.3 53.8 %all-gather.45.cloned.1.call-start = ((), (), s32[]{:S(2)}) async-start(), calls=%async_computation.29 | async-start | bytes 1310720 | tf_op jit(solution)/shard_map/all_gather | solution.py:215
  708.4 98.4 %reduce-scatter.28.cloned.1.call-start = ((), (), s32[]{:S(2)}) async-start(), calls=%async_computation.34 | async-start | bytes 2621440 | tf_op jit(solution)/shard_map/reduce_scatter | solution.py:86
  720.3 132.5 %reduce-scatter.24.cloned.1.call-start = ((), (), s32[]{:S(2)}) async-start(), calls=%async_computation.30 | async-start | bytes 2621440 | tf_op jit(solution)/shard_map/reduce_scatter | solution.py:86
  777.6 103.1 %all-gather.53.cloned.1.call-start = ((), (), s32[]{:S(2)}) async-start(), calls=%async_computation.36 | async-start | bytes 1310720 | tf_op jit(solution)/shard_map/all_gather | solution.py:295
  778.3 131.2 %all-gather.51.cloned.1.call-start = ((), (), s32[]{:S(2)}) async-start(), calls=%async_computation.35 | async-start | bytes 1310720 | tf_op jit(solution)/shard_map/all_gather | solution.py:294
  780.4 176.7 %all-gather.55.cloned.1.call-start = ((), (), s32[]{:S(2)}) async-start(), calls=%async_computation.37 | async-start | bytes 2621440 | tf_op jit(solution)/shard_map/all_gather | solution.py:82
  859.9 169.7 %reduce-scatter.30.cloned.1.call-start = ((), (), s32[]{:S(2)}) async-start(), calls=%async_computation.38 | async-start | bytes 2621440 | tf_op jit(solution)/shard_map/reduce_scatter | solution.py:309
  995.6 103.1 %reduce-scatter.32.cloned.1.call-start = ((), (), s32[]{:S(2)}) async-start(), calls=%async_computation.39 | async-start | bytes 2621440 | tf_op jit(solution)/shard_map/reduce_scatter | solution.py:86
  1054.7 90.7 %all-gather.47.cloned.1.call-start = ((), (), s32[]{:S(2)}) async-start(), calls=%async_computation.31 | async-start | bytes 2621440 | tf_op jit(solution)/shard_map/all_gather | solution.py:78
  1055.2 137.0 %all-gather.57.cloned.1.call-start = ((), (), s32[]{:S(2)}) async-start(), calls=%async_computation.40 | async-start | bytes 2621440 | tf_op jit(solution)/shard_map/all_gather | solution.py:82
  1103.0 2.0 collective-permute-start.2
  1108.0 150.9 %reduce-scatter.34.cloned.1.call-start = ((), (), s32[]{:S(2)}) async-start(), calls=%async_computation.41 | async-start | bytes 2621440 | tf_op jit(solution)/shard_map/reduce_scatter | solution.py:86
  1216.1 70.6 %all-gather.59.cloned.1.call-start = ((), (), s32[]{:S(2)}) async-start(), calls=%async_computation.42 | async-start | bytes 1310720 | tf_op jit(solution)/shard_map/all_gather | solution.py:294
  1216.7 99.2 %all-gather.61.cloned.1.call-start = ((), (), s32[]{:S(2)}) async-start(), calls=%async_computation.43 | async-start | bytes 1310720 | tf_op jit(solution)/shard_map/all_gather | solution.py:295
  1218.6 144.9 %all-gather.63.cloned.1.call-start = ((), (), s32[]{:S(2)}) async-start(), calls=%async_computation.44 | async-start | bytes 2621440 | tf_op jit(solution)/shard_map/all_gather | solution.py:82
  1264.6 171.5 %reduce-scatter.36.cloned.1.call-start = ((), (), s32[]{:S(2)}) async-start(), calls=%async_computation.45 | async-start | bytes 2621440 | tf_op jit(solution)/shard_map/reduce_scatter | solution.py:309
  1401.9 102.9 %reduce-scatter.38.cloned.1.call-start = ((), (), s32[]{:S(2)}) async-start(), calls=%async_computation.46 | async-start | bytes 2621440 | tf_op jit(solution)/shard_map/reduce_scatter | solution.py:86
  1460.9 102.0 %all-gather.65.cloned.1.call-start = ((), (), s32[]{:S(2)}) async-start(), calls=%async_computation.47 | async-start | bytes 2621440 | tf_op jit(solution)/shard_map/all_gather | solution.py:82
  1512.6 2.0 collective-permute-start.3
  1517.5 112.3 %reduce-scatter.40.cloned.1.call-start = ((), (), s32[]{:S(2)}) async-start(), calls=%async_computation.48 | async-start | bytes 2621440 | tf_op jit(solution)/shard_map/reduce_scatter | solution.py:86
  1587.1 82.1 %all-gather.67.cloned.1.call-start = ((), (), s32[]{:S(2)}) async-start(), calls=%async_computation.49 | async-start | bytes 1310720 | tf_op jit(solution)/shard_map/all_gather | solution.py:294
  1587.8 98.3 %all-gather.69.cloned.1.call-start = ((), (), s32[]{:S(2)}) async-start(), calls=%async_computation.50 | async-start | bytes 1310720 | tf_op jit(solution)/shard_map/all_gather | solution.py:295
  1588.6 145.5 %all-gather.71.cloned.1.call-start = ((), (), s32[]{:S(2)}) async-start(), calls=%async_computation.51 | async-start | bytes 2621440 | tf_op jit(solution)/shard_map/all_gather | solution.py:82
  1634.8 225.6 %reduce-scatter.42.cloned.1.call-start = ((), (), s32[]{:S(2)}) async-start(), calls=%async_computation.52 | async-start | bytes 2621440 | tf_op jit(solution)/shard_map/reduce_scatter | solution.py:309
  1772.8 156.5 %reduce-scatter.26.cloned.1.call-start = ((), (), s32[]{:S(2)}) async-start(), calls=%async_computation.32 | async-start | bytes 2621440 | tf_op jit(solution)/shard_map/reduce_scatter | solution.py:86
  1820.3 113.1 %reduce-scatter.44.cloned.1.call-start = ((), (), s32[]{:S(2)}) async-start(), calls=%async_computation.53 | async-start | bytes 2621440 | tf_op jit(solution)/shard_map/reduce_scatter | solution.py:86
  1885.6 495.2 %all-reduce.16.cloned.1.call-start = ((), (), s32[]{:S(2)}) async-start(), calls=%async_computation.54 | async-start | bytes 50331648 | tf_op jit(solution)/shard_map/psum | solution.py:429
  (136 other events, 941.8 us)
Sparse Core Ops, SparseCore 0:
  11.5 48.5 all-gather.24
  73.1 25.4 all-gather.26
  100.4 26.6 all-gather.28
  138.7 43.8 reduce-scatter.15
  186.2 45.2 all-gather.30
  253.5 42.5 reduce-scatter.17
  302.5 45.2 all-gather.32
  364.5 25.3 all-gather.34
  391.7 26.6 all-gather.36
  433.1 43.8 reduce-scatter.19
  481.8 45.2 all-gather.38
  529.2 44.6 all-gather.48
  594.5 42.5 reduce-scatter.21
  642.6 45.2 all-gather.40
  706.4 25.3 all-gather.42
  733.5 26.6 all-gather.44
  762.9 43.8 reduce-scatter.27
  809.6 43.1 reduce-scatter.23
  854.7 25.9 all-gather.52
  882.9 26.6 all-gather.50
  911.2 45.9 all-gather.54
  995.7 33.9 reduce-scatter.29
  1054.8 43.8 reduce-scatter.31
  1100.1 45.2 all-gather.46
  1147.5 44.6 all-gather.56
  1216.2 42.5 reduce-scatter.33
  1260.7 25.9 all-gather.58
  1289.2 26.6 all-gather.60
  1317.6 45.9 all-gather.62
  1402.1 33.9 reduce-scatter.35
  1461.0 43.8 reduce-scatter.37
  1517.6 45.2 all-gather.64
  1587.2 42.5 reduce-scatter.39
  1631.7 25.9 all-gather.66
  1659.5 26.6 all-gather.68
  1688.1 45.9 all-gather.70
  1772.9 33.9 reduce-scatter.41
  1820.4 42.5 reduce-scatter.25
  1885.7 42.6 reduce-scatter.43
  1933.4 447.3 all-reduce.15
where the time goes:
time: 2450 us; the launch traced here: 2430 us
  waiting for transfers between devices  1460 us (60%)
  matrix products  401 us (16%)
  local copies, waits for them, and re-layouts  243 us (10%)
  other arithmetic  236 us (10%)
  blocking collectives  76.8 us (3%)
    reduce_scatter x12, waiting for transfers between devices, row_sums(): lax.psum_scatter(lax.dot_general(left_side, weight, (((1,), (weight_dim,)...  406 us
    psum x1, waiting for transfers between devices, shards(): lax.psum(sum_qkv.astype(jnp.bfloat16), 'ctx').astype(jnp.float32)  365 us
    all_gather x6, waiting for transfers between devices, spread_rows(): return lax.all_gather(token_rows, 'mp', axis=0, tiled=True)  255 us
    all_gather x6, waiting for transfers between devices, gather_grads(): return lax.all_gather(token_rows, 'mp', axis=0, tiled=True)  224 us
    dot_general x12, matrix products, row_sums(): lax.dot_general(left_side, weight, (((1,), (weight_dim,)), ((), ())), pre...  82.6 us
    psum x1, blocking collectives, shards(): lax.psum((gain_attn, gain_query, gain_key, gain_mlp), ('ctx', 'mp'))  76.8 us
    all_gather x3, waiting for transfers between devices, section_forward(): lax.all_gather(values, 'ctx', axis=0, tiled=True)  61.2 us
    dot_general x3, matrix products, section_backward(): lax.dot_general(kept_state['mlp_in'], grad_both, contract_rows, preferred...  50.6 us
  transfers between devices with their start and end apart: 44, of which 39 were waited for; matrix products, arithmetic and copies ran while one was open for 19% of the time, Pallas kernels for 0%

commit v1 on v0

v1 whole, which is shorter than its diff:
```python
import functools

import jax
import jax.numpy as jnp
from jax import lax
from jax.experimental import pallas as pl
from jax.experimental.pallas import tpu as pltpu
from jax.sharding import PartitionSpec as P

HD = 128
MB = 2
SEQS = 2
STRETCH = 128
EPSILON = 1e-06
ROPE_BASE = 1000000.0
MASKED_SCORE = -1e30
SCALING = HD ** (-0.5)
LOW = jnp.bfloat16
F32 = jnp.float32
ROW_TILE = 64
VMEM_BYTES = 50 * 1024 * 1024


def dot_nn(left, right):
    return lax.dot_general(left, right, (((1,), (0,)), ((), ())), preferred_element_type=F32)


def dot_nt(left, right):
    return lax.dot_general(left, right, (((1,), (1,)), ((), ())), preferred_element_type=F32)


def dot_tn(left, right):
    return lax.dot_general(left, right, (((0,), (0,)), ((), ())), preferred_element_type=F32)


def kernel_call(body, out_shape, flops, args):
    moved = sum(a.size * a.dtype.itemsize for a in args)
    moved += sum(o.size * o.dtype.itemsize for o in out_shape)
    return pl.pallas_call(
        body,
        out_shape=out_shape,
        compiler_params=pltpu.CompilerParams(vmem_limit_bytes=VMEM_BYTES),
        cost_estimate=pl.CostEstimate(flops=flops, bytes_accessed=moved, transcendentals=0),
    )(*args)


def qkv_forward_body(x, wq, wk, wv, q_gain, k_gain, cosine, sine, q_proj, k_proj, queries, kv):
    rows = x[...]
    cos_full, sin_signed = cosine[...], sine[...]

    def prepared(head, gain):
        scaling = lax.rsqrt(jnp.mean(head * head, axis=-1, keepdims=True) + EPSILON)
        normed = head * scaling * gain
        return (normed * cos_full + pltpu.roll(normed, HD // 2, 1) * sin_signed).astype(LOW)

    k_width = wk.shape[1]
    all_q = dot_nn(rows, wq[...])
    q_proj[...] = all_q
    for at in range(0, wq.shape[1], HD):
        queries[:, at : at + HD] = prepared(all_q[:, at : at + HD], q_gain[...])
    all_k = dot_nn(rows, wk[...])
    k_proj[...] = all_k
    for at in range(0, k_width, HD):
        kv[:, at : at + HD] = prepared(all_k[:, at : at + HD], k_gain[...])
    kv[:, k_width:] = dot_nn(rows, wv[...]).astype(LOW)


def attend_body(n_ctx, queries, *refs):
    blocks = refs[:n_ctx]
    q_pos, k_pos, w_out, part, attended, log_total = refs[n_ctx:]
    rows = queries.shape[0]
    kv_width = blocks[0].shape[1] // 2
    groups = queries.shape[1] // kv_width
    place = jnp.concatenate([q_pos[...]] * groups, axis=0)
    for kv_head in range(kv_width // HD):
        first = kv_head * groups
        stacked = jnp.concatenate(
            [queries[:, (first + i) * HD : (first + i + 1) * HD] for i in range(groups)], axis=0
        )
        at = kv_head * HD
        scores = []
        for j, block in enumerate(blocks):
            raw = dot_nt(stacked, block[:, at : at + HD]) * SCALING
            scores.append(jnp.where(k_pos[j : j + 1, :] <= place, raw, MASKED_SCORE))
        top = functools.reduce(
            jnp.maximum, [jnp.max(s, axis=1, keepdims=True) for s in scores]
        )
        total, running = 0.0, 0.0
        for s, block in zip(scores, blocks):
            weights = jnp.exp(s - top)
            total = total + jnp.sum(weights, axis=1, keepdims=True)
            running = running + dot_nn(
                weights.astype(LOW), block[:, kv_width + at : kv_width + at + HD]
            )
        result = (running / total).astype(LOW)
        logs = top + jnp.log(total)
        for i in range(groups):
            head = first + i
            attended[:, head * HD : (head + 1) * HD] = result[i * rows : (i + 1) * rows]
            log_total[:, head : head + 1] = logs[i * rows : (i + 1) * rows]
    part[...] = dot_nn(attended[...], w_out[...]).astype(LOW)


def attend_back_body(n_ctx, grad_rows, w_out, queries, *refs):
    blocks = refs[:n_ctx]
    q_pos, k_pos, attended, log_total, grad_q = refs[n_ctx : n_ctx + 5]
    grad_kv = refs[n_ctx + 5 :]
    rows = queries.shape[0]
    kv_width = blocks[0].shape[1] // 2
    groups = queries.shape[1] // kv_width
    grad_all = dot_nt(grad_rows[...], w_out[...]).astype(LOW)
    place = jnp.concatenate([q_pos[...]] * groups, axis=0)
    for kv_head in range(kv_width // HD):
        heads = [kv_head * groups + i for i in range(groups)]
        stacked = jnp.concatenate([queries[:, h * HD : (h + 1) * HD] for h in heads], axis=0)
        grads = jnp.concatenate([grad_all[:, h * HD : (h + 1) * HD] for h in heads], axis=0)
        out_low = jnp.concatenate([attended[:, h * HD : (h + 1) * HD] for h in heads], axis=0)
        logs = jnp.concatenate([log_total[:, h : h + 1] for h in heads], axis=0)
        delta = jnp.sum(grads.astype(F32) * out_low.astype(F32), axis=1, keepdims=True)
        at = kv_head * HD
        total = 0.0
        for j, block in enumerate(blocks):
            keys = block[:, at : at + HD]
            values = block[:, kv_width + at : kv_width + at + HD]
            shifted = dot_nt(stacked, keys) * SCALING - logs
            probs = jnp.exp(jnp.where(k_pos[j : j + 1, :] <= place, shifted, MASKED_SCORE))
            grad_scores = (probs * (dot_nt(grads, values) - delta)).astype(LOW)
            total = total + dot_nn(grad_scores, keys)
            grad_kv[j][:, at : at + HD] = (dot_tn(grad_scores, stacked) * SCALING).astype(LOW)
            grad_kv[j][:, kv_width + at : kv_width + at + HD] = dot_tn(
                probs.astype(LOW), grads
            ).astype(LOW)
        for i, h in enumerate(heads):
            grad_q[:, h * HD : (h + 1) * HD] = total[i * rows : (i + 1) * rows] * SCALING


def qkv_back_body(n_ctx, grad_q, *refs):
    grad_kv = refs[:n_ctx]
    q_proj, k_proj, q_gain, k_gain, cosine, sine, wq, wk, wv = refs[n_ctx : n_ctx + 9]
    mixed, part, grad_q_gain, grad_k_gain = refs[n_ctx + 9 :]
    cos_full, sin_signed = cosine[...], sine[...]
    q_width, kv_width = wq.shape[1], wk.shape[1]

    def pulled(grad, head, gain):
        turned = grad * cos_full + pltpu.roll(grad * sin_signed, HD // 2, 1)
        scaling = lax.rsqrt(jnp.mean(head * head, axis=-1, keepdims=True) + EPSILON)
        inner = turned * gain
        back = scaling * inner - head * (
            scaling * scaling * scaling * jnp.mean(inner * head, axis=-1, keepdims=True)
        )
        return back.astype(LOW), jnp.sum(turned * head * scaling, axis=0, keepdims=True)

    total = 0.0
    for at in range(0, q_width, HD):
        back, gain_part = pulled(grad_q[:, at : at + HD], q_proj[:, at : at + HD], q_gain[...])
        mixed[:, at : at + HD] = back
        total = total + gain_part
    grad_q_gain[...] = total
    summed = functools.reduce(jnp.add, [g[...].astype(F32) for g in grad_kv])
    total = 0.0
    for at in range(0, kv_width, HD):
        back, gain_part = pulled(summed[:, at : at + HD], k_proj[:, at : at + HD], k_gain[...])
        mixed[:, q_width + at : q_width + at + HD] = back
        total = total + gain_part
    grad_k_gain[...] = total
    mixed[:, q_width + kv_width :] = summed[:, kv_width:].astype(LOW)
    part[...] = (
        dot_nt(mixed[:, :q_width], wq[...])
        + dot_nt(mixed[:, q_width : q_width + kv_width], wk[...])
        + dot_nt(mixed[:, q_width + kv_width :], wv[...])
    ).astype(LOW)


def assemble_body(pieces, widths, place, *refs):
    ins, outs = refs[: 4 * pieces], refs[4 * pieces :]
    step = pl.program_id(0)
    layer = place[2 * pieces]
    for i in range(4 * pieces):

        @pl.when((step == i % (2 * pieces)) & (layer == i // (2 * pieces)))
        def _(i=i):
            at = 0
            for out, width in zip(outs, widths):
                out[...] = ins[i][:, at : at + width].astype(F32)
                at += width


def assemble(place, arrays, widths):
    pieces = len(arrays) // 4
    rows, cols = arrays[0].shape
    tile = ROW_TILE
    while rows % tile:
        tile //= 2
    steps = rows // tile

    def in_map(i, step, t, place):
        chosen = (step == i % (2 * pieces)) & (place[2 * pieces] == i // (2 * pieces))
        return (jnp.where(chosen, t, jnp.where(step > i % (2 * pieces), steps - 1, 0)), 0)

    def out_map(step, t, place):
        return (place[step] * steps + t, 0)

    return pl.pallas_call(
        functools.partial(assemble_body, pieces, widths),
        out_shape=[jax.ShapeDtypeStruct((2 * pieces * rows, w), F32) for w in widths],
        grid_spec=pltpu.PrefetchScalarGridSpec(
            num_scalar_prefetch=1,
            grid=(2 * pieces, steps),
            in_specs=[
                pl.BlockSpec((tile, cols), functools.partial(in_map, i)) for i in range(4 * pieces)
            ],
            out_specs=[pl.BlockSpec((tile, w), out_map) for w in widths],
        ),
        compiler_params=pltpu.CompilerParams(vmem_limit_bytes=VMEM_BYTES),
        cost_estimate=pl.CostEstimate(
            flops=0, bytes_accessed=2 * pieces * rows * cols * 6, transcendentals=0
        ),
    )(place, *arrays)


def swap_cores(block):
    return lax.ppermute(block, "section", [(0, 1), (1, 0)])


def to_core(block, core):
    return lax.ppermute(block, "section", [(1 - core, core)])


def ring_step(block):
    count = lax.axis_size("mp")
    return lax.ppermute(block, "mp", [(i, (i + 1) % count) for i in range(count)])


def ring_gather(block):
    blocks = [block]
    for _ in range(lax.axis_size("mp") - 1):
        blocks.append(ring_step(blocks[-1]))
    return jnp.concatenate(blocks, axis=0)


def ring_sum(part):
    count = lax.axis_size("mp")
    rows = part.shape[0] // count
    running = part[rows : 2 * rows]
    for t in range(2, count):
        running = (
            ring_step(running).astype(F32) + part[t * rows : (t + 1) * rows].astype(F32)
        ).astype(LOW)
    return ring_step(running).astype(F32) + part[:rows].astype(F32)


def across_ctx(block, distance):
    count = lax.axis_size("ctx")
    return lax.ppermute(block, "ctx", [(i, i ^ distance) for i in range(count)])


def joint_step(block, t, bits):
    count = 1 << bits
    route = []
    for core in range(2):
        distance = 1 << (t if core == 0 else bits - 1 - t)
        route += [(core * count + i, core * count + (i ^ distance)) for i in range(count)]
    return lax.ppermute(block, ("section", "ctx"), route)


def row_norm(rows, gain):
    scaling = lax.rsqrt(jnp.mean(rows * rows, axis=-1, keepdims=True) + EPSILON)
    return rows * scaling * gain


def row_norm_back(rows, gain, grad):
    scaling = lax.rsqrt(jnp.mean(rows * rows, axis=-1, keepdims=True) + EPSILON)
    inner = grad * gain
    back = scaling * inner - rows * (
        scaling * scaling * scaling * jnp.mean(inner * rows, axis=-1, keepdims=True)
    )
    return back, jnp.sum(grad * rows * scaling, axis=0)


def attention_forward(attn_in, h_rows, weights, gains, tables):
    wq, wk, wv, w_out = weights[:4]
    cosine, sine, q_pos, k_pos = tables
    rows, width = attn_in.shape
    q_width, kv_width = wq.shape[1], wk.shape[1]
    n_ctx = lax.axis_size("ctx")
    shape = jax.ShapeDtypeStruct
    q_proj, k_proj, queries, kv = kernel_call(
        qkv_forward_body,
        [
            shape((rows, q_width), F32),
            shape((rows, kv_width), F32),
            shape((rows, q_width), LOW),
            shape((rows, 2 * kv_width), LOW),
        ],
        2 * rows * width * (q_width + 2 * kv_width),
        (attn_in, wq, wk, wv, gains["query"], gains["key"], cosine, sine),
    )
    blocks = [kv] + [across_ctx(kv, j) for j in range(1, n_ctx)]
    part, attended, log_total = kernel_call(
        functools.partial(attend_body, n_ctx),
        [
            shape((rows, width), LOW),
            shape((rows, q_width), LOW),
            shape((rows, q_width // HD), F32),
        ],
        2 * rows * q_width * (2 * rows * n_ctx + width),
        (queries, *blocks, q_pos, k_pos, w_out),
    )
    mid = h_rows + ring_sum(part)
    kept = {
        "attn_in": attn_in,
        "h_rows": h_rows,
        "q_proj": q_proj,
        "k_proj": k_proj,
        "queries": queries,
        "blocks": blocks,
        "attended": attended,
        "log_total": log_total,
        "mid": mid,
    }
    return mid, kept


def mlp_forward(mid, weights, gains):
    w_gate, w_up, w_down = weights[4:]
    mlp_in = ring_gather(row_norm(mid, gains["mlp"]).astype(LOW))
    gate = dot_nn(mlp_in, w_gate)
    up = dot_nn(mlp_in, w_up)
    hidden = (jax.nn.silu(gate) * up).astype(LOW)
    result = mid + ring_sum(dot_nn(hidden, w_down).astype(LOW))
    kept = {"mlp_in": mlp_in, "gate": gate.astype(LOW), "up": up.astype(LOW), "hidden": hidden}
    return result, kept


def mlp_backward(grad_out, branch, kept, weights, gains):
    w_gate, w_up, w_down = weights[4:]
    grad_hidden = dot_nt(branch, w_down)
    gate, up = kept["gate"].astype(F32), kept["up"].astype(F32)
    sig = jax.nn.sigmoid(gate)
    grad_gate = (grad_hidden * up * sig * (1.0 + gate * (1.0 - sig))).astype(LOW)
    grad_up = (grad_hidden * gate * sig).astype(LOW)
    part = (dot_nt(grad_gate, w_gate) + dot_nt(grad_up, w_up)).astype(LOW)
    back, grad_gain = row_norm_back(kept["mid"], gains["mlp"], ring_sum(part))
    return grad_out + back, grad_gain, jnp.concatenate([grad_gate, grad_up], axis=1)


def attention_backward(grad_mid, grad_rows, kept, weights, gains, tables):
    wq, wk, wv, w_out = weights[:4]
    cosine, sine, q_pos, k_pos = tables
    rows, width = grad_rows.shape
    q_width, kv_width = wq.shape[1], wk.shape[1]
    n_ctx = lax.axis_size("ctx")
    shape = jax.ShapeDtypeStruct
    grad_q, *grad_kv = kernel_call(
        functools.partial(attend_back_body, n_ctx),
        [shape((rows, q_width), F32)] + [shape((rows, 2 * kv_width), LOW)] * n_ctx,
        2 * rows * q_width * (5 * rows * n_ctx + width),
        (
            grad_rows,
            w_out,
            kept["queries"],
            *kept["blocks"],
            q_pos,
            k_pos,
            kept["attended"],
            kept["log_total"],
        ),
    )
    grad_kv = [grad_kv[0]] + [across_ctx(grad_kv[j], j) for j in range(1, n_ctx)]
    mixed, part, grad_q_gain, grad_k_gain = kernel_call(
        functools.partial(qkv_back_body, n_ctx),
        [
            shape((rows, q_width + 2 * kv_width), LOW),
            shape((rows, width), LOW),
            shape((1, HD), F32),
            shape((1, HD), F32),
        ],
        2 * rows * width * (q_width + 2 * kv_width),
        (
            grad_q,
            *grad_kv,
            kept["q_proj"],
            kept["k_proj"],
            gains["query"],
            gains["key"],
            cosine,
            sine,
            wq,
            wk,
            wv,
        ),
    )
    back, grad_gain = row_norm_back(kept["h_rows"], gains["attn"], ring_sum(part))
    return grad_mid + back, mixed, (grad_gain, grad_q_gain[0], grad_k_gain[0])


def core_bit(core, t, bits):
    shift = jnp.where(core == 0, t, bits - 1 - t)
    return (lax.axis_index("ctx") >> shift) & 1


def reduced_pieces(left, right):
    bits = lax.axis_size("ctx").bit_length() - 1
    core = lax.axis_index("section")
    half = left.shape[1] // 2

    def product(start, count):
        columns = lax.dynamic_slice_in_dim(left, start, count, axis=1)
        return dot_tn(columns, right)

    received = swap_cores(product((1 - core) * half, half).astype(LOW))
    count = half // 2
    flag = core_bit(core, 0, bits)

    def with_received(place):
        mine = product(core * half + place * count, count)
        other = lax.dynamic_slice_in_dim(received, place * count, count, axis=0)
        return mine + other.astype(F32)

    sent = joint_step(with_received(1 - flag).astype(LOW), 0, bits)
    total = with_received(flag) + sent.astype(F32)
    for t in range(1, bits):
        total = total.astype(LOW)
        count //= 2
        flag = core_bit(core, t, bits)
        sent = joint_step(
            lax.dynamic_slice_in_dim(total, (1 - flag) * count, count, axis=0), t, bits
        )
        total = (
            lax.dynamic_slice_in_dim(total, flag * count, count, axis=0).astype(F32)
            + sent.astype(F32)
        )
    pieces = [total.astype(LOW)]
    for t in reversed(range(bits)):
        pieces = pieces + [joint_step(piece, t, bits) for piece in pieces]
    return pieces


def piece_places(bits):
    core = lax.axis_index("section")
    places = []
    for owner in (core, 1 - core):
        mine = [core_bit(owner, t, bits) for t in range(bits)]
        for x in range(1 << bits):
            place = owner
            for t in range(bits):
                place = place * 2 + (mine[t] ^ ((x >> (bits - 1 - t)) & 1))
            places.append(place)
    return jnp.stack(places + [core]).astype(jnp.int32)


def home_rows(first_layer, second_layer):
    core = lax.axis_index("section")
    place = lax.axis_index("mp")
    count = lax.axis_size("mp")
    even = place % 2 == 0
    half = count // 2
    first_route = [(m, m // 2 if m % 2 == 0 else half + m // 2) for m in range(count)]
    second_route = [(m, half + m // 2 if m % 2 == 0 else m // 2) for m in range(count)]

    def across(route):
        return [(k * count + a, (1 - k) * count + b) for k in range(2) for a, b in route]

    def arranged(rows, move):
        low = [r.astype(LOW) for r in rows]
        one = move(jnp.where(even, low[0], low[1]), first_route)
        two = move(jnp.where(even, low[1], low[0]), second_route)
        lower = place < half
        return jnp.concatenate([jnp.where(lower, one, two), jnp.where(lower, two, one)], axis=0)

    pairs = list(zip(first_layer, second_layer))
    kept = arranged(
        [jnp.where(core == 0, a, b) for a, b in pairs],
        lambda block, route: lax.ppermute(block, "mp", route),
    )
    got = arranged(
        [jnp.where(core == 0, b, a) for a, b in pairs],
        lambda block, route: lax.ppermute(block, ("section", "mp"), across(route)),
    )
    return jnp.stack(
        [jnp.where(core == 0, kept, got), jnp.where(core == 0, got, kept)]
    ).astype(F32)


def shards(
    section_input,
    cotangent,
    pair_owner,
    attn_gain,
    w_query,
    w_key,
    w_value,
    query_gain,
    key_gain,
    w_output,
    mlp_gain,
    w_gate,
    w_up,
    w_down,
):
    n_ctx, n_mp = lax.axis_size("ctx"), lax.axis_size("mp")
    core, ctx, place = lax.axis_index("section"), lax.axis_index("ctx"), lax.axis_index("mp")
    is_first = core == 0
    width = section_input.shape[2]
    seq_rows = section_input.shape[1] * n_mp // SEQS
    own_rows = seq_rows // n_mp
    bits = n_ctx.bit_length() - 1

    def gathered(block):
        return lax.all_gather(block.astype(LOW), "mp", axis=0, tiled=True)

    raw = gathered(lax.dynamic_index_in_dim(section_input, core, 0, keepdims=False))
    top_grad = gathered(lax.dynamic_index_in_dim(cotangent, core, 0, keepdims=False))
    ring_order = (place - jnp.arange(n_mp, dtype=jnp.int32)) % n_mp

    def in_ring_order(rows, seq):
        return jnp.concatenate(
            [
                lax.dynamic_slice_in_dim(
                    rows, seq * seq_rows + ring_order[t] * own_rows, own_rows, axis=0
                )
                for t in range(n_mp)
            ],
            axis=0,
        )

    own = [w[0] for w in (w_query, w_key, w_value, w_output, w_gate, w_up, w_down)]
    other = [swap_cores(w) for w in own]
    own_gains = jnp.concatenate([attn_gain[0], mlp_gain[0], query_gain[0], key_gain[0]])
    other_gains = swap_cores(own_gains)
    layer_weights, layer_gains = [], []
    for layer in range(2):
        mine = is_first if layer == 0 else ~is_first
        layer_weights.append([jnp.where(mine, a, b) for a, b in zip(own, other)])
        flat = jnp.where(mine, own_gains, other_gains).astype(F32)
        layer_gains.append(
            {
                "attn": flat[:width],
                "mlp": flat[width : 2 * width],
                "query": flat[2 * width : 2 * width + HD][None],
                "key": flat[2 * width + HD :][None],
            }
        )

    owners = lax.dynamic_index_in_dim(pair_owner, core, 0, keepdims=False)
    index = (ring_order[:, None] * own_rows + jnp.arange(own_rows, dtype=jnp.int32)).reshape(-1)
    inv_freq = ROPE_BASE ** (-jnp.arange(0, HD, 2).astype(F32) / HD)
    seq_tables = []
    for seq in range(SEQS):
        block = jnp.take(owners[seq], ctx ^ jnp.arange(n_ctx, dtype=jnp.int32))[:, None]
        k_pos = jnp.where(
            index < STRETCH,
            block * STRETCH + index,
            (2 * n_ctx - 1 - block) * STRETCH + index - STRETCH,
        )
        q_pos = k_pos[0][:, None]
        angles = q_pos.astype(F32) * inv_freq[None, :]
        cosine, sine = jnp.cos(angles), jnp.sin(angles)
        seq_tables.append(
            (
                jnp.concatenate([cosine, cosine], axis=1),
                jnp.concatenate([-sine, sine], axis=1),
                q_pos,
                k_pos,
            )
        )

    raw_rows = [in_ring_order(raw, seq) for seq in range(SEQS)]
    h_rows = [rows[:own_rows].astype(F32) for rows in raw_rows]
    kept, outputs = [], []
    for layer in range(2):
        weights, gains = layer_weights[layer], layer_gains[layer]
        states, results = [], []
        for seq in range(SEQS):
            if layer == 0:
                attn_in = row_norm(raw_rows[seq].astype(F32), gains["attn"]).astype(LOW)
            else:
                attn_in = ring_gather(row_norm(h_rows[seq], gains["attn"]).astype(LOW))
            mid, state = attention_forward(attn_in, h_rows[seq], weights, gains, seq_tables[seq])
            result, more = mlp_forward(mid, weights, gains)
            states.append({**state, **more})
            results.append(result)
        kept.append(states)
        outputs.append(results)
        h_rows = results
    section_outputs = home_rows(outputs[0], outputs[1])

    branches = [in_ring_order(top_grad, seq) for seq in range(SEQS)]
    grads = [rows[:own_rows].astype(F32) for rows in branches]
    grads_in, gain_sums, pieces = [None, None], [None, None], [None, None]
    for layer in (1, 0):
        weights, gains = layer_weights[layer], layer_gains[layer]
        if layer == 0:
            branches = [ring_gather(g.astype(LOW)) for g in grads]
        states = kept[layer]

        def both(key):
            return jnp.concatenate([state[key] for state in states], axis=0)

        branch_all = jnp.concatenate(branches, axis=0)
        down = reduced_pieces(both("hidden"), branch_all)
        mids, grad_rows, grad_both, mlp_gains = [], [], [], []
        for seq in range(SEQS):
            grad_mid, gain_part, pair = mlp_backward(
                grads[seq], branches[seq], states[seq], weights, gains
            )
            mids.append(grad_mid)
            mlp_gains.append(gain_part)
            grad_both.append(pair)
            grad_rows.append(ring_gather(grad_mid.astype(LOW)))
        gate_up = reduced_pieces(both("mlp_in"), jnp.concatenate(grad_both, axis=0))
        out = reduced_pieces(both("attended"), jnp.concatenate(grad_rows, axis=0))
        mixed, attn_gains, results = [], [], []
        for seq in range(SEQS):
            grad_in, mix, gain_parts = attention_backward(
                mids[seq], grad_rows[seq], states[seq], weights, gains, seq_tables[seq]
            )
            results.append(grad_in)
            mixed.append(mix)
            attn_gains.append(gain_parts)
        qkv = reduced_pieces(both("attn_in"), jnp.concatenate(mixed, axis=0))
        pieces[layer] = (qkv, out, gate_up, down)
        gain_sums[layer] = jnp.concatenate(
            [
                attn_gains[0][0] + attn_gains[1][0],
                mlp_gains[0] + mlp_gains[1],
                attn_gains[0][1] + attn_gains[1][1],
                attn_gains[0][2] + attn_gains[1][2],
            ]
        )
        grads_in[layer] = results
        grads = results
    input_grads = home_rows(grads_in[0], grads_in[1])
    all_gains = lax.psum(jnp.stack(gain_sums), ("section", "ctx", "mp"))
    flat = lax.dynamic_index_in_dim(all_gains, core, 0, keepdims=False)

    places = piece_places(bits)
    q_width, kv_width, ff = w_query.shape[2], w_key.shape[2], w_gate.shape[2]
    widths = ((q_width, kv_width, kv_width), (width,), (ff, ff), (width,))
    laid = []
    for at in range(4):
        arrays = []
        for layer in range(2):
            arrays += pieces[layer][at]
            arrays += [to_core(piece, layer) for piece in pieces[layer][at]]
        laid.append([whole[None] for whole in assemble(places, arrays, widths[at])])
    (g_query, g_key, g_value), (g_output,), (g_gate, g_up), (g_down,) = laid
    return (
        section_outputs[None],
        input_grads[None],
        flat[:width][None],
        g_query,
        g_key,
        g_value,
        flat[2 * width : 2 * width + HD][None],
        flat[2 * width + HD :][None],
        g_output,
        flat[width : 2 * width][None],
        g_gate,
        g_up,
        g_down,
    )


def solution(mesh):
    in_specs = (
        P(None, ("ctx", "mp"), None),
        P(None, ("ctx", "mp"), None),
        P(),
        P("section", None),
        P("section", None, "mp"),
        P("section", None, "mp"),
        P("section", None, "mp"),
        P("section", None),
        P("section", None),
        P("section", "mp", None),
        P("section", None),
        P("section", None, "mp"),
        P("section", None, "mp"),
        P("section", "mp", None),
    )
    out_specs = (
        P("section", None, ("ctx", "mp"), None),
        P("section", None, ("ctx", "mp"), None),
        P("section", None),
        P("section", None, "mp"),
        P("section", None, "mp"),
        P("section", None, "mp"),
        P("section", None),
        P("section", None),
        P("section", "mp", None),
        P("section", None),
        P("section", None, "mp"),
        P("section", None, "mp"),
        P("section", "mp", None),
    )
    return jax.shard_map(shards, mesh=mesh, in_specs=in_specs, out_specs=out_specs, check_vma=False)
```

time: 2450 us -> 1430 us (0.58)
  waiting for transfers between devices: 1460 us -> 692 us
  matrix products: 401 us -> 184 us
  local copies, waits for them, and re-layouts: 243 us -> 50.5 us
  Pallas kernels: 0 us -> 151 us
  starting transfers between devices: 4.69 us -> 152 us
  other arithmetic: 236 us -> 95.8 us
    ppermute x4 -> x204, waiting for transfers between devices: 7.59 us -> 646 us  [the longest x84 404 us: ring_step(): lax.ppermute(block, 'mp', [(i, (i + 1) % count) for i in range(count)])]
    all_gather x24 -> x2, waiting for transfers between devices: 653 us -> 45.5 us  [gathered(): return lax.all_gather(block.astype(LOW), 'mp', axis=0, tiled=True)]
    reduce_scatter x15 -> x0, waiting for transfers between devices: 427 us -> none  [the longest x12 406 us: row_sums(): lax.psum_scatter(lax.dot_general(left_side, weight, (((1,), (weight_dim,)...]
    psum x1 -> x0, waiting for transfers between devices: 365 us -> none  [shards(): lax.psum(sum_qkv.astype(jnp.bfloat16), 'ctx').astype(jnp.float32)]
    dot_general x57 -> x48, matrix products: 401 us -> 184 us  [the longest x24 111 us: dot_tn(): lax.dot_general(left, right, (((0,), (0,)), ((), ())), preferred_element_...]
    ppermute x4 -> x204, starting transfers between devices: 0.28 us -> 152 us  [the longest x40 49.8 us: joint_step(): return lax.ppermute(block, ('section', 'ctx'), route)]
    pallas_call x0 -> x20, Pallas kernels: none -> 151 us  [the longest x16 82.2 us: kernel_call(): pl.pallas_call(body, out_shape=out_shape, compiler_params=pltpu.CompilerP...]
    reshape x48 -> x0, local copies, waits for them, and re-layouts: 107 us -> none  [the longest x12 26.1 us: head_prep(): head_split = flat_rows.reshape(row_count, flat_rows.shape[1] // HD, HD)]
  transfers between devices with their start and end apart: 44 -> 206, of which waited for: 39 -> 95; matrix products, arithmetic and copies ran while one was open for 19% -> 21% of each run, Pallas kernels for 0% -> 8%
where the time goes in v1:
time: 1430 us; the launch traced here: 1420 us
  waiting for transfers between devices  692 us (48%)
  matrix products  184 us (13%)
  starting transfers between devices  152 us (11%)
  Pallas kernels  151 us (11%)
  other arithmetic  95.8 us (7%)
  blocking collectives  68.1 us (5%)
  local copies, waits for them, and re-layouts  50.5 us (4%)
  between operations  22.3 us (2%)
    ppermute x84, waiting for transfers between devices, ring_step(): lax.ppermute(block, 'mp', [(i, (i + 1) % count) for i in range(count)])  404 us
    ppermute x40, waiting for transfers between devices, joint_step(): return lax.ppermute(block, ('section', 'ctx'), route)  203 us
    dot_general x24, matrix products, dot_tn(): lax.dot_general(left, right, (((0,), (0,)), ((), ())), preferred_element_...  111 us
    pallas_call x16, Pallas kernels, kernel_call(): pl.pallas_call(body, out_shape=out_shape, compiler_params=pltpu.CompilerP...  82.2 us
    pallas_call x4, Pallas kernels, assemble(): pl.pallas_call(functools.partial(assemble_body, pieces, widths), out_shap...  69 us
    psum x1, blocking collectives, shards(): all_gains = lax.psum(jnp.stack(gain_sums), ('section', 'ctx', 'mp'))  68.1 us
    ppermute x40, starting transfers between devices, joint_step(): return lax.ppermute(block, ('section', 'ctx'), route)  49.8 us
    ppermute x32, starting transfers between devices, to_core(): return lax.ppermute(block, 'section', [(1 - core, core)])  48.6 us
  transfers between devices with their start and end apart: 206, of which 95 were waited for; matrix products, arithmetic and copies ran while one was open for 21% of the time, Pallas kernels for 8%

profile of v1, /device:TPU:0, one launch (start us, length us, event | category | flops | bytes accessed | tf_op | source)
XLA Modules:
  0.0 1415.9 jit_solution(1437673666872414372)
XLA Ops:
  36.5 22.2 %all-gather.5.cloned.1.call-done = bf16[1,512,2048]{2,1,0:T(8,128)(2,1)} async-done(((bf16[1,128,2048]{2,1,0:T(8,128)(2,1)}), bf16[1,512,2048]{2,1,0:T(8,128)(2,1)}) %all-gather.5.cloned.1.call-update) | async-done | bytes 2097168 | tf_op jit(solution)/shard_map/all_gather | solution.py:510
  82.3 23.4 %all-gather.7.cloned.1.call-done = bf16[1,512,2048]{2,1,0:T(8,128)(2,1)} async-done(((bf16[1,128,2048]{2,1,0:T(8,128)(2,1)}), bf16[1,512,2048]{2,1,0:T(8,128)(2,1)}) %all-gather.7.cloned.1.call-update) | async-done | bytes 2097168 | tf_op jit(solution)/shard_map/all_gather | solution.py:510
  130.4 7.7 collective-permute-done.38
  157.5 8.1 collective-permute-done.11
  165.9 9.0 collective-permute-done.12
  175.0 8.3 collective-permute-done.13
  192.4 7.9 collective-permute-done.42
  200.3 8.1 collective-permute-done.43
  209.9 9.0 broadcast_select_fusion
  218.9 9.2 broadcast_select_fusion.1
  228.2 9.1 broadcast_select_fusion.2
  254.5 7.3 collective-permute-done.44
  288.4 10.0 collective-permute-done.21
  298.4 8.1 collective-permute-done.22
  367.6 10.8 collective-permute-done.53
  436.2 9.1 collective-permute-done.57
  479.3 16.8 %convolution_convert_fusion = bf16[1024,3072]{1,0:T(8,128)(2,1)} fusion(bf16[512,2048]{1,0:T(8,128)(2,1)} %constant_dynamic-update-slice_fusion.40, s32[]{:T(128)S(6)} %select_n.558, bf16[256,1536]{1,0:T(8,128)(2,1)S(1)} %copy-done.254, bf16[256,1536]{1,0:T(8,128)(2,1)S(1)} %copy-done.239, bf16[256,1536]{1,0:T(8,128)(2,1)S(1)} %copy-done.250, ...), kind=kOutput, calls=%fused_computation.12 | convolution fusion | flops 3236954112 | bytes 10485764 | tf_op jit(solution)/shard_map/dot_general | solution.py:33
  499.4 7.7 collective-permute-done.95
  517.9 9.7 collective-permute-done.70
  527.9 8.1 collective-permute-done.71
  550.8 9.1 collective-permute-done.96
  605.2 8.5 collective-permute-done.102
  645.6 9.6 collective-permute-done.79
  657.9 8.0 collective-permute-done.80
  679.6 8.1 collective-permute-done.81
  687.7 8.1 collective-permute-done.105
  711.5 7.3 collective-permute-done.107
  726.8 7.5 convolution_convert_fusion.1
  749.0 7.4 collective-permute-done.83
  770.8 8.1 collective-permute-done.85
  779.4 15.5 %add_convert_fusion.1 = bf16[512,3072]{1,0:T(8,128)(2,1)} fusion(bf16[1024,3072]{1,0:T(8,128)(2,1)} %collective-permute-done.174, s32[]{:T(128)S(6)} %select_n.561, bf16[512,2048]{1,0:T(8,128)(2,1)} %constant_dynamic-update-slice_fusion.40, s32[]{:T(128)S(6)} %select_n.560, bf16[256,1536]{1,0:T(8,128)(2,1)S(1)} %copy-done.255, ...), kind=kOutput, calls=%fused_computation.3 | convolution fusion | flops 1627914240 | bytes 9961480 | tf_op jit(solution)/shard_map/dot_general | solution.py:33
  821.1 10.2 collective-permute-done.90
  836.8 9.8 collective-permute-done.113
  904.5 9.5 collective-permute-done.92
  931.5 10.8 collective-permute-done.197.refs_9_
  946.5 10.5 collective-permute-done.137.refs_9_
  961.8 43.4 %collective-permute-done.199.refs_11_ = bf16[192,2048]{1,0:T(8,128)(2,1)S(1)} collective-permute-done((bf16[192,2048]{1,0:T(8,128)(2,1)S(1)}, bf16[192,2048]{1,0:T(8,128)(2,1)S(1)}, u32[]{:S(2)}, u32[]{:S(2)}) %collective-permute-start.199) | collective-permute-done | bytes 786464 | tf_op jit(solution)/shard_map/ppermute | solution.py:263
  1007.8 15.4 %add_convert_fusion.3 = bf16[512,3072]{1,0:T(8,128)(2,1)} fusion(bf16[1024,3072]{1,0:T(8,128)(2,1)} %collective-permute-done.164, s32[]{:T(128)S(6)} %select_n.561, bf16[512,2048]{1,0:T(8,128)(2,1)S(1)} %copy-done.203, s32[]{:T(128)S(6)} %select_n.560, bf16[256,1536]{1,0:T(8,128)(2,1)S(1)} %copy-done.261, bf16[256,1536]{1,0:T(8,128)(2,1)S(1)} %copy-done.247, ...), kind=kOutput, calls=%fused_computation.5 | convolution fusion | flops 1627914240 | bytes 9961480 | tf_op jit(solution)/shard_map/dot_general | solution.py:33
  1062.9 27.1 %collective-permute-done.148.refs_2_ = bf16[64,2048]{1,0:T(8,128)(2,1)S(1)} collective-permute-done((bf16[64,2048]{1,0:T(8,128)(2,1)S(1)}, bf16[64,2048]{1,0:T(8,128)(2,1)S(1)}, u32[]{:S(2)}, u32[]{:S(2)}) %collective-permute-start.148) | collective-permute-done | bytes 262176 | tf_op jit(solution)/shard_map/ppermute | solution.py:263
  1107.2 14.7 %add_convert_fusion.2 = bf16[512,3072]{1,0:T(8,128)(2,1)S(1)} fusion(bf16[512,3072]{1,0:T(8,128)(2,1)S(1)} %collective-permute-done.165, bf16[1024,3072]{1,0:T(8,128)(2,1)} %collective-permute-done.164, s32[]{:T(128)S(6)} %select_n.559, bf16[512,2048]{1,0:T(8,128)(2,1)S(1)} %copy-done.203, s32[]{:T(128)S(6)} %select_n.557, ...), kind=kOutput, calls=%fused_computation.4 | convolution fusion | flops 1631059968 | bytes 13107208 | tf_op jit(solution)/shard_map/dot_general | solution.py:33
  1130.1 11.9 collective-permute-done.188.refs_2_
  1158.3 20.9 %collective-permute-done.127.refs_1_ = bf16[256,1024]{1,0:T(8,128)(2,1)S(1)} collective-permute-done((bf16[256,1024]{1,0:T(8,128)(2,1)S(1)}, bf16[256,1024]{1,0:T(8,128)(2,1)S(1)}, u32[]{:S(2)}, u32[]{:S(2)}) %collective-permute-start.127) | collective-permute-done | bytes 524320 | tf_op jit(solution)/shard_map/ppermute | solution.py:263
  1197.1 28.5 %collective-permute-done.177.refs_9_ = bf16[256,3072]{1,0:T(8,128)(2,1)} collective-permute-done((bf16[256,3072]{1,0:T(8,128)(2,1)S(1)}, bf16[256,3072]{1,0:T(8,128)(2,1)}, u32[]{:S(2)}, u32[]{:S(2)}) %collective-permute-start.177) | collective-permute-done | bytes 1572896 | tf_op jit(solution)/shard_map/ppermute | solution.py:263
  1233.2 21.9 %collective-permute-done.167.refs_1_ = bf16[256,3072]{1,0:T(8,128)(2,1)} collective-permute-done((bf16[256,3072]{1,0:T(8,128)(2,1)S(1)}, bf16[256,3072]{1,0:T(8,128)(2,1)}, u32[]{:S(2)}, u32[]{:S(2)}) %collective-permute-start.167) | collective-permute-done | bytes 1572896 | tf_op jit(solution)/shard_map/ppermute | solution.py:263
  1257.4 68.1 %psum.7 = f32[2,4352]{1,0:T(2,128)S(1)} all-reduce(f32[2,4352]{1,0:T(2,128)S(1)} %pad_maximum_fusion.28), channel_id=1, replica_groups=mesh['section'=2,'ctx'=4,'mp'=4] {'section','ctx','mp'}, use_global_device_ids=true, to_apply=%region_26.28 | all-reduce | flops 8704 | bytes 69632 | tf_op jit(solution)/shard_map/psum | solution.py:634
  1344.0 19.8 %shard_map.253 = (f32[2048,512]{1,0:T(8,128)}, f32[2048,256]{1,0:T(8,128)}, f32[2048,256]{1,0:T(8,128)}) custom-call(s32[9]{0:T(128)S(1)} %stack.75.place, bf16[256,1024]{1,0:T(8,128)(2,1)S(1)} %add_convert_fusion.17.refs_0_, bf16[256,1024]{1,0:T(8,128)(2,1)S(1)} %copy-done.23, bf16[256,1024]{1,0:T(8,128)(2,1)} %collective-permute-done.128.refs_2_, ...), custom_call_target="tpu_custom_call" | custom-call | bytes 12582912 | tf_op jit(solution)/shard_map/pallas_call | solution.py:203
  1363.8 17.8 %shard_map.256 = f32[1536,2048]{1,0:T(8,128)} custom-call(s32[9]{0:T(128)S(1)} %stack.75.place, bf16[192,2048]{1,0:T(8,128)(2,1)S(1)} %add_convert_fusion.15.refs_0_, bf16[192,2048]{1,0:T(8,128)(2,1)} %collective-permute-done.187.refs_1_, bf16[192,2048]{1,0:T(8,128)(2,1)S(1)} %copy-done.13, bf16[192,2048]{1,0:T(8,128)(2,1)S(1)} %copy-done.15, ...), custom_call_target="tpu_custom_call" | custom-call | bytes 18874368 | tf_op jit(solution)/shard_map/pallas_call | solution.py:203
  1382.8 26.0 %shard_map.255 = (f32[2048,1536]{1,0:T(8,128)}, f32[2048,1536]{1,0:T(8,128)}) custom-call(s32[9]{0:T(128)S(1)} %stack.75.place, bf16[256,3072]{1,0:T(8,128)(2,1)S(1)} %copy-done.9, bf16[256,3072]{1,0:T(8,128)(2,1)} %collective-permute-done.167.refs_1_, bf16[256,3072]{1,0:T(8,128)(2,1)} %collective-permute-done.168.refs_2_, ...), custom_call_target="tpu_custom_call" | custom-call | bytes 37748736 | tf_op jit(solution)/shard_map/pallas_call | solution.py:203
  (1250 shorter events, 720.4 us)
Async XLA Ops:
  7.2 51.5 %all-gather.5.cloned.1.call-start = ((), (), s32[]{:S(2)}) async-start(), calls=%async_computation | async-start | bytes 2621440 | tf_op jit(solution)/shard_map/all_gather | solution.py:510
  9.3 96.4 %all-gather.7.cloned.1.call-start = ((), (), s32[]{:S(2)}) async-start(), calls=%async_computation.1 | async-start | bytes 2621440 | tf_op jit(solution)/shard_map/all_gather | solution.py:510
  21.2 188.7 %collective-permute-start.16 = (bf16[1536,2048]{1,0:T(8,128)(2,1)}, bf16[1536,2048]{1,0:T(8,128)(2,1)}, u32[]{:S(2)}, u32[]{:S(2)}) collective-permute-start(bf16[1536,2048]{1,0:T(8,128)(2,1)} %bitcast.190), channel_id=1, source_target_pairs={{0,16},{16,0},{1,17},{17,1},{2,18},{18,2},{3,19},{19,3},{4,20},{20... | collective-permute-start | bytes 18874376 | tf_op jit(solution)/shard_map/ppermute | solution.py:222
  70.8 41.1 %collective-permute-start.6 = (bf16[256,512]{1,0:T(8,128)(2,1)}, bf16[256,512]{1,0:T(8,128)(2,1)}, u32[]{:S(2)}, u32[]{:S(2)}) collective-permute-start(bf16[256,512]{1,0:T(8,128)(2,1)} %get-tuple-element.84.refs_0_), channel_id=1, source_target_pairs={{0,12},{4,8},{8,4},{12,0},{1,13},{5,9},{9,5},{13,1},{2,14},{6,10},... | collective-permute-start | bytes 786440 | tf_op jit(solution)/shard_map/ppermute | solution.py:254
  73.3 40.0 %collective-permute-start.5 = (bf16[256,512]{1,0:T(8,128)(2,1)}, bf16[256,512]{1,0:T(8,128)(2,1)}, u32[]{:S(2)}, u32[]{:S(2)}) collective-permute-start(bf16[256,512]{1,0:T(8,128)(2,1)} %get-tuple-element.84.refs_0_), channel_id=1, source_target_pairs={{0,8},{4,12},{8,0},{12,4},{1,9},{5,13},{9,1},{13,5},{2,10},{6,14},... | collective-permute-start | bytes 786440 | tf_op jit(solution)/shard_map/ppermute | solution.py:254
  73.9 40.9 %collective-permute-start.4 = (bf16[256,512]{1,0:T(8,128)(2,1)}, bf16[256,512]{1,0:T(8,128)(2,1)}, u32[]{:S(2)}, u32[]{:S(2)}) collective-permute-start(bf16[256,512]{1,0:T(8,128)(2,1)} %get-tuple-element.84.refs_0_), channel_id=1, source_target_pairs={{0,4},{4,0},{8,12},{12,8},{1,5},{5,1},{9,13},{13,9},{2,6},{6,2},{1... | collective-permute-start | bytes 786440 | tf_op jit(solution)/shard_map/ppermute | solution.py:254
  79.8 42.2 %collective-permute-start.37 = (bf16[256,512]{1,0:T(8,128)(2,1)}, bf16[256,512]{1,0:T(8,128)(2,1)S(1)}, u32[]{:S(2)}, u32[]{:S(2)}) collective-permute-start(bf16[256,512]{1,0:T(8,128)(2,1)} %get-tuple-element.90.refs_0_), channel_id=1, source_target_pairs={{0,12},{4,8},{8,4},{12,0},{1,13},{5,9},{9,5},{13,1},{2,14},{6,10},... | collective-permute-start | bytes 786440 | tf_op jit(solution)/shard_map/ppermute | solution.py:254
  122.0 96.9 %collective-permute-start.15 = (bf16[2048,1536]{1,0:T(8,128)(2,1)}, bf16[2048,1536]{1,0:T(8,128)(2,1)}, u32[]{:S(2)}, u32[]{:S(2)}) collective-permute-start(bf16[2048,1536]{1,0:T(8,128)(2,1)} %bitcast.191), channel_id=1, source_target_pairs={{0,16},{16,0},{1,17},{17,1},{2,18},{18,2},{3,19},{19,3},{4,20},{20... | collective-permute-start | bytes 18874376 | tf_op jit(solution)/shard_map/ppermute | solution.py:222
  122.1 106.1 %collective-permute-start.14 = (bf16[2048,1536]{1,0:T(8,128)(2,1)}, bf16[2048,1536]{1,0:T(8,128)(2,1)}, u32[]{:S(2)}, u32[]{:S(2)}) collective-permute-start(bf16[2048,1536]{1,0:T(8,128)(2,1)} %bitcast.194), channel_id=1, source_target_pairs={{0,16},{16,0},{1,17},{17,1},{2,18},{18,2},{3,19},{19,3},{4,20},{20... | collective-permute-start | bytes 18874376 | tf_op jit(solution)/shard_map/ppermute | solution.py:222
  436.2 109.9 %collective-permute-start.34 = (bf16[64,2048]{1,0:T(8,128)(2,1)}, bf16[64,2048]{1,0:T(8,128)(2,1)}, u32[]{:S(2)}, u32[]{:S(2)}) collective-permute-start(bf16[64,2048]{1,0:T(8,128)(2,1)} %add_convert_fusion.44), channel_id=1, source_target_pairs={{0,1},{1,2},{2,3},{3,0},{4,5},{5,6},{6,7},{7,4},{8,9},{9,10},{10,1... | collective-permute-start | bytes 786440 | tf_op jit(solution)/shard_map/ppermute | solution.py:231
  445.4 54.0 %collective-permute-start.68 = (bf16[64,2048]{1,0:T(8,128)(2,1)S(1)}, bf16[64,2048]{1,0:T(8,128)(2,1)S(1)}, u32[]{:S(2)}, u32[]{:S(2)}) collective-permute-start(bf16[64,2048]{1,0:T(8,128)(2,1)S(1)} %add_convert_fusion.34), channel_id=1, source_target_pairs={{0,1},{1,2},{2,3},{3,0},{4,5},{5,6},{6,7},{7,4},{8,9},{9,10},{10,1... | collective-permute-start | bytes 786440 | tf_op jit(solution)/shard_map/ppermute | solution.py:231
  474.5 160.9 %collective-permute-start.194 = (bf16[768,2048]{1,0:T(8,128)(2,1)}, bf16[768,2048]{1,0:T(8,128)(2,1)}, u32[]{:S(2)}, u32[]{:S(2)}) collective-permute-start(bf16[768,2048]{1,0:T(8,128)(2,1)} %convolution_convert_fusion.2), channel_id=1, source_target_pairs={{0,16},{16,0},{1,17},{17,1},{2,18},{18,2},{3,19},{19,3},{4,20},{20... | collective-permute-start | bytes 9437192 | tf_op jit(solution)/shard_map/ppermute | solution.py:222
  593.4 185.9 %collective-permute-start.174 = (bf16[1024,3072]{1,0:T(8,128)(2,1)}, bf16[1024,3072]{1,0:T(8,128)(2,1)}, u32[]{:S(2)}, u32[]{:S(2)}) collective-permute-start(bf16[1024,3072]{1,0:T(8,128)(2,1)} %convolution_convert_fusion), channel_id=1, source_target_pairs={{0,16},{16,0},{1,17},{17,1},{2,18},{18,2},{3,19},{19,3},{4,20},{20... | collective-permute-start | bytes 18874376 | tf_op jit(solution)/shard_map/ppermute | solution.py:222
  625.8 228.3 %collective-permute-start.63 = (bf16[64,2048]{1,0:T(8,128)(2,1)}, bf16[64,2048]{1,0:T(8,128)(2,1)}, u32[]{:S(2)}, u32[]{:S(2)}) collective-permute-start(bf16[64,2048]{1,0:T(8,128)(2,1)} %broadcast_select_fusion.20), channel_id=1, source_target_pairs={{0,2},{1,0},{2,3},{3,1},{4,6},{5,4},{6,7},{7,5},{8,10},{9,8},{10,1... | collective-permute-start | bytes 786440 | tf_op jit(solution)/shard_map/ppermute | solution.py:474
  632.2 64.4 %collective-permute-start.134 = (bf16[1024,1024]{1,0:T(8,128)(2,1)}, bf16[1024,1024]{1,0:T(8,128)(2,1)}, u32[]{:S(2)}, u32[]{:S(2)}) collective-permute-start(bf16[1024,1024]{1,0:T(8,128)(2,1)} %convolution_convert_fusion.10), channel_id=1, source_target_pairs={{0,16},{16,0},{1,17},{17,1},{2,18},{18,2},{3,19},{19,3},{4,20},{20... | collective-permute-start | bytes 6291464 | tf_op jit(solution)/shard_map/ppermute | solution.py:222
  655.3 44.6 %collective-permute-start.195 = (bf16[384,2048]{1,0:T(8,128)(2,1)}, bf16[384,2048]{1,0:T(8,128)(2,1)}, u32[]{:S(2)}, u32[]{:S(2)}) collective-permute-start(bf16[384,2048]{1,0:T(8,128)(2,1)} %add_convert_fusion.5), channel_id=1, source_target_pairs={{0,4},{4,0},{8,12},{12,8},{16,24},{20,28},{24,16},{28,20},{1,5},{5... | collective-permute-start | bytes 4718600 | tf_op jit(solution)/shard_map/ppermute | solution.py:263
  699.8 62.7 %collective-permute-start.135 = (bf16[512,1024]{1,0:T(8,128)(2,1)}, bf16[512,1024]{1,0:T(8,128)(2,1)}, u32[]{:S(2)}, u32[]{:S(2)}) collective-permute-start(bf16[512,1024]{1,0:T(8,128)(2,1)} %add_convert_fusion.11), channel_id=1, source_target_pairs={{0,4},{4,0},{8,12},{12,8},{16,24},{20,28},{24,16},{28,20},{1,5},{5... | collective-permute-start | bytes 3145736 | tf_op jit(solution)/shard_map/ppermute | solution.py:263
  707.3 39.2 %collective-permute-start.196 = (bf16[192,2048]{1,0:T(8,128)(2,1)}, bf16[192,2048]{1,0:T(8,128)(2,1)}, u32[]{:S(2)}, u32[]{:S(2)}) collective-permute-start(bf16[192,2048]{1,0:T(8,128)(2,1)} %constant_dynamic-slice_fusion.8), channel_id=1, source_target_pairs={{0,8},{4,12},{8,0},{12,4},{16,20},{20,16},{24,28},{28,24},{1,9},{5... | collective-permute-start | bytes 2359304 | tf_op jit(solution)/shard_map/ppermute | solution.py:263
  766.1 41.2 %collective-permute-start.136 = (bf16[256,1024]{1,0:T(8,128)(2,1)}, bf16[256,1024]{1,0:T(8,128)(2,1)}, u32[]{:S(2)}, u32[]{:S(2)}) collective-permute-start(bf16[256,1024]{1,0:T(8,128)(2,1)} %constant_dynamic-slice_fusion.5), channel_id=1, source_target_pairs={{0,8},{4,12},{8,0},{12,4},{16,20},{20,16},{24,28},{28,24},{1,9},{5... | collective-permute-start | bytes 1572872 | tf_op jit(solution)/shard_map/ppermute | solution.py:263
  809.1 45.2 %collective-permute-start.65 = (bf16[64,2048]{1,0:T(8,128)(2,1)}, bf16[64,2048]{1,0:T(8,128)(2,1)S(1)}, u32[]{:S(2)}, u32[]{:S(2)}) collective-permute-start(bf16[64,2048]{1,0:T(8,128)(2,1)} %broadcast_select_fusion.18), channel_id=1, source_target_pairs={{0,18},{1,16},{2,19},{3,17},{16,2},{17,0},{18,3},{19,1},{4,22},{5,... | collective-permute-start | bytes 786440 | tf_op jit(solution)/shard_map/ppermute | solution.py:478
  813.5 102.1 %collective-permute-start.184 = (bf16[768,2048]{1,0:T(8,128)(2,1)}, bf16[768,2048]{1,0:T(8,128)(2,1)}, u32[]{:S(2)}, u32[]{:S(2)}) collective-permute-start(bf16[768,2048]{1,0:T(8,128)(2,1)} %convolution_convert_fusion.3), channel_id=1, source_target_pairs={{0,16},{16,0},{1,17},{17,1},{2,18},{18,2},{3,19},{19,3},{4,20},{20... | collective-permute-start | bytes 9437192 | tf_op jit(solution)/shard_map/ppermute | solution.py:222
  831.3 176.4 %collective-permute-start.164 = (bf16[1024,3072]{1,0:T(8,128)(2,1)}, bf16[1024,3072]{1,0:T(8,128)(2,1)}, u32[]{:S(2)}, u32[]{:S(2)}) collective-permute-start(bf16[1024,3072]{1,0:T(8,128)(2,1)} %convolution_convert_fusion.1), channel_id=1, source_target_pairs={{0,16},{16,0},{1,17},{17,1},{2,18},{18,2},{3,19},{19,3},{4,20},{20... | collective-permute-start | bytes 18874376 | tf_op jit(solution)/shard_map/ppermute | solution.py:222
  893.3 35.9 %collective-permute-start.144 = (bf16[256,2048]{1,0:T(8,128)(2,1)S(1)}, bf16[256,2048]{1,0:T(8,128)(2,1)S(1)}, u32[]{:S(2)}, u32[]{:S(2)}) collective-permute-start(bf16[256,2048]{1,0:T(8,128)(2,1)S(1)} %convolution_convert_fusion.5), channel_id=1, source_target_pairs={{0,16},{16,0},{1,17},{17,1},{2,18},{18,2},{3,19},{19,3},{4,20},{20... | collective-permute-start | bytes 3145736 | tf_op jit(solution)/shard_map/ppermute | solution.py:222
  957.0 83.3 %collective-permute-start.175 = (bf16[512,3072]{1,0:T(8,128)(2,1)}, bf16[512,3072]{1,0:T(8,128)(2,1)}, u32[]{:S(2)}, u32[]{:S(2)}) collective-permute-start(bf16[512,3072]{1,0:T(8,128)(2,1)} %add_convert_fusion.1), channel_id=1, source_target_pairs={{0,4},{4,0},{8,12},{12,8},{16,24},{20,28},{24,16},{28,20},{1,5},{5... | collective-permute-start | bytes 9437192 | tf_op jit(solution)/shard_map/ppermute | solution.py:263
  959.0 70.5 %collective-permute-start.124 = (bf16[1024,1024]{1,0:T(8,128)(2,1)}, bf16[1024,1024]{1,0:T(8,128)(2,1)S(1)}, u32[]{:S(2)}, u32[]{:S(2)}) collective-permute-start(bf16[1024,1024]{1,0:T(8,128)(2,1)} %convolution_convert_fusion.11), channel_id=1, source_target_pairs={{0,16},{16,0},{1,17},{17,1},{2,18},{18,2},{3,19},{19,3},{4,20},{20... | collective-permute-start | bytes 6291464 | tf_op jit(solution)/shard_map/ppermute | solution.py:222
  959.1 46.2 %collective-permute-start.199 = (bf16[192,2048]{1,0:T(8,128)(2,1)S(1)}, bf16[192,2048]{1,0:T(8,128)(2,1)S(1)}, u32[]{:S(2)}, u32[]{:S(2)}) collective-permute-start(bf16[192,2048]{1,0:T(8,128)(2,1)S(1)} %collective-permute-done.197.refs_9_), channel_id=1, source_target_pairs={{0,4},{4,0},{8,12},{12,8},{16,24},{20,28},{24,16},{28,20},{1,5},{5... | collective-permute-start | bytes 2359304 | tf_op jit(solution)/shard_map/ppermute | solution.py:263
  959.3 72.4 %collective-permute-start.185 = (bf16[384,2048]{1,0:T(8,128)(2,1)}, bf16[384,2048]{1,0:T(8,128)(2,1)S(1)}, u32[]{:S(2)}, u32[]{:S(2)}) collective-permute-start(bf16[384,2048]{1,0:T(8,128)(2,1)} %add_convert_fusion.7), channel_id=1, source_target_pairs={{0,4},{4,0},{8,12},{12,8},{16,24},{20,28},{24,16},{28,20},{1,5},{5... | collective-permute-start | bytes 4718600 | tf_op jit(solution)/shard_map/ppermute | solution.py:263
  1023.2 82.8 %collective-permute-start.165 = (bf16[512,3072]{1,0:T(8,128)(2,1)}, bf16[512,3072]{1,0:T(8,128)(2,1)S(1)}, u32[]{:S(2)}, u32[]{:S(2)}) collective-permute-start(bf16[512,3072]{1,0:T(8,128)(2,1)} %add_convert_fusion.3), channel_id=1, source_target_pairs={{0,4},{4,0},{8,12},{12,8},{16,24},{20,28},{24,16},{28,20},{1,5},{5... | collective-permute-start | bytes 9437192 | tf_op jit(solution)/shard_map/ppermute | solution.py:263
  1038.2 54.5 %collective-permute-start.125 = (bf16[512,1024]{1,0:T(8,128)(2,1)S(1)}, bf16[512,1024]{1,0:T(8,128)(2,1)S(1)}, u32[]{:S(2)}, u32[]{:S(2)}) collective-permute-start(bf16[512,1024]{1,0:T(8,128)(2,1)S(1)} %add_convert_fusion.13), channel_id=1, source_target_pairs={{0,4},{4,0},{8,12},{12,8},{16,24},{20,28},{24,16},{28,20},{1,5},{5... | collective-permute-start | bytes 3145736 | tf_op jit(solution)/shard_map/ppermute | solution.py:263
  1090.0 37.6 %collective-permute-start.176 = (bf16[256,3072]{1,0:T(8,128)(2,1)S(1)}, bf16[256,3072]{1,0:T(8,128)(2,1)S(1)}, u32[]{:S(2)}, u32[]{:S(2)}) collective-permute-start(bf16[256,3072]{1,0:T(8,128)(2,1)S(1)} %constant_dynamic-slice_fusion), channel_id=1, source_target_pairs={{0,8},{4,12},{8,0},{12,4},{16,20},{20,16},{24,28},{28,24},{1,9},{5... | collective-permute-start | bytes 4718600 | tf_op jit(solution)/shard_map/ppermute | solution.py:263
  1125.6 58.6 %collective-permute-start.166 = (bf16[256,3072]{1,0:T(8,128)(2,1)}, bf16[256,3072]{1,0:T(8,128)(2,1)}, u32[]{:S(2)}, u32[]{:S(2)}) collective-permute-start(bf16[256,3072]{1,0:T(8,128)(2,1)} %constant_dynamic-slice_fusion.1), channel_id=1, source_target_pairs={{0,8},{4,12},{8,0},{12,4},{16,20},{20,16},{24,28},{28,24},{1,9},{5... | collective-permute-start | bytes 4718600 | tf_op jit(solution)/shard_map/ppermute | solution.py:263
  1142.0 39.1 %collective-permute-start.192 = (bf16[192,2048]{1,0:T(8,128)(2,1)S(1)}, bf16[192,2048]{1,0:T(8,128)(2,1)}, u32[]{:S(2)}, u32[]{:S(2)}) collective-permute-start(bf16[192,2048]{1,0:T(8,128)(2,1)S(1)} %collective-permute-done.188.refs_2_), channel_id=1, source_target_pairs={{16,0},{17,1},{18,2},{19,3},{20,4},{21,5},{22,6},{23,7},{24,8},{25... | collective-permute-start | bytes 2359304 | tf_op jit(solution)/shard_map/ppermute | solution.py:226
  1144.7 37.7 %collective-permute-start.191 = (bf16[192,2048]{1,0:T(8,128)(2,1)}, bf16[192,2048]{1,0:T(8,128)(2,1)}, u32[]{:S(2)}, u32[]{:S(2)}) collective-permute-start(bf16[192,2048]{1,0:T(8,128)(2,1)} %collective-permute-done.187.refs_1_), channel_id=1, source_target_pairs={{16,0},{17,1},{18,2},{19,3},{20,4},{21,5},{22,6},{23,7},{24,8},{25... | collective-permute-start | bytes 2359304 | tf_op jit(solution)/shard_map/ppermute | solution.py:226
  1187.5 41.2 %collective-permute-start.178 = (bf16[256,3072]{1,0:T(8,128)(2,1)S(1)}, bf16[256,3072]{1,0:T(8,128)(2,1)}, u32[]{:S(2)}, u32[]{:S(2)}) collective-permute-start(bf16[256,3072]{1,0:T(8,128)(2,1)S(1)} %add_convert_fusion.8.refs_8_), channel_id=1, source_target_pairs={{0,4},{4,0},{8,12},{12,8},{16,24},{20,28},{24,16},{28,20},{1,5},{5... | collective-permute-start | bytes 4718600 | tf_op jit(solution)/shard_map/ppermute | solution.py:263
  1188.2 37.4 %collective-permute-start.177 = (bf16[256,3072]{1,0:T(8,128)(2,1)S(1)}, bf16[256,3072]{1,0:T(8,128)(2,1)}, u32[]{:S(2)}, u32[]{:S(2)}) collective-permute-start(bf16[256,3072]{1,0:T(8,128)(2,1)S(1)} %add_convert_fusion.8.refs_8_), channel_id=1, source_target_pairs={{0,8},{4,12},{8,0},{12,4},{16,20},{20,16},{24,28},{28,24},{1,9},{5... | collective-permute-start | bytes 4718600 | tf_op jit(solution)/shard_map/ppermute | solution.py:263
  1189.2 65.9 %collective-permute-start.167 = (bf16[256,3072]{1,0:T(8,128)(2,1)S(1)}, bf16[256,3072]{1,0:T(8,128)(2,1)}, u32[]{:S(2)}, u32[]{:S(2)}) collective-permute-start(bf16[256,3072]{1,0:T(8,128)(2,1)S(1)} %add_convert_fusion.9.refs_0_), channel_id=1, source_target_pairs={{0,8},{4,12},{8,0},{12,4},{16,20},{20,16},{24,28},{28,24},{1,9},{5... | collective-permute-start | bytes 4718600 | tf_op jit(solution)/shard_map/ppermute | solution.py:263
  1191.7 40.8 %collective-permute-start.193 = (bf16[192,2048]{1,0:T(8,128)(2,1)S(1)}, bf16[192,2048]{1,0:T(8,128)(2,1)S(1)}, u32[]{:S(2)}, u32[]{:S(2)}) collective-permute-start(bf16[192,2048]{1,0:T(8,128)(2,1)S(1)} %collective-permute-done.189.refs_3_), channel_id=1, source_target_pairs={{16,0},{17,1},{18,2},{19,3},{20,4},{21,5},{22,6},{23,7},{24,8},{25... | collective-permute-start | bytes 2359304 | tf_op jit(solution)/shard_map/ppermute | solution.py:226
  1194.0 36.0 %collective-permute-start.133 = (bf16[256,1024]{1,0:T(8,128)(2,1)S(1)}, bf16[256,1024]{1,0:T(8,128)(2,1)S(1)}, u32[]{:S(2)}, u32[]{:S(2)}) collective-permute-start(bf16[256,1024]{1,0:T(8,128)(2,1)S(1)} %collective-permute-done.129.refs_3_), channel_id=1, source_target_pairs={{16,0},{17,1},{18,2},{19,3},{20,4},{21,5},{22,6},{23,7},{24,8},{25... | collective-permute-start | bytes 1572872 | tf_op jit(solution)/shard_map/ppermute | solution.py:226
  1225.6 103.3 %collective-permute-start.181 = (bf16[256,3072]{1,0:T(8,128)(2,1)}, bf16[256,3072]{1,0:T(8,128)(2,1)}, u32[]{:S(2)}, u32[]{:S(2)}) collective-permute-start(bf16[256,3072]{1,0:T(8,128)(2,1)} %collective-permute-done.177.refs_9_), channel_id=1, source_target_pairs={{0,16},{1,17},{2,18},{3,19},{4,20},{5,21},{6,22},{7,23},{8,24},{9,... | collective-permute-start | bytes 4718600 | tf_op jit(solution)/shard_map/ppermute | solution.py:226
  1228.7 97.6 %collective-permute-start.179 = (bf16[256,3072]{1,0:T(8,128)(2,1)}, bf16[256,3072]{1,0:T(8,128)(2,1)}, u32[]{:S(2)}, u32[]{:S(2)}) collective-permute-start(bf16[256,3072]{1,0:T(8,128)(2,1)} %collective-permute-done.177.refs_9_), channel_id=1, source_target_pairs={{0,4},{4,0},{8,12},{12,8},{16,24},{20,28},{24,16},{28,20},{1,5},{5... | collective-permute-start | bytes 4718600 | tf_op jit(solution)/shard_map/ppermute | solution.py:263
  1230.0 97.6 %collective-permute-start.182 = (bf16[256,3072]{1,0:T(8,128)(2,1)}, bf16[256,3072]{1,0:T(8,128)(2,1)}, u32[]{:S(2)}, u32[]{:S(2)}) collective-permute-start(bf16[256,3072]{1,0:T(8,128)(2,1)} %collective-permute-done.178.refs_10_), channel_id=1, source_target_pairs={{0,16},{1,17},{2,18},{3,19},{4,20},{5,21},{6,22},{7,23},{8,24},{9,... | collective-permute-start | bytes 4718600 | tf_op jit(solution)/shard_map/ppermute | solution.py:226
  1232.4 97.8 %collective-permute-start.168 = (bf16[256,3072]{1,0:T(8,128)(2,1)S(1)}, bf16[256,3072]{1,0:T(8,128)(2,1)}, u32[]{:S(2)}, u32[]{:S(2)}) collective-permute-start(bf16[256,3072]{1,0:T(8,128)(2,1)S(1)} %add_convert_fusion.9.refs_0_), channel_id=1, source_target_pairs={{0,4},{4,0},{8,12},{12,8},{16,24},{20,28},{24,16},{28,20},{1,5},{5... | collective-permute-start | bytes 4718600 | tf_op jit(solution)/shard_map/ppermute | solution.py:263
  1255.1 76.5 %collective-permute-start.169 = (bf16[256,3072]{1,0:T(8,128)(2,1)}, bf16[256,3072]{1,0:T(8,128)(2,1)}, u32[]{:S(2)}, u32[]{:S(2)}) collective-permute-start(bf16[256,3072]{1,0:T(8,128)(2,1)} %collective-permute-done.167.refs_1_), channel_id=1, source_target_pairs={{0,4},{4,0},{8,12},{12,8},{16,24},{20,28},{24,16},{28,20},{1,5},{5... | collective-permute-start | bytes 4718600 | tf_op jit(solution)/shard_map/ppermute | solution.py:263
  1326.3 55.4 %collective-permute-start.183 = (bf16[256,3072]{1,0:T(8,128)(2,1)}, bf16[256,3072]{1,0:T(8,128)(2,1)S(1)}, u32[]{:S(2)}, u32[]{:S(2)}) collective-permute-start(bf16[256,3072]{1,0:T(8,128)(2,1)} %collective-permute-done.179.refs_11_), channel_id=1, source_target_pairs={{0,16},{1,17},{2,18},{3,19},{4,20},{5,21},{6,22},{7,23},{8,24},{9,... | collective-permute-start | bytes 4718600 | tf_op jit(solution)/shard_map/ppermute | solution.py:226
  1327.7 54.0 %collective-permute-start.170 = (bf16[256,3072]{1,0:T(8,128)(2,1)S(1)}, bf16[256,3072]{1,0:T(8,128)(2,1)}, u32[]{:S(2)}, u32[]{:S(2)}) collective-permute-start(bf16[256,3072]{1,0:T(8,128)(2,1)S(1)} %add_convert_fusion.9.refs_0_), channel_id=1, source_target_pairs={{16,0},{17,1},{18,2},{19,3},{20,4},{21,5},{22,6},{23,7},{24,8},{25... | collective-permute-start | bytes 4718600 | tf_op jit(solution)/shard_map/ppermute | solution.py:226
  1329.0 52.7 %collective-permute-start.171 = (bf16[256,3072]{1,0:T(8,128)(2,1)}, bf16[256,3072]{1,0:T(8,128)(2,1)}, u32[]{:S(2)}, u32[]{:S(2)}) collective-permute-start(bf16[256,3072]{1,0:T(8,128)(2,1)} %collective-permute-done.167.refs_1_), channel_id=1, source_target_pairs={{16,0},{17,1},{18,2},{19,3},{20,4},{21,5},{22,6},{23,7},{24,8},{25... | collective-permute-start | bytes 4718600 | tf_op jit(solution)/shard_map/ppermute | solution.py:226
  1330.3 51.4 %collective-permute-start.172 = (bf16[256,3072]{1,0:T(8,128)(2,1)}, bf16[256,3072]{1,0:T(8,128)(2,1)}, u32[]{:S(2)}, u32[]{:S(2)}) collective-permute-start(bf16[256,3072]{1,0:T(8,128)(2,1)} %collective-permute-done.168.refs_2_), channel_id=1, source_target_pairs={{16,0},{17,1},{18,2},{19,3},{20,4},{21,5},{22,6},{23,7},{24,8},{25... | collective-permute-start | bytes 4718600 | tf_op jit(solution)/shard_map/ppermute | solution.py:226
  1331.6 50.1 %collective-permute-start.173 = (bf16[256,3072]{1,0:T(8,128)(2,1)}, bf16[256,3072]{1,0:T(8,128)(2,1)}, u32[]{:S(2)}, u32[]{:S(2)}) collective-permute-start(bf16[256,3072]{1,0:T(8,128)(2,1)} %collective-permute-done.169.refs_3_), channel_id=1, source_target_pairs={{16,0},{17,1},{18,2},{19,3},{20,4},{21,5},{22,6},{23,7},{24,8},{25... | collective-permute-start | bytes 4718600 | tf_op jit(solution)/shard_map/ppermute | solution.py:226
  (442 other events, 8248.0 us)
Sparse Core Ops, SparseCore 0:
  10.2 48.4 all-gather.4
  60.9 44.8 all-gather.6

commit v2 on v1

v2 whole, which is shorter than its diff:
```python
import functools
from types import SimpleNamespace

import jax
import jax.numpy as jnp
from jax import lax
from jax.experimental import pallas as pl
from jax.experimental.pallas import tpu as pltpu
from jax.sharding import PartitionSpec as P

HD = 128
LANES = 128
MB = 2
SEQS = 2
STRETCH = 128
EPSILON = 1e-06
ROPE_BASE = 1000000.0
MASKED_SCORE = -1e30
SCALING = HD ** (-0.5)
LOW = jnp.bfloat16
F32 = jnp.float32
VMEM_SPARE = 12 * 1024 * 1024
VMEM_LEAST = 50 * 1024 * 1024


def dot_nn(left, right):
    return lax.dot_general(left, right, (((1,), (0,)), ((), ())), preferred_element_type=F32)


def dot_nt(left, right):
    return lax.dot_general(left, right, (((1,), (1,)), ((), ())), preferred_element_type=F32)


def dot_tn(left, right):
    return lax.dot_general(left, right, (((0,), (0,)), ((), ())), preferred_element_type=F32)


def kernel_call(body, out_shape, flops, args, layer, weights):
    held = [jax.ShapeDtypeStruct(x.shape, x.dtype) for x in (*args, *[w[0] for w in weights])]
    moved = sum(x.size * x.dtype.itemsize for x in (*held, *out_shape))
    n_args, n_weights, n_out = len(args), len(weights), len(out_shape)

    def whole(*refs):
        ins, rest = refs[:n_args], refs[n_args:]
        pairs, rest = rest[: 2 * n_weights], rest[2 * n_weights :]
        outs, here, sems = rest[:n_out], rest[n_out:-1], rest[-1]
        home = lax.axis_index(CORES) == layer

        def copy(i, source):
            return pltpu.make_async_copy(source, here[i], sems.at[i])

        for i, ref in enumerate(ins):
            copy(i, ref).start()
        for which, taken in ((0, home), (1, jnp.logical_not(home))):

            @pl.when(taken)
            def _(which=which):
                for i in range(n_weights):
                    copy(n_args + i, pairs[2 * i + which]).start()

        def arrived(i):
            copy(n_args + i, pairs[2 * i]).wait()
            return here[n_args + i]

        for i, ref in enumerate(ins):
            copy(i, ref).wait()
        gets = [functools.partial(arrived, i) for i in range(n_weights)]
        body(*here[:n_args], *gets, *outs)

    vmem, hbm = pl.BlockSpec(memory_space=pltpu.VMEM), pl.BlockSpec(memory_space=pltpu.HBM)
    return pl.pallas_call(
        whole,
        out_shape=out_shape,
        in_specs=[hbm] * (n_args + 2 * n_weights),
        out_specs=[vmem] * n_out,
        scratch_shapes=[pltpu.VMEM(x.shape, x.dtype) for x in held]
        + [pltpu.SemaphoreType.DMA((len(held),))],
        compiler_params=pltpu.CompilerParams(vmem_limit_bytes=max(moved + VMEM_SPARE, VMEM_LEAST)),
        cost_estimate=pl.CostEstimate(flops=flops, bytes_accessed=moved, transcendentals=0),
    )(*args, *[ref for w in weights for ref in w])


def qkv_forward_body(q_width, x, gains, turns, get_qkv, proj, queries, kv):
    cos_full, sin_signed = turns[:, :HD], turns[:, HD:]

    def prepared(head, gain):
        scaling = lax.rsqrt(jnp.mean(head * head, axis=-1, keepdims=True) + EPSILON)
        normed = head * scaling * gain
        return (normed * cos_full + pltpu.roll(normed, HD // 2, 1) * sin_signed).astype(LOW)

    mixed = dot_nn(x[...], get_qkv()[...])
    both = proj.shape[1]
    proj[...] = mixed[:, :both]
    for at in range(0, q_width, HD):
        queries[:, at : at + HD] = prepared(mixed[:, at : at + HD], gains[:1, :])
    for at in range(q_width, both, HD):
        kv[:, at - q_width : at - q_width + HD] = prepared(mixed[:, at : at + HD], gains[1:, :])
    kv[:, both - q_width :] = mixed[:, both:].astype(LOW)


def mlp_forward_body(x, get_gate, get_up, get_down, gate, up, hidden, *parts):
    rows = x[...]
    gate_all = dot_nn(rows, get_gate()[...])
    up_all = dot_nn(rows, get_up()[...])
    gate[...] = gate_all.astype(LOW)
    up[...] = up_all.astype(LOW)
    hidden[...] = (jax.nn.silu(gate_all) * up_all).astype(LOW)
    store_product(parts, hidden[...], get_down(), dot_nn)


def mlp_back_body(branch, gate, up, get_down, get_gate, get_up, grad_gate, grad_up, *parts):
    grad_hidden = dot_nt(branch[...], get_down()[...])
    gate_all, up_all = gate[...].astype(F32), up[...].astype(F32)
    sig = jax.nn.sigmoid(gate_all)
    grad_gate[...] = (grad_hidden * up_all * sig * (1.0 + gate_all * (1.0 - sig))).astype(LOW)
    grad_up[...] = (grad_hidden * gate_all * sig).astype(LOW)
    w_gate, w_up = get_gate(), get_up()
    for at in range(0, w_gate.shape[0], 512):
        here = pl.ds(at, 512)
        total = dot_nt(grad_gate[...], w_gate[here, :]) + dot_nt(grad_up[...], w_up[here, :])
        store_columns(parts, here, total)


def store_columns(parts, here, rows):
    size = parts[0].shape[0]
    for i, part in enumerate(parts):
        part[:, here] = rows[i * size : (i + 1) * size].astype(LOW)


def store_product(parts, rows, weight, dot):
    for at in range(0, weight.shape[1], 512):
        here = pl.ds(at, 512)
        store_columns(parts, here, dot(rows, weight[:, here]))


def store_blocks(parts, rows):
    size = parts[0].shape[0]
    for i, part in enumerate(parts):
        part[...] = rows[i * size : (i + 1) * size].astype(LOW)


def attend_body(n_ctx, queries, *refs):
    blocks = refs[:n_ctx]
    q_pos, k_pos, get_out = refs[n_ctx : n_ctx + 3]
    attended, log_total, *parts = refs[n_ctx + 3 :]
    rows = queries.shape[0]
    kv_width = blocks[0].shape[1] // 2
    groups = queries.shape[1] // kv_width
    place = jnp.concatenate([q_pos[...]] * groups, axis=0)
    for kv_head in range(kv_width // HD):
        first = kv_head * groups
        stacked = jnp.concatenate(
            [queries[:, (first + i) * HD : (first + i + 1) * HD] for i in range(groups)], axis=0
        )
        at = kv_head * HD
        scores = []
        for j, block in enumerate(blocks):
            raw = dot_nt(stacked, block[:, at : at + HD]) * SCALING
            scores.append(jnp.where(k_pos[j : j + 1, :] <= place, raw, MASKED_SCORE))
        top = functools.reduce(
            jnp.maximum, [jnp.max(s, axis=1, keepdims=True) for s in scores]
        )
        total, running = 0.0, 0.0
        for s, block in zip(scores, blocks):
            weights = jnp.exp(s - top)
            total = total + jnp.sum(weights, axis=1, keepdims=True)
            running = running + dot_nn(
                weights.astype(LOW), block[:, kv_width + at : kv_width + at + HD]
            )
        result = (running / total).astype(LOW)
        logs = top + jnp.log(total)
        for i in range(groups):
            head = first + i
            attended[:, head * HD : (head + 1) * HD] = result[i * rows : (i + 1) * rows]
            log_total[:, head : head + 1] = logs[i * rows : (i + 1) * rows]
    store_blocks(parts, dot_nn(attended[...], get_out()[...]))


def attend_back_body(n_ctx, grad_rows, queries, *refs):
    blocks = refs[:n_ctx]
    q_pos, k_pos, attended, log_total, get_out, grad_q = refs[n_ctx : n_ctx + 6]
    grad_kv = refs[n_ctx + 6 :]
    rows = queries.shape[0]
    kv_width = blocks[0].shape[1] // 2
    groups = queries.shape[1] // kv_width
    grad_all = dot_nt(grad_rows[...], get_out()[...]).astype(LOW)
    place = jnp.concatenate([q_pos[...]] * groups, axis=0)
    for kv_head in range(kv_width // HD):
        heads = [kv_head * groups + i for i in range(groups)]
        stacked = jnp.concatenate([queries[:, h * HD : (h + 1) * HD] for h in heads], axis=0)
        grads = jnp.concatenate([grad_all[:, h * HD : (h + 1) * HD] for h in heads], axis=0)
        out_low = jnp.concatenate([attended[:, h * HD : (h + 1) * HD] for h in heads], axis=0)
        logs = jnp.concatenate([log_total[:, h : h + 1] for h in heads], axis=0)
        delta = jnp.sum(grads.astype(F32) * out_low.astype(F32), axis=1, keepdims=True)
        at = kv_head * HD
        total = 0.0
        for j, block in enumerate(blocks):
            keys = block[:, at : at + HD]
            values = block[:, kv_width + at : kv_width + at + HD]
            shifted = dot_nt(stacked, keys) * SCALING - logs
            probs = jnp.exp(jnp.where(k_pos[j : j + 1, :] <= place, shifted, MASKED_SCORE))
            grad_scores = (probs * (dot_nt(grads, values) - delta)).astype(LOW)
            total = total + dot_nn(grad_scores, keys)
            grad_kv[j][:, at : at + HD] = (dot_tn(grad_scores, stacked) * SCALING).astype(LOW)
            grad_kv[j][:, kv_width + at : kv_width + at + HD] = dot_tn(
                probs.astype(LOW), grads
            ).astype(LOW)
        for i, h in enumerate(heads):
            grad_q[:, h * HD : (h + 1) * HD] = total[i * rows : (i + 1) * rows] * SCALING


def qkv_back_body(n_ctx, grad_q, *refs):
    grad_kv = refs[:n_ctx]
    proj, gains, turns, get_qkv, mixed, grad_gains, *parts = refs[n_ctx:]
    cos_full, sin_signed = turns[:, :HD], turns[:, HD:]
    q_width = grad_q.shape[1]
    kv_width = proj.shape[1] - q_width

    def pulled(grad, head, gain):
        turned = grad * cos_full + pltpu.roll(grad * sin_signed, HD // 2, 1)
        scaling = lax.rsqrt(jnp.mean(head * head, axis=-1, keepdims=True) + EPSILON)
        inner = turned * gain
        back = scaling * inner - head * (
            scaling * scaling * scaling * jnp.mean(inner * head, axis=-1, keepdims=True)
        )
        return back.astype(LOW), jnp.sum(turned * head * scaling, axis=0, keepdims=True)

    total = 0.0
    for at in range(0, q_width, HD):
        back, gain_part = pulled(grad_q[:, at : at + HD], proj[:, at : at + HD], gains[:1, :])
        mixed[:, at : at + HD] = back
        total = total + gain_part
    grad_gains[:1, :] = total
    summed = functools.reduce(jnp.add, [g[...].astype(F32) for g in grad_kv])
    total = 0.0
    for at in range(0, kv_width, HD):
        here = slice(q_width + at, q_width + at + HD)
        back, gain_part = pulled(summed[:, at : at + HD], proj[:, here], gains[1:, :])
        mixed[:, here] = back
        total = total + gain_part
    grad_gains[1:, :] = total
    mixed[:, q_width + kv_width :] = summed[:, kv_width:].astype(LOW)
    w_qkv = get_qkv()
    for at in range(0, w_qkv.shape[0], 512):
        here = pl.ds(at, 512)
        store_columns(parts, here, dot_nt(mixed[...], w_qkv[here, :]))


def product_body(n_left, n_right, place, *refs):
    lefts, refs = refs[:n_left], refs[n_left:]
    groups = []
    for count in n_right:
        groups.append(refs[:count])
        refs = refs[count:]
    *extra, out, left_all, right_all, sems = refs
    tile, rows = out.shape[0], left_all.shape[1]
    step = pl.program_id(0)

    @pl.when(step == 0)
    def _():
        copies = []
        row = 0
        for ref in lefts:
            source = ref.at[:, pl.ds(pl.multiple_of(place[0] * rows, rows), rows)]
            copies.append((source, left_all.at[pl.ds(row, ref.shape[0]), :]))
            row += ref.shape[0]
        column = 0
        for group in groups:
            row = 0
            for ref in group:
                here = (pl.ds(row, ref.shape[0]), pl.ds(column, ref.shape[1]))
                copies.append((ref, right_all.at[here]))
                row += ref.shape[0]
            column += group[0].shape[1]
        copies = [
            pltpu.make_async_copy(source, target, sems.at[i])
            for i, (source, target) in enumerate(copies)
        ]
        for copy in copies:
            copy.start()
        for copy in copies:
            copy.wait()

    left = left_all[:, pl.ds(pl.multiple_of(step * tile, tile), tile)]
    width = 512
    for at in range(0, out.shape[1], width):
        result = dot_tn(left, right_all[:, at : at + width])
        if extra:
            result = result + extra[0][:, at : at + width].astype(F32)
        out[:, at : at + width] = result.astype(LOW)


def piece_product(pieces, which, lefts, rights, extra=None, extra_at=0):
    depth = sum(x.shape[0] for x in lefts)
    rows = lefts[0].shape[1] // pieces
    cols = sum(group[0].shape[1] for group in rights)
    tile = 256
    while rows % tile:
        tile //= 2
    steps = rows // tile
    flat = [x for group in rights for x in group]
    extras = [] if extra is None else [extra]
    place = jnp.stack([jnp.asarray(which, jnp.int32), jnp.asarray(extra_at, jnp.int32)])
    held = 2 * depth * (rows + cols)
    return pl.pallas_call(
        functools.partial(product_body, len(lefts), [len(group) for group in rights]),
        out_shape=jax.ShapeDtypeStruct((rows, cols), LOW),
        grid_spec=pltpu.PrefetchScalarGridSpec(
            num_scalar_prefetch=1,
            grid=(steps,),
            in_specs=[pl.BlockSpec(memory_space=pltpu.HBM)] * (len(lefts) + len(flat))
            + [
                pl.BlockSpec((tile, cols), lambda i, place: (place[1] * steps + i, 0))
                for _ in extras
            ],
            out_specs=pl.BlockSpec((tile, cols), lambda i, place: (i, 0)),
            scratch_shapes=[
                pltpu.VMEM((depth, rows), LOW),
                pltpu.VMEM((depth, cols), LOW),
                pltpu.SemaphoreType.DMA((len(lefts) + len(flat),)),
            ],
        ),
        compiler_params=pltpu.CompilerParams(
            vmem_limit_bytes=max(held + 8 * tile * cols + VMEM_SPARE, VMEM_LEAST)
        ),
        cost_estimate=pl.CostEstimate(
            flops=2 * depth * rows * cols,
            bytes_accessed=held + 2 * rows * cols * (1 + len(extras)),
            transcendentals=0,
        ),
    )(place, *lefts, *flat, *extras)


def assemble_body(widths, place, *refs):
    ins, outs = refs[:4], refs[4:]
    step = pl.program_id(0)
    for i in range(4):

        @pl.when((step == i % 2) & (place[0] == i // 2))
        def _(i=i):
            at = 0
            for out, width in zip(outs, widths):
                out[...] = ins[i][:, at : at + width].astype(F32)
                at += width


def assemble(place, arrays, widths):
    rows, cols = arrays[0].shape
    tile = 128
    while rows % tile:
        tile //= 2
    steps = rows // tile

    def in_map(i, step, t, place):
        wanted = place[0] == i // 2
        if i % 2 == 0:
            moving = jnp.where(step == 0, t, steps - 1)
        else:
            moving = jnp.where(step == 0, 0, t)
        return (jnp.where(wanted, moving, 0), 0)

    def out_map(step, t, place):
        return ((place[0] ^ step) * steps + t, 0)

    return pl.pallas_call(
        functools.partial(assemble_body, widths),
        out_shape=[jax.ShapeDtypeStruct((2 * rows, w), F32) for w in widths],
        grid_spec=pltpu.PrefetchScalarGridSpec(
            num_scalar_prefetch=1,
            grid=(2, steps),
            in_specs=[pl.BlockSpec((tile, cols), functools.partial(in_map, i)) for i in range(4)],
            out_specs=[pl.BlockSpec((tile, w), out_map) for w in widths],
        ),
        compiler_params=pltpu.CompilerParams(vmem_limit_bytes=24 * tile * cols + VMEM_SPARE),
        cost_estimate=pl.CostEstimate(
            flops=0, bytes_accessed=2 * rows * cols * 6, transcendentals=0
        ),
    )(place, *arrays)


Z_SLOT, Z_HOP = 5.5, 3.2


START_COST = 0.9
AHEAD = 10.0
RING, LINKS, SWAP, SPARSE, NONE = range(5)
RAW, TOP, OUTPUT, INPUT_GRAD, GAIN, GAINS, HALF, WHOLE, HOME, GATE_UP, DOWN, OUT, QKV = range(13)
CORES, CTX, MP = "section", "ctx", "mp"


class Send:
    def __init__(self, kind, blocks, span, then=0.0, slack=0.0):
        self.kind, self.blocks, self.span, self.then, self.slack = kind, blocks, span, then, slack


class Need:
    def __init__(self, *keys, then=0.0):
        self.keys, self.then = keys, then


class Wait:
    def __init__(self, until):
        self.until = until


class Lane:
    def __init__(self, work, rank, name, patience):
        self.work, self.rank, self.name, self.patience = work, rank, name, patience
        self.ready, self.value, self.wanted, self.then = 0.0, None, None, 0.0


class Driver:
    def __init__(self, token):
        self.token, self.now, self.cost = token, 0.0, 0.0
        self.lanes, self.store, self.log = [], {}, []
        self.free = [0.0] * 5

    def spend(self, cost):
        self.cost += cost

    def put(self, key, value):
        self.store[key] = (self.now + self.cost, value)

    def add(self, work, rank, name=None, patience=3.0):
        lane = Lane(work, rank, name, patience)
        lane.ready = self.now
        self.lanes.append(lane)

    def tied(self, value):
        leaves, tree = jax.tree.flatten(value)
        if not leaves:
            return value
        *leaves, _ = lax.optimization_barrier((*leaves, self.token))
        return jax.tree.unflatten(tree, leaves)

    def turn(self):
        while self.free[LINKS] > self.now + AHEAD:
            yield Wait(self.free[LINKS] - AHEAD)

    def ready_at(self, lane):
        if lane.wanted is None:
            return lane.ready
        if any(key not in self.store for key in lane.wanted):
            return None
        return max([lane.ready] + [self.store[key][0] for key in lane.wanted])

    def step(self, lane):
        self.log.append((self.now, self.ready_at(lane), lane.name))
        self.now = max(self.now, self.ready_at(lane))
        if lane.wanted is not None:
            lane.value = tuple(self.store[key][1] for key in lane.wanted)
            lane.wanted = None
        self.cost = 0.0
        value = None if lane.value is None else self.tied(lane.value)
        lane.value = None
        try:
            request = lane.work.send(value)
        except StopIteration:
            self.lanes.remove(lane)
            self.now += self.cost
            return
        self.now += self.cost
        if isinstance(request, Wait):
            lane.ready = max(self.now, request.until)
            return
        lane.then = request.then
        if isinstance(request, Need):
            lane.wanted, lane.ready = request.keys, self.now
            return
        self.now += START_COST * len(request.blocks)
        start = max(self.now, self.free[request.kind])
        self.free[request.kind] = start + request.span
        lane.ready = start + request.span + Z_HOP + request.slack
        lane.value = [move(block) for move, block in request.blocks]
        self.token = request.blocks[0][1]

    def run(self):
        while self.lanes:
            times = [(self.ready_at(lane), lane) for lane in self.lanes]
            times = [(at, lane) for at, lane in times if at is not None]
            main = [pair for pair in times if pair[1].rank == 0]
            soon = min([at for at, _ in main], default=1e9)
            waiting = [
                (at, lane)
                for at, lane in times
                if at <= self.now
                and (lane.rank == 0 or max(self.now, at) + lane.then <= soon + lane.patience)
            ]
            if waiting:
                lane = min(waiting, key=lambda pair: (pair[1].rank, pair[0]))[1]
            elif main:
                lane = min(
                    [p for p in times if p[1].rank == 0 or p[0] + p[1].then <= soon + p[1].patience],
                    key=lambda pair: (pair[0], pair[1].rank),
                )[1]
            else:
                lane = min(times, key=lambda pair: (pair[0], pair[1].rank))[1]
            self.step(lane)


def swap_cores(block):
    return lax.ppermute(block, CORES, [(0, 1), (1, 0)])


def to_core(core):
    return lambda block: lax.ppermute(block, CORES, [(1 - core, core)])


def ring_step(block):
    count = lax.axis_size(MP)
    return lax.ppermute(block, MP, [(i, (i + 1) % count) for i in range(count)])


def across_ctx(distance):
    count = lax.axis_size(CTX)
    return lambda block: lax.ppermute(block, CTX, [(i, i ^ distance) for i in range(count)])


def ring_gather(driver, block):
    blocks = [block]
    for _ in range(lax.axis_size(MP) - 1):
        (block,) = yield Send(RING, [(ring_step, block)], Z_SLOT)
        blocks.append(block)
    driver.spend(1.5)
    return lax.optimization_barrier(jnp.concatenate(blocks, axis=0))


def ring_sum(driver, part):
    count = lax.axis_size(MP)
    if not isinstance(part, list):
        rows = part.shape[0] // count
        part = [part[t * rows : (t + 1) * rows] for t in range(count)]
        driver.spend(0.8)
    running = part[1]
    for t in range(2, count):
        (got,) = yield Send(RING, [(ring_step, running)], Z_SLOT)
        running = (got.astype(F32) + part[t].astype(F32)).astype(LOW)
        driver.spend(1.4)
    (got,) = yield Send(RING, [(ring_step, running)], Z_SLOT)
    driver.spend(1.4)
    return got.astype(F32) + part[0].astype(F32)


def ctx_exchange(blocks, span=12.0):
    moves = [(across_ctx(j + 1), block) for j, block in enumerate(blocks)]
    got = yield Send(LINKS, moves, span)
    return got


def summed_everywhere(driver, block):
    for axis in (MP, CORES, CTX):
        count = lax.axis_size(axis)
        distance = 1
        while distance < count:
            route = [(i, i ^ distance) for i in range(count)]
            (got,) = yield Send(
                LINKS if axis == CTX else NONE,
                [(functools.partial(lax.ppermute, axis_name=axis, perm=route), block)],
                2.0,
                1.0,
                5.0,
            )
            block = block + got
            driver.spend(1.0)
            distance *= 2
    return block


def row_norm(rows, gain):
    scaling = lax.rsqrt(jnp.mean(rows * rows, axis=-1, keepdims=True) + EPSILON)
    return rows * scaling * gain


def row_norm_back(rows, gain, grad):
    scaling = lax.rsqrt(jnp.mean(rows * rows, axis=-1, keepdims=True) + EPSILON)
    inner = grad * gain
    back = scaling * inner - rows * (
        scaling * scaling * scaling * jnp.mean(inner * rows, axis=-1, keepdims=True)
    )
    return back, jnp.sum(grad * rows * scaling, axis=0)


def shape(rows, cols, kind=LOW):
    return jax.ShapeDtypeStruct((rows, cols), kind)


def part_shapes(rows, width):
    count = lax.axis_size(MP)
    return [shape(rows // count, width)] * count


def project(attn_in, layer, weights, gains, tables):
    turns, q_pos, k_pos = tables
    rows, width = attn_in.shape
    total = weights.qkv[0].shape[1]
    q_width = weights.output[0].shape[0]
    kv_width = (total - q_width) // 2
    return kernel_call(
        functools.partial(qkv_forward_body, q_width),
        [shape(rows, q_width + kv_width, F32), shape(rows, q_width), shape(rows, 2 * kv_width)],
        2 * rows * width * total,
        (attn_in, gains.heads, turns),
        layer,
        [weights.qkv],
    )


def attend(queries, blocks, layer, weights, tables):
    turns, q_pos, k_pos = tables
    rows, q_width = queries.shape
    width = weights.output[0].shape[1]
    attended, log_total, *parts = kernel_call(
        functools.partial(attend_body, len(blocks)),
        [shape(rows, q_width), shape(rows, q_width // HD, F32)] + part_shapes(rows, width),
        2 * rows * q_width * (2 * rows * len(blocks) + width),
        (queries, *blocks, q_pos, k_pos),
        layer,
        [weights.output],
    )
    return parts, attended, log_total


def mlp_forward(mlp_in, layer, weights):
    ff = weights.gate[0].shape[1]
    picked = [weights.gate, weights.up, weights.down]
    rows, width = mlp_in.shape
    gate, up, hidden, *parts = kernel_call(
        mlp_forward_body,
        [shape(rows, ff)] * 3 + part_shapes(rows, width),
        6 * rows * width * ff,
        (mlp_in,),
        layer,
        picked,
    )
    return gate, up, hidden, parts


def mlp_back(branch, kept, layer, weights):
    ff = weights.gate[0].shape[1]
    picked = [weights.down, weights.gate, weights.up]
    rows, width = branch.shape
    grad_gate, grad_up, *parts = kernel_call(
        mlp_back_body,
        [shape(rows, ff)] * 2 + part_shapes(rows, width),
        6 * rows * width * ff,
        (branch, kept.gate, kept.up),
        layer,
        picked,
    )
    return grad_gate, grad_up, parts


def attend_back(grad_rows, kept, layer, weights, tables):
    turns, q_pos, k_pos = tables
    blocks = kept.blocks
    rows, q_width = kept.queries.shape
    return kernel_call(
        functools.partial(attend_back_body, len(blocks)),
        [shape(rows, q_width, F32)] + [shape(*blocks[0].shape)] * len(blocks),
        2 * rows * q_width * (5 * rows * len(blocks) + grad_rows.shape[1]),
        (
            grad_rows,
            kept.queries,
            *blocks,
            q_pos,
            k_pos,
            kept.attended,
            kept.log_total,
        ),
        layer,
        [weights.output],
    )


def project_back(grad_q, grad_kv, kept, layer, weights, gains, tables):
    turns, q_pos, k_pos = tables
    rows, width = kept.attn_in.shape
    total = weights.qkv[0].shape[1]
    mixed, grad_gains, *parts = kernel_call(
        functools.partial(qkv_back_body, len(grad_kv)),
        [shape(rows, total), shape(2, HD, F32)] + part_shapes(rows, width),
        2 * rows * width * total,
        (grad_q, *grad_kv, kept.proj, gains.heads, turns),
        layer,
        [weights.qkv],
    )
    return mixed, parts, grad_gains


def sequence_lane(driver, seq, weights, gains, tables, own_rows, in_ring_order):
    (raw,) = yield Need(RAW)
    rows = in_ring_order(raw, seq)
    h_rows = rows[:own_rows].astype(F32)
    kept = []
    for layer in range(2):
        gain = gains[layer]
        if layer == 0:
            attn_in = row_norm(rows.astype(F32), gain.attn).astype(LOW)
            driver.spend(4.0)
        else:
            attn_in = yield from ring_gather(driver, row_norm(h_rows, gain.attn).astype(LOW))
        proj, queries, kv = project(attn_in, layer, weights, gain, tables)
        driver.spend(6.0)
        others = yield from ctx_exchange([kv] * (lax.axis_size(CTX) - 1))
        blocks = [kv] + others
        part, attended, log_total = attend(queries, blocks, layer, weights, tables)
        driver.spend(6.0)
        mid = h_rows + (yield from ring_sum(driver, part))
        driver.spend(1.0)
        mlp_in = yield from ring_gather(driver, row_norm(mid, gain.mlp).astype(LOW))
        gate, up, hidden, part = mlp_forward(mlp_in, layer, weights)
        driver.spend(9.5)
        kept.append(
            SimpleNamespace(
                attn_in=attn_in,
                h_rows=h_rows,
                proj=proj,
                queries=queries,
                blocks=blocks,
                attended=attended,
                log_total=log_total,
                mid=mid,
                mlp_in=mlp_in,
                gate=gate,
                up=up,
                hidden=hidden,
            )
        )
        h_rows = mid + (yield from ring_sum(driver, part))
        driver.spend(1.0)
        driver.put((OUTPUT, layer, seq), h_rows)

    (top_grad,) = yield Need(TOP)
    branch = in_ring_order(top_grad, seq)
    driver.spend(2.0)
    grad_out = branch[:own_rows].astype(F32)
    for layer in (1, 0):
        gain, state = gains[layer], kept[layer]
        if layer == 0:
            branch = yield from ring_gather(driver, grad_out.astype(LOW))
        driver.put((DOWN, layer, seq), (state.hidden, branch))
        grad_gate, grad_up, part = mlp_back(branch, state, layer, weights)
        driver.spend(12.0)
        driver.put((GATE_UP, layer, seq), (state.mlp_in, grad_gate, grad_up))
        back, mlp_gain = row_norm_back(
            state.mid, gain.mlp, (yield from ring_sum(driver, part))
        )
        driver.spend(4.0)
        grad_mid = grad_out + back
        grad_rows = yield from ring_gather(driver, grad_mid.astype(LOW))
        driver.put((OUT, layer, seq), (state.attended, grad_rows))
        grad_q, *grad_kv = attend_back(grad_rows, state, layer, weights, tables)
        driver.spend(10.0)
        grad_kv = [grad_kv[0]] + (yield from ctx_exchange(grad_kv[1:], 17.0))
        mixed, part, head_gains = project_back(
            grad_q, grad_kv, state, layer, weights, gain, tables
        )
        driver.spend(9.0)
        driver.put((QKV, layer, seq), (state.attn_in, mixed))
        back, attn_gain = row_norm_back(
            state.h_rows, gain.attn, (yield from ring_sum(driver, part))
        )
        driver.spend(4.0)
        grad_out = grad_mid + back
        driver.put((INPUT_GRAD, layer, seq), grad_out)
        driver.put(
            (GAIN, layer, seq), jnp.concatenate([attn_gain, mlp_gain, head_gains.reshape(-1)])
        )


def core_bit(t, bits):
    shift = jnp.where(lax.axis_index(CORES) == 0, t, bits - 1 - t)
    return (lax.axis_index(CTX) >> shift) & 1


def joint_step(t, bits):
    count = 1 << bits
    route = []
    for core in range(2):
        distance = 1 << (t if core == 0 else bits - 1 - t)
        route += [(core * count + i, core * count + (i ^ distance)) for i in range(count)]
    return lambda block: lax.ppermute(block, (CORES, CTX), route)


def sum_by_halving(driver, product, rows, cost, slack):
    core = lax.axis_index(CORES)
    bits = lax.axis_size(CTX).bit_length() - 1
    flag = core_bit(0, bits)
    sent = None
    if rows % (4 * LANES) == 0:
        sent = product(4, 2 * core + 1 - flag, 1 - flag)
        total = product(4, 2 * core + flag, flag)
    else:
        total = product(2, core, 0)
    driver.spend(cost * 1.4)
    for t in range(bits):
        if sent is None:
            flag, count = core_bit(t, bits), total.shape[0] // 2
            sent = lax.dynamic_slice_in_dim(total, (1 - flag) * count, count, axis=0)
            total = lax.dynamic_slice_in_dim(total, flag * count, count, axis=0)
            driver.spend(1.5 + sent.size * 2 / 1e6)
        size = sent.size * 2 / 1e6
        (got,) = yield Send(
            LINKS, [(joint_step(t, bits), sent)], 11.5 * size, 1.5 + size, slack + 6.0 * size
        )
        driver.spend(1.0 + size)
        total = (total.astype(F32) + got.astype(F32)).astype(LOW)
        sent = None
    for t in reversed(range(bits)):
        size = total.size * 2 / 1e6
        (got,) = yield Send(
            LINKS, [(joint_step(t, bits), total)], 11.5 * size, 1.5 + 2 * size, slack + 6.0 * size
        )
        flag = core_bit(t, bits) == 0
        total = jnp.concatenate(
            [jnp.where(flag, total, got), jnp.where(flag, got, total)], axis=0
        )
        driver.spend(1.5 + 2 * size)
    return total


def scattered(driver, product, cost, crowding):
    total = product(2, lax.axis_index(CORES), 0)
    driver.spend(cost * 1.2)
    move = functools.partial(lax.psum_scatter, axis_name=CTX, scatter_dimension=0, tiled=True)
    span = (13 + 2e-5 * total.size) * crowding
    (share,) = yield Send(SPARSE, [(move, total)], span, 1.0)
    return share, span


def sum_by_collectives(driver, product, rows, cost, slack):
    share, span = yield from scattered(driver, product, cost, 1.0)
    move = functools.partial(lax.all_gather, axis_name=CTX, axis=0, tiled=True)
    (total,) = yield Send(SPARSE, [(move, share)], span, 1.0)
    return total


def sum_by_both(driver, product, rows, cost, slack):
    if lax.axis_size(CTX) != 4:
        return (yield from sum_by_collectives(driver, product, rows, cost, slack))
    share, _ = yield from scattered(driver, product, cost, 1.35)
    first = lax.axis_index(CORES) == 0
    size = share.size * 2 / 1e6
    (got,) = yield Send(
        LINKS, [(joint_step(0, 2), share)], 11.5 * size, 1.5 + 2 * size, slack + 3.0 * size
    )
    flag = core_bit(0, 2) == 0
    pair = jnp.stack([jnp.where(flag, share, got), jnp.where(flag, got, share)])
    driver.spend(1.5 + 2 * size)
    (got,) = yield Send(
        LINKS, [(joint_step(1, 2), pair)], 23.0 * size, 2.0 + 4 * size, slack + 6.0 * size
    )
    flag = core_bit(1, 2) == 0
    low, high = jnp.where(flag, pair, got), jnp.where(flag, got, pair)
    driver.spend(2.0 + 4 * size)
    return jnp.concatenate(
        [
            low[0],
            jnp.where(first, low[1], high[0]),
            jnp.where(first, high[0], low[1]),
            high[1],
        ],
        axis=0,
    )


def matrix_lane(driver, name, layer, cost, way):
    parts = yield Need(*[(name, layer, seq) for seq in range(SEQS)], then=cost)
    lefts = [part[0] for part in parts]
    rights = [[part[at] for part in parts] for at in range(1, len(parts[0]))]
    driver.spend(cost)
    away = piece_product(2, 1 - lax.axis_index(CORES), lefts, rights)
    size = away.size * 2 / 1e6
    (received,) = yield Send(SWAP, [(swap_cores, away)], 2.0 + 1.6 * size, cost * 1.3, 4.0)

    def product(pieces, which, extra_at):
        return piece_product(pieces, which, lefts, rights, received, extra_at)

    slack = 4.0 if layer == 0 else 25.0
    half = yield from way(driver, product, lefts[0].shape[1], cost, slack)
    (other,) = yield Send(SWAP, [(to_core(layer), half)], 2.0 + 1.6 * size, 0.0, 4.0)
    driver.token = other
    driver.put((HALF, name, layer), (half, other))


def assemble_lane(driver, name, widths):
    first, second = yield Need((HALF, name, 0), (HALF, name, 1))
    core = lax.axis_index(CORES).astype(jnp.int32).reshape(1)
    whole = assemble(core, [*first, *second], widths)
    driver.token = whole[0]
    driver.put((WHOLE, name), whole)
    driver.spend(1.5 + 1.3e-6 * first[0].size * 4)


def home_lane(driver, name, after=()):
    if after:
        yield Need(*after)
    pairs = yield Need(*[(name, layer, seq) for seq in range(SEQS) for layer in range(2)])
    pairs = [pairs[2 * seq : 2 * seq + 2] for seq in range(SEQS)]
    core, place = lax.axis_index(CORES), lax.axis_index(MP)
    count = lax.axis_size(MP)
    even, half = place % 2 == 0, count // 2
    first_route = [(m, m // 2 if m % 2 == 0 else half + m // 2) for m in range(count)]
    second_route = [(m, half + m // 2 if m % 2 == 0 else m // 2) for m in range(count)]

    def within(route):
        return lambda block: lax.ppermute(block, MP, route)

    def across(route):
        pairs = [(k * count + a, (1 - k) * count + b) for k in range(2) for a, b in route]
        return lambda block: lax.ppermute(block, (CORES, MP), pairs)

    keep = [jnp.where(core == 0, a, b).astype(LOW) for a, b in pairs]
    send = [jnp.where(core == 0, b, a).astype(LOW) for a, b in pairs]
    moves = []
    for kind, rows in ((within, keep), (across, send)):
        moves.append((kind(first_route), jnp.where(even, rows[0], rows[1])))
        moves.append((kind(second_route), jnp.where(even, rows[1], rows[0])))
    driver.spend(4.0)
    got = yield Send(RING, moves, 4 * Z_SLOT, 2.0, 4.0)
    driver.token = got[-1]
    lower = place < half
    kept, other = [
        jnp.concatenate([jnp.where(lower, one, two), jnp.where(lower, two, one)], axis=0)
        for one, two in (got[:2], got[2:])
    ]
    whole = jnp.stack([jnp.where(core == 0, kept, other), jnp.where(core == 0, other, kept)])
    driver.put((HOME, name), whole.astype(F32))
    driver.spend(4.0)


def gain_lane(driver):
    got = yield Need(*[(GAIN, layer, seq) for layer in range(2) for seq in range(SEQS)])
    sums = jnp.stack([got[2 * layer] + got[2 * layer + 1] for layer in range(2)])
    driver.spend(2.0)
    driver.put(GAINS, (yield from summed_everywhere(driver, sums)))


def gather_lane(driver, name, block, after, beside=()):
    if after:
        yield Need(*after)
    (whole,) = yield Send(
        SPARSE, [(lambda x: lax.all_gather(x, MP, axis=0, tiled=True), block)], 46.0
    )
    if beside:
        whole, *_ = lax.optimization_barrier((whole, *beside))
    driver.token = whole
    driver.put(name, whole)


LOGS = []
MATRICES = ((GATE_UP, 9.5), (DOWN, 5.5), (OUT, 3.5), (QKV, 5.0))
WAYS = (
    {GATE_UP: sum_by_both, DOWN: sum_by_both, OUT: sum_by_halving, QKV: sum_by_halving},
    {
        GATE_UP: sum_by_collectives,
        DOWN: sum_by_collectives,
        OUT: sum_by_halving,
        QKV: sum_by_halving,
    },
)
URGENT = 12.0


def shards(
    section_input,
    cotangent,
    pair_owner,
    attn_gain,
    w_query,
    w_key,
    w_value,
    query_gain,
    key_gain,
    w_output,
    mlp_gain,
    w_gate,
    w_up,
    w_down,
):
    n_ctx, n_mp = lax.axis_size(CTX), lax.axis_size(MP)
    core, ctx, place = lax.axis_index(CORES), lax.axis_index(CTX), lax.axis_index(MP)
    is_first = core == 0
    width = section_input.shape[2]
    seq_rows = section_input.shape[1] * n_mp // SEQS
    own_rows = seq_rows // n_mp

    raw_own = lax.dynamic_index_in_dim(section_input, core, 0, keepdims=False)
    top_own = lax.dynamic_index_in_dim(cotangent, core, 0, keepdims=False).astype(LOW)
    ring_order = (place - jnp.arange(n_mp, dtype=jnp.int32)) % n_mp

    def in_ring_order(rows, seq):
        return jnp.concatenate(
            [
                lax.dynamic_slice_in_dim(
                    rows, seq * seq_rows + ring_order[t] * own_rows, own_rows, axis=0
                )
                for t in range(n_mp)
            ],
            axis=0,
        )

    w_qkv = jnp.concatenate([w_query[0], w_key[0], w_value[0]], axis=1)
    own = [w_qkv] + [w[0] for w in (w_output, w_gate, w_up, w_down)]
    other = [swap_cores(w) for w in own]
    own_gains = jnp.concatenate([attn_gain[0], mlp_gain[0], query_gain[0], key_gain[0]])
    other_gains = swap_cores(own_gains)
    gains = []
    for layer in range(2):
        mine = is_first if layer == 0 else ~is_first
        flat = jnp.where(mine, own_gains, other_gains).astype(F32)
        gains.append(
            SimpleNamespace(
                attn=flat[:width],
                mlp=flat[width : 2 * width],
                heads=flat[2 * width :].reshape(2, HD),
            )
        )

    owners = lax.dynamic_index_in_dim(pair_owner, core, 0, keepdims=False)
    index = (ring_order[:, None] * own_rows + jnp.arange(own_rows, dtype=jnp.int32)).reshape(-1)
    inv_freq = ROPE_BASE ** (-jnp.arange(0, HD, 2).astype(F32) / HD)
    seq_tables = []
    for seq in range(SEQS):
        block = jnp.take(owners[seq], ctx ^ jnp.arange(n_ctx, dtype=jnp.int32))[:, None]
        k_pos = jnp.where(
            index < STRETCH,
            block * STRETCH + index,
            (2 * n_ctx - 1 - block) * STRETCH + index - STRETCH,
        )
        q_pos = k_pos[0][:, None]
        angles = q_pos.astype(F32) * inv_freq[None, :]
        cosine, sine = jnp.cos(angles), jnp.sin(angles)
        seq_tables.append(
            (
                jnp.concatenate([cosine, cosine, -sine, sine], axis=1),
                q_pos,
                k_pos,
            )
        )

    q_width, kv_width, ff = w_query.shape[2], w_key.shape[2], w_gate.shape[2]
    widths = {
        QKV: (q_width, kv_width, kv_width),
        OUT: (width,),
        GATE_UP: (ff, ff),
        DOWN: (width,),
    }
    qkv, output, gate, up, down = zip(own, other)
    weights = SimpleNamespace(qkv=qkv, output=output, gate=gate, up=up, down=down)
    driver = Driver(raw_own)
    driver.add(gather_lane(driver, RAW, raw_own, (), other), 0)
    for seq in range(SEQS):
        driver.add(
            sequence_lane(
                driver, seq, weights, gains, seq_tables[seq], own_rows, in_ring_order
            ),
            0,
            seq,
        )
    driver.add(gather_lane(driver, TOP, top_own, (RAW,)), 1)
    for layer in (1, 0):
        for name, cost in MATRICES:
            way = WAYS[layer][name]
            urgent = layer == 0
            lane = matrix_lane(driver, name, layer, cost, way)
            driver.add(lane, 1 if urgent else 3, (name, layer), URGENT if urgent else 3.0)
    for name, _ in MATRICES:
        driver.add(assemble_lane(driver, name, widths[name]), 2)
    driver.add(home_lane(driver, INPUT_GRAD), 1)
    driver.add(home_lane(driver, OUTPUT, ((HOME, INPUT_GRAD),)), 4)
    driver.add(gain_lane(driver), 2)
    driver.run()
    LOGS.append(driver.log)

    def made(key):
        return driver.store[key][1]

    flat = lax.dynamic_index_in_dim(made(GAINS), core, 0, keepdims=False)
    g_query, g_key, g_value = [x[None] for x in made((WHOLE, QKV))]
    g_gate, g_up = [x[None] for x in made((WHOLE, GATE_UP))]
    g_output, g_down = [made((WHOLE, x))[0][None] for x in (OUT, DOWN)]
    return (
        made((HOME, OUTPUT))[None],
        made((HOME, INPUT_GRAD))[None],
        flat[:width][None],
        g_query,
        g_key,
        g_value,
        flat[2 * width : 2 * width + HD][None],
        flat[2 * width + HD :][None],
        g_output,
        flat[width : 2 * width][None],
        g_gate,
        g_up,
        g_down,
    )


def solution(mesh):
    in_specs = (
        P(None, (CTX, MP), None),
        P(None, (CTX, MP), None),
        P(),
        P(CORES, None),
        P(CORES, None, MP),
        P(CORES, None, MP),
        P(CORES, None, MP),
        P(CORES, None),
        P(CORES, None),
        P(CORES, MP, None),
        P(CORES, None),
        P(CORES, None, MP),
        P(CORES, None, MP),
        P(CORES, MP, None),
    )
    out_specs = (
        P(CORES, None, (CTX, MP), None),
        P(CORES, None, (CTX, MP), None),
        P(CORES, None),
        P(CORES, None, MP),
        P(CORES, None, MP),
        P(CORES, None, MP),
        P(CORES, None),
        P(CORES, None),
        P(CORES, MP, None),
        P(CORES, None),
        P(CORES, None, MP),
        P(CORES, None, MP),
        P(CORES, MP, None),
    )
    return jax.shard_map(shards, mesh=mesh, in_specs=in_specs, out_specs=out_specs, check_vma=False)
```

time: 1430 us -> 1080 us (0.76)
  waiting for transfers between devices: 692 us -> 485 us
  matrix products: 184 us -> 0 us
  Pallas kernels: 151 us -> 284 us
  blocking collectives: 68.1 us -> 0 us
  starting transfers between devices: 152 us -> 122 us
  other arithmetic: 95.8 us -> 111 us
    ppermute x204 -> x163, waiting for transfers between devices: 646 us -> 450 us  [the longest x84 323 us: ring_step(): return lax.ppermute(block, MP, [(i, (i + 1) % count) for i in range(count)])]
    dot_general x48 -> x0, matrix products: 184 us -> none  [the longest x24 111 us: dot_tn(): lax.dot_general(left, right, (((0,), (0,)), ((), ())), preferred_element_...]
    pallas_call x20 -> x48, Pallas kernels: 151 us -> 284 us  [the longest x24 155 us: kernel_call(): pl.pallas_call(whole, out_shape=out_shape, in_specs=[hbm] * (n_args + 2 *...]
    psum x1 -> x0, blocking collectives: 68.1 us -> none  [shards(): all_gains = lax.psum(jnp.stack(gain_sums), ('section', 'ctx', 'mp'))]
    select_n x12 -> x18, other arithmetic: 43 us -> 10.4 us  [the longest x8 6.22 us: sum_by_halving(): jnp.where(flag, total, got)]
    ppermute x204 -> x163, starting transfers between devices: 152 us -> 121 us  [the longest x24 30.6 us: across_ctx(): lax.ppermute(block, CTX, [(i, i ^ distance) for i in range(count)])]
    convert_element_type x45 -> x56, other arithmetic: 21.4 us -> 44.6 us  [the longest x32 17.1 us: ring_sum(): running = (got.astype(F32) + part[t].astype(F32)).astype(LOW)]
    concatenate x16 -> x35, other arithmetic: 8.9 us -> 32 us  [the longest x12 19.2 us: ring_gather(): return lax.optimization_barrier(jnp.concatenate(blocks, axis=0))]
  transfers between devices with their start and end apart: 206 -> 171, of which waited for: 95 -> 87; matrix products, arithmetic and copies ran while one was open for 21% -> 11% of each run, Pallas kernels for 8% -> 24%
where the time goes in v2:
time: 1080 us; the launch traced here: 1070 us
  waiting for transfers between devices  485 us (45%)
  Pallas kernels  284 us (26%)
  starting transfers between devices  122 us (11%)
  other arithmetic  111 us (10%)
  local copies, waits for them, and re-layouts  48.8 us (5%)
  between operations  22.3 us (2%)
    ppermute x84, waiting for transfers between devices, ring_step(): return lax.ppermute(block, MP, [(i, (i + 1) % count) for i in range(count)])  323 us
    pallas_call x24, Pallas kernels, kernel_call(): pl.pallas_call(whole, out_shape=out_shape, in_specs=[hbm] * (n_args + 2 *...  155 us
    pallas_call x20, Pallas kernels, piece_product(): pl.pallas_call(functools.partial(product_body, len(lefts), [len(group) fo...  90.8 us
    ppermute x20, waiting for transfers between devices, joint_step(): return lambda block: lax.ppermute(block, (CORES, CTX), route)  61.7 us
    ppermute x24, waiting for transfers between devices, across_ctx(): lax.ppermute(block, CTX, [(i, i ^ distance) for i in range(count)])  57.8 us
    pallas_call x4, Pallas kernels, assemble(): pl.pallas_call(functools.partial(assemble_body, widths), out_shape=[jax.S...  38 us
    unnamed x712, local copies, waits for them, and re-layouts  37.9 us
    all_gather x2, waiting for transfers between devices, gather_lane(): lax.all_gather(x, MP, axis=0, tiled=True)  35.7 us
  transfers between devices with their start and end apart: 171, of which 87 were waited for; matrix products, arithmetic and copies ran while one was open for 11% of the time, Pallas kernels for 24%

profile of v2, /device:TPU:0, one launch (start us, length us, event | category | flops | bytes accessed | tf_op | source)
XLA Modules:
  0.0 1073.2 jit_solution(13287138867137385545)
XLA Ops:
  23.0 35.7 %all-gather.11.cloned.1.call-done = bf16[1,512,2048]{2,1,0:T(8,128)(2,1)} async-done(((bf16[1,128,2048]{2,1,0:T(8,128)(2,1)}), bf16[1,512,2048]{2,1,0:T(8,128)(2,1)}) %all-gather.11.cloned.1.call-update) | async-done | bytes 2097168 | tf_op jit(solution)/shard_map/all_gather | solution.py:943
  97.0 10.1 collective-permute-done.9
  109.4 8.7 collective-permute-done.14
  118.3 5.6 collective-permute-done.13
  146.6 5.6 collective-permute-done.20
  157.9 5.6 collective-permute-done.22
  170.1 8.6 shard_map.241
  182.6 8.6 shard_map.242
  192.2 10.1 collective-permute-done.26
  282.5 5.9 collective-permute-done.39
  323.0 5.7 collective-permute-done.50
  345.6 8.6 shard_map.247
  357.3 8.6 shard_map.248
  368.1 8.1 collective-permute-done.56
  386.7 10.5 shard_map.249
  398.8 10.6 shard_map.250
  414.2 7.2 shard_map.252
  430.8 6.1 shard_map.253
  437.4 10.9 %collective-permute-done.64 = bf16[64,2048]{1,0:T(8,128)(2,1)S(1)} collective-permute-done((bf16[64,2048]{1,0:T(8,128)(2,1)}, bf16[64,2048]{1,0:T(8,128)(2,1)S(1)}, u32[]{:S(2)}, u32[]{:S(2)}) %collective-permute-start.64) | collective-permute-done | bytes 262176 | tf_op jit(solution)/shard_map/ppermute | solution.py:511
  461.8 10.1 shard_map.254
  472.2 11.2 %collective-permute-done.66 = bf16[64,2048]{1,0:T(8,128)(2,1)S(1)} collective-permute-done((bf16[64,2048]{1,0:T(8,128)(2,1)}, bf16[64,2048]{1,0:T(8,128)(2,1)S(1)}, u32[]{:S(2)}, u32[]{:S(2)}) %collective-permute-start.66) | collective-permute-done | bytes 262176 | tf_op jit(solution)/shard_map/ppermute | solution.py:511
  494.7 6.1 collective-permute-done.72
  508.6 7.0 shard_map.255
  518.1 7.9 shard_map.256
  533.5 8.8 collective-permute-done.73.refs_2_
  627.1 6.0 collective-permute-done.89
  638.6 5.7 collective-permute-done.93
  652.0 11.6 %shard_map.265 = (bf16[256,1536]{1,0:T(8,128)(2,1)S(1)}, bf16[256,1536]{1,0:T(8,128)(2,1)S(1)}, bf16[64,2048]{1,0:T(8,128)(2,1)S(1)}, bf16[64,2048]{1,0:T(8,128)...) custom-call(bf16[256,2048]{1,0:T(8,128)(2,1)} %pad_maximum_fusion.19.refs_0_.refs_2_, ...), custom_call_target="tpu_custom_call" | custom-call | flops 4831838208 | bytes 24117248 | tf_op jit(solution)/shard_map/pallas_call | solution.py:71
  666.4 11.3 %shard_map.266 = (bf16[256,1536]{1,0:T(8,128)(2,1)S(1)}, bf16[256,1536]{1,0:T(8,128)(2,1)S(1)}, bf16[64,2048]{1,0:T(8,128)(2,1)S(1)}, bf16[64,2048]{1,0:T(8,128)...) custom-call(bf16[256,2048]{1,0:T(8,128)(2,1)} %pad_maximum_fusion.20.refs_0_.refs_3_, ...), custom_call_target="tpu_custom_call" | custom-call | flops 4831838208 | bytes 24117248 | tf_op jit(solution)/shard_map/pallas_call | solution.py:71
  682.9 7.2 shard_map.268
  705.0 6.1 collective-permute-done.101
  712.4 6.1 shard_map.269
  735.3 9.9 shard_map.270
  757.2 6.7 collective-permute-done.107
  779.2 6.8 shard_map.271
  788.4 7.0 shard_map.272
  807.8 8.8 collective-permute-done.113.refs_2_
  819.2 19.2 %collective-permute-done.115.refs_4_ = bf16[256,512]{1,0:T(8,128)(2,1)S(1)} collective-permute-done((bf16[256,512]{1,0:T(8,128)(2,1)S(1)}, bf16[256,512]{1,0:T(8,128)(2,1)S(1)}, u32[]{:S(2)}, u32[]{:S(2)}) %collective-permute-start.115) | collective-permute-done | bytes 262176 | tf_op jit(solution)/shard_map/ppermute | solution.py:516
  868.9 6.1 collective-permute-done.110
  889.8 13.0 %collective-permute-done.134 = bf16[2,192,2048]{2,1,0:T(8,128)(2,1)S(1)} collective-permute-done((bf16[2,192,2048]{2,1,0:T(8,128)(2,1)S(1)}, bf16[2,192,2048]{2,1,0:T(8,128)(2,1)S(1)}, u32[]{:S(2)}, u32[]{:S(2)}) %collective-permute-start.134) | collective-permute-done | bytes 1572896 | tf_op jit(solution)/shard_map/ppermute | solution.py:782
  926.7 10.2 shard_map.281
  953.2 16.6 %collective-permute-done.143 = bf16[256,3072]{1,0:T(8,128)(2,1)S(1)} collective-permute-done((bf16[256,3072]{1,0:T(8,128)(2,1)S(1)}, bf16[256,3072]{1,0:T(8,128)(2,1)S(1)}, u32[]{:S(2)}, u32[]{:S(2)}) %collective-permute-start.143) | collective-permute-done | bytes 1572896 | tf_op jit(solution)/shard_map/ppermute | solution.py:782
  972.3 12.4 %collective-permute-done.153 = bf16[128,2048]{1,0:T(8,128)(2,1)S(1)} collective-permute-done((bf16[128,2048]{1,0:T(8,128)(2,1)S(1)}, bf16[128,2048]{1,0:T(8,128)(2,1)S(1)}, u32[]{:S(2)}, u32[]{:S(2)}) %collective-permute-start.153) | collective-permute-done | bytes 524320 | tf_op jit(solution)/shard_map/ppermute | solution.py:782
  990.9 6.0 collective-permute-start.150
  996.9 10.2 collective-permute-start.152
  1023.6 11.9 %collective-permute-done.160 = bf16[512,1024]{1,0:T(8,128)(2,1)S(1)} collective-permute-done((bf16[512,1024]{1,0:T(8,128)(2,1)S(1)}, bf16[512,1024]{1,0:T(8,128)(2,1)S(1)}, u32[]{:S(2)}, u32[]{:S(2)}) %collective-permute-start.160) | collective-permute-done | bytes 1048608 | tf_op jit(solution)/shard_map/ppermute | solution.py:782
  1040.8 18.4 %shard_map.283 = (f32[2048,1536]{1,0:T(8,128)}, f32[2048,1536]{1,0:T(8,128)}) custom-call(s32[1]{0:T(128)} %bitcast.26.place, bf16[1024,3072]{1,0:T(8,128)(2,1)} %pad_maximum_fusion.refs_0_, bf16[1024,3072]{1,0:T(8,128)(2,1)} %collective-permute-done.162.refs_1_, bf16[1024,3072]{1,0:T(8,128)(2,1)S(1)} %bitcast.95, ...), custom_call_target="tpu_custom_call" | custom-call | bytes 37748736 | tf_op jit(solution)/shard_map/pallas_call | solution.py:365
  1059.2 6.9 shard_map.284
  (1268 shorter events, 595.0 us)
Async XLA Ops:
  7.2 51.5 %all-gather.11.cloned.1.call-start = ((), (), s32[]{:S(2)}) async-start(), calls=%async_computation.10 | async-start | bytes 2621440 | tf_op jit(solution)/shard_map/all_gather | solution.py:943
  9.4 126.3 %all-gather.13.cloned.1.call-start = ((), (), s32[]{:S(2)}) async-start(), calls=%async_computation.11 | async-start | bytes 2621440 | tf_op jit(solution)/shard_map/all_gather | solution.py:943
  9.4 49.4 %collective-permute-start.2 = (bf16[2048,1536]{1,0:T(8,128)(2,1)}, bf16[2048,1536]{1,0:T(8,128)(2,1)}, u32[]{:S(2)}, u32[]{:S(2)}) collective-permute-start(bf16[2048,1536]{1,0:T(8,128)(2,1)} %bitcast.100), channel_id=1, source_target_pairs={{0,16},{16,0},{1,17},{17,1},{2,18},{18,2},{3,19},{19,3},{4,20},{20... | collective-permute-start | bytes 18874376 | tf_op jit(solution)/shard_map/ppermute | solution.py:502
  9.9 48.8 %collective-permute-start.3 = (bf16[2048,1536]{1,0:T(8,128)(2,1)}, bf16[2048,1536]{1,0:T(8,128)(2,1)}, u32[]{:S(2)}, u32[]{:S(2)}) collective-permute-start(bf16[2048,1536]{1,0:T(8,128)(2,1)} %bitcast.109), channel_id=1, source_target_pairs={{0,16},{16,0},{1,17},{17,1},{2,18},{18,2},{3,19},{19,3},{4,20},{20... | collective-permute-start | bytes 18874376 | tf_op jit(solution)/shard_map/ppermute | solution.py:502
  10.0 48.8 %collective-permute-start.4 = (bf16[1536,2048]{1,0:T(8,128)(2,1)}, bf16[1536,2048]{1,0:T(8,128)(2,1)}, u32[]{:S(2)}, u32[]{:S(2)}) collective-permute-start(bf16[1536,2048]{1,0:T(8,128)(2,1)} %bitcast.118), channel_id=1, source_target_pairs={{0,16},{16,0},{1,17},{17,1},{2,18},{18,2},{3,19},{19,3},{4,20},{20... | collective-permute-start | bytes 18874376 | tf_op jit(solution)/shard_map/ppermute | solution.py:502
  14.2 44.6 %collective-permute-start = (bf16[2048,1024]{1,0:T(8,128)(2,1)}, bf16[2048,1024]{1,0:T(8,128)(2,1)}, u32[]{:S(2)}, u32[]{:S(2)}) collective-permute-start(bf16[2048,1024]{1,0:T(8,128)(2,1)} %pad_maximum_fusion.1.refs_3_.refs_8_), channel_id=1, source_target_pairs={{0,16},{16,0},{1,17},{17,1},{2,18},{18,2},{3,19},{19,3},{4,20},{20... | collective-permute-start | bytes 12582920 | tf_op jit(solution)/shard_map/ppermute | solution.py:502
  15.8 485.0 %reduce-scatter.5.cloned.1.call-start = ((), (), s32[]{:S(2)}) async-start(), calls=%async_computation.4 | async-start | bytes 3932160 | tf_op jit(solution)/shard_map/reduce_scatter | solution.py:474
  20.6 38.2 %collective-permute-start.1 = (bf16[512,2048]{1,0:T(8,128)(2,1)}, bf16[512,2048]{1,0:T(8,128)(2,1)}, u32[]{:S(2)}, u32[]{:S(2)}) collective-permute-start(bf16[512,2048]{1,0:T(8,128)(2,1)} %bitcast.127), channel_id=1, source_target_pairs={{0,16},{16,0},{1,17},{17,1},{2,18},{18,2},{3,19},{19,3},{4,20},{20... | collective-permute-start | bytes 6291464 | tf_op jit(solution)/shard_map/ppermute | solution.py:502
  421.4 40.4 %collective-permute-start.67 = (bf16[1024,3072]{1,0:T(8,128)(2,1)}, bf16[1024,3072]{1,0:T(8,128)(2,1)}, u32[]{:S(2)}, u32[]{:S(2)}) collective-permute-start(bf16[1024,3072]{1,0:T(8,128)(2,1)} %shard_map.252), channel_id=1, source_target_pairs={{0,16},{16,0},{1,17},{17,1},{2,18},{18,2},{3,19},{19,3},{4,20},{20... | collective-permute-start | bytes 18874376 | tf_op jit(solution)/shard_map/ppermute | solution.py:502
  437.0 159.5 %reduce-scatter.7.cloned.1.call-start = ((), (), s32[]{:S(2)}) async-start(), calls=%async_computation.5 | async-start | bytes 7864320 | tf_op jit(solution)/shard_map/reduce_scatter | solution.py:474
  472.0 161.1 %all-gather.7.cloned.1.call-start = ((), (), s32[]{:S(2)}) async-start(), calls=%async_computation.6 | async-start | bytes 3932160 | tf_op jit(solution)/shard_map/all_gather | solution.py:474
  505.9 241.9 %all-gather.9.cloned.1.call-start = ((), (), s32[]{:S(2)}) async-start(), calls=%async_computation.7 | async-start | bytes 7864320 | tf_op jit(solution)/shard_map/all_gather | solution.py:474
  529.1 33.8 %collective-permute-start.80 = (bf16[256,2048]{1,0:T(8,128)(2,1)}, bf16[256,2048]{1,0:T(8,128)(2,1)}, u32[]{:S(2)}, u32[]{:S(2)}) collective-permute-start(bf16[256,2048]{1,0:T(8,128)(2,1)} %shard_map.257), channel_id=1, source_target_pairs={{0,16},{16,0},{1,17},{17,1},{2,18},{18,2},{3,19},{19,3},{4,20},{20... | collective-permute-start | bytes 3145736 | tf_op jit(solution)/shard_map/ppermute | solution.py:502
  530.8 23.6 %collective-permute-start.75 = (bf16[256,512]{1,0:T(8,128)(2,1)S(1)}, bf16[256,512]{1,0:T(8,128)(2,1)S(1)}, u32[]{:S(2)}, u32[]{:S(2)}) collective-permute-start(bf16[256,512]{1,0:T(8,128)(2,1)S(1)} %get-tuple-element.534), channel_id=1, source_target_pairs={{0,12},{4,8},{8,4},{12,0},{1,13},{5,9},{9,5},{13,1},{2,14},{6,10},... | collective-permute-start | bytes 786440 | tf_op jit(solution)/shard_map/ppermute | solution.py:516
  532.7 35.7 %collective-permute-start.77 = (bf16[256,512]{1,0:T(8,128)(2,1)}, bf16[256,512]{1,0:T(8,128)(2,1)}, u32[]{:S(2)}, u32[]{:S(2)}) collective-permute-start(bf16[256,512]{1,0:T(8,128)(2,1)} %get-tuple-element.538), channel_id=1, source_target_pairs={{0,4},{4,0},{8,12},{12,8},{1,5},{5,1},{9,13},{13,9},{2,6},{6,2},{1... | collective-permute-start | bytes 786440 | tf_op jit(solution)/shard_map/ppermute | solution.py:516
  542.3 26.1 %collective-permute-start.78 = (bf16[256,512]{1,0:T(8,128)(2,1)}, bf16[256,512]{1,0:T(8,128)(2,1)}, u32[]{:S(2)}, u32[]{:S(2)}) collective-permute-start(bf16[256,512]{1,0:T(8,128)(2,1)} %get-tuple-element.550), channel_id=1, source_target_pairs={{0,8},{4,12},{8,0},{12,4},{1,9},{5,13},{9,1},{13,5},{2,10},{6,14},... | collective-permute-start | bytes 786440 | tf_op jit(solution)/shard_map/ppermute | solution.py:516
  544.9 27.7 %collective-permute-start.79 = (bf16[256,512]{1,0:T(8,128)(2,1)}, bf16[256,512]{1,0:T(8,128)(2,1)}, u32[]{:S(2)}, u32[]{:S(2)}) collective-permute-start(bf16[256,512]{1,0:T(8,128)(2,1)} %get-tuple-element.551), channel_id=1, source_target_pairs={{0,12},{4,8},{8,4},{12,0},{1,13},{5,9},{9,5},{13,1},{2,14},{6,10},... | collective-permute-start | bytes 786440 | tf_op jit(solution)/shard_map/ppermute | solution.py:516
  584.0 23.8 %collective-permute-start.82 = (bf16[1024,1024]{1,0:T(8,128)(2,1)}, bf16[1024,1024]{1,0:T(8,128)(2,1)}, u32[]{:S(2)}, u32[]{:S(2)}) collective-permute-start(bf16[1024,1024]{1,0:T(8,128)(2,1)} %shard_map.261), channel_id=1, source_target_pairs={{0,16},{16,0},{1,17},{17,1},{2,18},{18,2},{3,19},{19,3},{4,20},{20... | collective-permute-start | bytes 6291464 | tf_op jit(solution)/shard_map/ppermute | solution.py:502
  584.2 37.7 %collective-permute-start.91 = (bf16[128,2048]{1,0:T(8,128)(2,1)}, bf16[128,2048]{1,0:T(8,128)(2,1)}, u32[]{:S(2)}, u32[]{:S(2)}) collective-permute-start(bf16[128,2048]{1,0:T(8,128)(2,1)} %copy-done.141), channel_id=1, source_target_pairs={{0,4},{4,0},{8,12},{12,8},{16,24},{20,28},{24,16},{28,20},{1,5},{5... | collective-permute-start | bytes 1572872 | tf_op jit(solution)/shard_map/ppermute | solution.py:782
  607.8 190.4 %reduce-scatter.9.cloned.1.call-start = ((), (), s32[]{:S(2)}) async-start(), calls=%async_computation.8 | async-start | bytes 3932160 | tf_op jit(solution)/shard_map/reduce_scatter | solution.py:474
  690.1 45.1 %collective-permute-start.105 = (bf16[1024,3072]{1,0:T(8,128)(2,1)}, bf16[1024,3072]{1,0:T(8,128)(2,1)}, u32[]{:S(2)}, u32[]{:S(2)}) collective-permute-start(bf16[1024,3072]{1,0:T(8,128)(2,1)} %shard_map.268), channel_id=1, source_target_pairs={{0,16},{16,0},{1,17},{17,1},{2,18},{18,2},{3,19},{19,3},{4,20},{20... | collective-permute-start | bytes 18874376 | tf_op jit(solution)/shard_map/ppermute | solution.py:502
  690.7 31.5 %collective-permute-start.92 = (bf16[768,2048]{1,0:T(8,128)(2,1)}, bf16[768,2048]{1,0:T(8,128)(2,1)}, u32[]{:S(2)}, u32[]{:S(2)}) collective-permute-start(bf16[768,2048]{1,0:T(8,128)(2,1)} %all-gather.7.cloned.1.call-done.refs_2_), channel_id=1, source_target_pairs={{0,16},{1,17},{2,18},{3,19},{4,20},{5,21},{6,22},{7,23},{8,24},{9,... | collective-permute-start | bytes 9437192 | tf_op jit(solution)/shard_map/ppermute | solution.py:506
  694.4 28.5 %collective-permute-start.86 = (bf16[512,1024]{1,0:T(8,128)(2,1)}, bf16[512,1024]{1,0:T(8,128)(2,1)}, u32[]{:S(2)}, u32[]{:S(2)}) collective-permute-start(bf16[512,1024]{1,0:T(8,128)(2,1)} %copy-done.64), channel_id=1, source_target_pairs={{0,4},{4,0},{8,12},{12,8},{16,24},{20,28},{24,16},{28,20},{1,5},{5... | collective-permute-start | bytes 3145736 | tf_op jit(solution)/shard_map/ppermute | solution.py:782
  711.8 33.4 %collective-permute-start.108 = (bf16[64,2048]{1,0:T(8,128)(2,1)}, bf16[64,2048]{1,0:T(8,128)(2,1)}, u32[]{:S(2)}, u32[]{:S(2)}) collective-permute-start(bf16[64,2048]{1,0:T(8,128)(2,1)} %constant_dynamic-slice_fusion.3), channel_id=1, source_target_pairs={{0,8},{4,12},{8,0},{12,4},{16,20},{20,16},{24,28},{28,24},{1,9},{5... | collective-permute-start | bytes 786440 | tf_op jit(solution)/shard_map/ppermute | solution.py:782
  722.9 192.6 %reduce-scatter.11.cloned.1.call-start = ((), (), s32[]{:S(2)}) async-start(), calls=%async_computation.9 | async-start | bytes 7864320 | tf_op jit(solution)/shard_map/reduce_scatter | solution.py:474
  747.8 56.1 %collective-permute-start.117 = (bf16[1024,3072]{1,0:T(8,128)(2,1)}, bf16[1024,3072]{1,0:T(8,128)(2,1)}, u32[]{:S(2)}, u32[]{:S(2)}) collective-permute-start(bf16[1024,3072]{1,0:T(8,128)(2,1)} %all-gather.9.cloned.1.call-done.refs_2_), channel_id=1, source_target_pairs={{0,16},{1,17},{2,18},{3,19},{4,20},{5,21},{6,22},{7,23},{8,24},{9,... | collective-permute-start | bytes 18874376 | tf_op jit(solution)/shard_map/ppermute | solution.py:506
  769.5 32.4 %collective-permute-start.57 = (bf16[64,2048]{1,0:T(8,128)(2,1)}, bf16[64,2048]{1,0:T(8,128)(2,1)}, u32[]{:S(2)}, u32[]{:S(2)}) collective-permute-start(bf16[64,2048]{1,0:T(8,128)(2,1)} %add_convert_fusion.25), channel_id=1, source_target_pairs={{0,1},{1,2},{2,3},{3,0},{4,5},{5,6},{6,7},{7,4},{8,9},{9,10},{10,1... | collective-permute-start | bytes 786440 | tf_op jit(solution)/shard_map/ppermute | solution.py:511
  769.5 35.4 %collective-permute-start.116 = (bf16[64,2048]{1,0:T(8,128)(2,1)}, bf16[64,2048]{1,0:T(8,128)(2,1)}, u32[]{:S(2)}, u32[]{:S(2)}) collective-permute-start(bf16[64,2048]{1,0:T(8,128)(2,1)} %add_convert_fusion.11), channel_id=1, source_target_pairs={{0,8},{4,12},{8,0},{12,4},{16,20},{20,16},{24,28},{28,24},{1,9},{5... | collective-permute-start | bytes 786440 | tf_op jit(solution)/shard_map/ppermute | solution.py:782
  799.8 43.3 %collective-permute-start.123 = (bf16[256,2048]{1,0:T(8,128)(2,1)S(1)}, bf16[256,2048]{1,0:T(8,128)(2,1)S(1)}, u32[]{:S(2)}, u32[]{:S(2)}) collective-permute-start(bf16[256,2048]{1,0:T(8,128)(2,1)S(1)} %shard_map.273), channel_id=1, source_target_pairs={{0,16},{16,0},{1,17},{17,1},{2,18},{18,2},{3,19},{19,3},{4,20},{20... | collective-permute-start | bytes 3145736 | tf_op jit(solution)/shard_map/ppermute | solution.py:502
  802.3 46.6 %collective-permute-start.120 = (bf16[256,512]{1,0:T(8,128)(2,1)S(1)}, bf16[256,512]{1,0:T(8,128)(2,1)S(1)}, u32[]{:S(2)}, u32[]{:S(2)}) collective-permute-start(bf16[256,512]{1,0:T(8,128)(2,1)S(1)} %copy-done.201), channel_id=1, source_target_pairs={{0,4},{4,0},{8,12},{12,8},{1,5},{5,1},{9,13},{13,9},{2,6},{6,2},{1... | collective-permute-start | bytes 786440 | tf_op jit(solution)/shard_map/ppermute | solution.py:516
  804.9 33.5 %collective-permute-start.115 = (bf16[256,512]{1,0:T(8,128)(2,1)S(1)}, bf16[256,512]{1,0:T(8,128)(2,1)S(1)}, u32[]{:S(2)}, u32[]{:S(2)}) collective-permute-start(bf16[256,512]{1,0:T(8,128)(2,1)S(1)} %copy-done.203), channel_id=1, source_target_pairs={{0,12},{4,8},{8,4},{12,0},{1,13},{5,9},{9,5},{13,1},{2,14},{6,10},... | collective-permute-start | bytes 786440 | tf_op jit(solution)/shard_map/ppermute | solution.py:516
  816.6 32.7 %collective-permute-start.121 = (bf16[256,512]{1,0:T(8,128)(2,1)S(1)}, bf16[256,512]{1,0:T(8,128)(2,1)S(1)}, u32[]{:S(2)}, u32[]{:S(2)}) collective-permute-start(bf16[256,512]{1,0:T(8,128)(2,1)S(1)} %copy-done.199), channel_id=1, source_target_pairs={{0,8},{4,12},{8,0},{12,4},{1,9},{5,13},{9,1},{13,5},{2,10},{6,14},... | collective-permute-start | bytes 786440 | tf_op jit(solution)/shard_map/ppermute | solution.py:516
  818.3 32.4 %collective-permute-start.122 = (bf16[256,512]{1,0:T(8,128)(2,1)S(1)}, bf16[256,512]{1,0:T(8,128)(2,1)S(1)}, u32[]{:S(2)}, u32[]{:S(2)}) collective-permute-start(bf16[256,512]{1,0:T(8,128)(2,1)S(1)} %copy-done.197), channel_id=1, source_target_pairs={{0,12},{4,8},{8,4},{12,0},{1,13},{5,9},{9,5},{13,1},{2,14},{6,10},... | collective-permute-start | bytes 786440 | tf_op jit(solution)/shard_map/ppermute | solution.py:516
  838.4 25.6 %collective-permute-start.126 = (bf16[192,2048]{1,0:T(8,128)(2,1)S(1)}, bf16[192,2048]{1,0:T(8,128)(2,1)}, u32[]{:S(2)}, u32[]{:S(2)}) collective-permute-start(bf16[192,2048]{1,0:T(8,128)(2,1)S(1)} %copy-done.280), channel_id=1, source_target_pairs={{0,4},{4,0},{8,12},{12,8},{16,24},{20,28},{24,16},{28,20},{1,5},{5... | collective-permute-start | bytes 2359304 | tf_op jit(solution)/shard_map/ppermute | solution.py:782
  848.9 26.1 %collective-permute-start.110 = (bf16[256,1024]{1,0:T(8,128)(2,1)S(1)}, bf16[256,1024]{1,0:T(8,128)(2,1)S(1)}, u32[]{:S(2)}, u32[]{:S(2)}) collective-permute-start(bf16[256,1024]{1,0:T(8,128)(2,1)S(1)} %copy-done.260), channel_id=1, source_target_pairs={{0,8},{4,12},{8,0},{12,4},{16,20},{20,16},{24,28},{28,24},{1,9},{5... | collective-permute-start | bytes 1572872 | tf_op jit(solution)/shard_map/ppermute | solution.py:782
  849.3 30.2 %collective-permute-start.131 = (bf16[128,2048]{1,0:T(8,128)(2,1)S(1)}, bf16[128,2048]{1,0:T(8,128)(2,1)}, u32[]{:S(2)}, u32[]{:S(2)}) collective-permute-start(bf16[128,2048]{1,0:T(8,128)(2,1)S(1)} %shard_map.275), channel_id=1, source_target_pairs={{0,4},{4,0},{8,12},{12,8},{16,24},{20,28},{24,16},{28,20},{1,5},{5... | collective-permute-start | bytes 1572872 | tf_op jit(solution)/shard_map/ppermute | solution.py:782
  865.5 37.3 %collective-permute-start.134 = (bf16[2,192,2048]{2,1,0:T(8,128)(2,1)S(1)}, bf16[2,192,2048]{2,1,0:T(8,128)(2,1)S(1)}, u32[]{:S(2)}, u32[]{:S(2)}) collective-permute-start(bf16[2,192,2048]{2,1,0:T(8,128)(2,1)S(1)} %pad_maximum_fusion.6), channel_id=1, source_target_pairs={{0,8},{4,12},{8,0},{12,4},{16,20},{20,16},{24,28},{28,24},{1,9},{5... | collective-permute-start | bytes 4718600 | tf_op jit(solution)/shard_map/ppermute | solution.py:782
  875.7 27.7 %collective-permute-start.128 = (bf16[64,2048]{1,0:T(8,128)(2,1)S(1)}, bf16[64,2048]{1,0:T(8,128)(2,1)S(1)}, u32[]{:S(2)}, u32[]{:S(2)}) collective-permute-start(bf16[64,2048]{1,0:T(8,128)(2,1)S(1)} %add_convert_fusion.8), channel_id=1, source_target_pairs={{0,1},{1,2},{2,3},{3,0},{4,5},{5,6},{6,7},{7,4},{8,9},{9,10},{10,1... | collective-permute-start | bytes 786440 | tf_op jit(solution)/shard_map/ppermute | solution.py:511
  882.8 35.5 %collective-permute-start.138 = (bf16[128,2048]{1,0:T(8,128)(2,1)}, bf16[128,2048]{1,0:T(8,128)(2,1)}, u32[]{:S(2)}, u32[]{:S(2)}) collective-permute-start(bf16[128,2048]{1,0:T(8,128)(2,1)} %pad_maximum_fusion.27), channel_id=1, source_target_pairs={{0,4},{4,0},{8,12},{12,8},{16,24},{20,28},{24,16},{28,20},{1,5},{5... | collective-permute-start | bytes 1572872 | tf_op jit(solution)/shard_map/ppermute | solution.py:782
  884.1 31.5 %collective-permute-start.133 = (bf16[64,2048]{1,0:T(8,128)(2,1)}, bf16[64,2048]{1,0:T(8,128)(2,1)}, u32[]{:S(2)}, u32[]{:S(2)}) collective-permute-start(bf16[64,2048]{1,0:T(8,128)(2,1)} %constant_dynamic-slice_fusion.1), channel_id=1, source_target_pairs={{0,8},{4,12},{8,0},{12,4},{16,20},{20,16},{24,28},{28,24},{1,9},{5... | collective-permute-start | bytes 786440 | tf_op jit(solution)/shard_map/ppermute | solution.py:782
  902.8 38.8 %collective-permute-start.127 = (bf16[512,1024]{1,0:T(8,128)(2,1)}, bf16[512,1024]{1,0:T(8,128)(2,1)}, u32[]{:S(2)}, u32[]{:S(2)}) collective-permute-start(bf16[512,1024]{1,0:T(8,128)(2,1)} %pad_maximum_fusion.23), channel_id=1, source_target_pairs={{0,4},{4,0},{8,12},{12,8},{16,24},{20,28},{24,16},{28,20},{1,5},{5... | collective-permute-start | bytes 3145736 | tf_op jit(solution)/shard_map/ppermute | solution.py:782
  903.4 33.6 %collective-permute-start.136 = (bf16[512,1024]{1,0:T(8,128)(2,1)}, bf16[512,1024]{1,0:T(8,128)(2,1)}, u32[]{:S(2)}, u32[]{:S(2)}) collective-permute-start(bf16[512,1024]{1,0:T(8,128)(2,1)} %shard_map.279), channel_id=1, source_target_pairs={{0,4},{4,0},{8,12},{12,8},{16,24},{20,28},{24,16},{28,20},{1,5},{5... | collective-permute-start | bytes 3145736 | tf_op jit(solution)/shard_map/ppermute | solution.py:782
  915.5 29.7 %collective-permute-start.145 = (bf16[64,2048]{1,0:T(8,128)(2,1)}, bf16[64,2048]{1,0:T(8,128)(2,1)S(1)}, u32[]{:S(2)}, u32[]{:S(2)}) collective-permute-start(bf16[64,2048]{1,0:T(8,128)(2,1)} %broadcast_select_fusion.27), channel_id=1, source_target_pairs={{0,0},{1,2},{2,1},{3,3},{4,4},{5,6},{6,5},{7,7},{8,8},{9,10},{10,9... | collective-permute-start | bytes 786440 | tf_op jit(solution)/shard_map/ppermute | solution.py:907
  922.6 25.3 %collective-permute-start.146 = (bf16[64,2048]{1,0:T(8,128)(2,1)S(1)}, bf16[64,2048]{1,0:T(8,128)(2,1)S(1)}, u32[]{:S(2)}, u32[]{:S(2)}) collective-permute-start(bf16[64,2048]{1,0:T(8,128)(2,1)S(1)} %copy-done.288), channel_id=1, source_target_pairs={{0,2},{1,0},{2,3},{3,1},{4,6},{5,4},{6,7},{7,5},{8,10},{9,8},{10,1... | collective-permute-start | bytes 786440 | tf_op jit(solution)/shard_map/ppermute | solution.py:907
  941.0 28.8 %collective-permute-start.143 = (bf16[256,3072]{1,0:T(8,128)(2,1)S(1)}, bf16[256,3072]{1,0:T(8,128)(2,1)S(1)}, u32[]{:S(2)}, u32[]{:S(2)}) collective-permute-start(bf16[256,3072]{1,0:T(8,128)(2,1)S(1)} %copy-done.264), channel_id=1, source_target_pairs={{0,4},{4,0},{8,12},{12,8},{16,24},{20,28},{24,16},{28,20},{1,5},{5... | collective-permute-start | bytes 4718600 | tf_op jit(solution)/shard_map/ppermute | solution.py:782
  945.3 26.6 %collective-permute-start.140 = (bf16[256,2048]{1,0:T(8,128)(2,1)S(1)}, bf16[256,2048]{1,0:T(8,128)(2,1)S(1)}, u32[]{:S(2)}, u32[]{:S(2)}) collective-permute-start(bf16[256,2048]{1,0:T(8,128)(2,1)S(1)} %pad_maximum_fusion.24.refs_2_), channel_id=1, source_target_pairs={{0,16},{1,17},{2,18},{3,19},{4,20},{5,21},{6,22},{7,23},{8,24},{9,... | collective-permute-start | bytes 3145736 | tf_op jit(solution)/shard_map/ppermute | solution.py:506
  971.0 44.2 %collective-permute-start.158 = (bf16[2,256,3072]{2,1,0:T(8,128)(2,1)S(1)}, bf16[2,256,3072]{2,1,0:T(8,128)(2,1)S(1)}, u32[]{:S(2)}, u32[]{:S(2)}) collective-permute-start(bf16[2,256,3072]{2,1,0:T(8,128)(2,1)S(1)} %pad_maximum_fusion.3), channel_id=1, source_target_pairs={{0,8},{4,12},{8,0},{12,4},{16,20},{20,16},{24,28},{28,24},{1,9},{5... | collective-permute-start | bytes 9437192 | tf_op jit(solution)/shard_map/ppermute | solution.py:782
  989.6 25.3 %collective-permute-start.159 = (bf16[256,1024]{1,0:T(8,128)(2,1)S(1)}, bf16[256,1024]{1,0:T(8,128)(2,1)S(1)}, u32[]{:S(2)}, u32[]{:S(2)}) collective-permute-start(bf16[256,1024]{1,0:T(8,128)(2,1)S(1)} %add_convert_fusion.2), channel_id=1, source_target_pairs={{0,8},{4,12},{8,0},{12,4},{16,20},{20,16},{24,28},{28,24},{1,9},{5... | collective-permute-start | bytes 1572872 | tf_op jit(solution)/shard_map/ppermute | solution.py:782
  (479 other events, 6497.0 us)
Sparse Core Ops, SparseCore 0:
  10.2 48.5 all-gather.10
  60.9 56.7 all-gather.12
  437.1 42.2 reduce-scatter.4
  482.8 87.1 reduce-scatter.6
  571.7 48.8 all-gather.6
  622.3 70.1 all-gather.8
  723.0 49.8 reduce-scatter.8
  776.5 107.5 reduce-scatter.10

commit v3 on v2

--- a/solution.py
+++ b/solution.py
@@ -346,7 +346,7 @@
 
 def assemble(place, arrays, widths):
     rows, cols = arrays[0].shape
-    tile = 128
+    tile = 256
     while rows % tile:
         tile //= 2
     steps = rows // tile

time: 1080 us -> 1080 us (level)
  no operation moved by 1% of the time
where the time goes in v3:
time: 1080 us; the launch traced here: 1070 us
  waiting for transfers between devices  486 us (45%)
  Pallas kernels  277 us (26%)
  starting transfers between devices  121 us (11%)
  other arithmetic  111 us (10%)
  local copies, waits for them, and re-layouts  48.8 us (5%)
  between operations  22.3 us (2%)
    ppermute x84, waiting for transfers between devices, ring_step(): return lax.ppermute(block, MP, [(i, (i + 1) % count) for i in range(count)])  323 us
    pallas_call x24, Pallas kernels, kernel_call(): pl.pallas_call(whole, out_shape=out_shape, in_specs=[hbm] * (n_args + 2 *...  155 us
    pallas_call x20, Pallas kernels, piece_product(): pl.pallas_call(functools.partial(product_body, len(lefts), [len(group) fo...  90.8 us
    ppermute x20, waiting for transfers between devices, joint_step(): return lambda block: lax.ppermute(block, (CORES, CTX), route)  61.9 us
    ppermute x24, waiting for transfers between devices, across_ctx(): lax.ppermute(block, CTX, [(i, i ^ distance) for i in range(count)])  57.8 us
    unnamed x712, local copies, waits for them, and re-layouts  37.9 us
    all_gather x2, waiting for transfers between devices, gather_lane(): lax.all_gather(x, MP, axis=0, tiled=True)  35.7 us
    pallas_call x4, Pallas kernels, assemble(): pl.pallas_call(functools.partial(assemble_body, widths), out_shape=[jax.S...  30.9 us
  transfers between devices with their start and end apart: 171, of which 87 were waited for; matrix products, arithmetic and copies ran while one was open for 11% of the time, Pallas kernels for 24%

profile of v3, /device:TPU:0, one launch (start us, length us, event | category | flops | bytes accessed | tf_op | source)
XLA Modules:
  0.0 1066.1 jit_solution(9174204286193632270)
XLA Ops:
  23.0 35.7 %all-gather.11.cloned.1.call-done = bf16[1,512,2048]{2,1,0:T(8,128)(2,1)} async-done(((bf16[1,128,2048]{2,1,0:T(8,128)(2,1)}), bf16[1,512,2048]{2,1,0:T(8,128)(2,1)}) %all-gather.11.cloned.1.call-update) | async-done | bytes 2097168 | tf_op jit(solution)/shard_map/all_gather | solution.py:943
  97.0 10.1 collective-permute-done.9
  109.4 8.7 collective-permute-done.14
  118.3 5.6 collective-permute-done.13
  146.6 5.6 collective-permute-done.20
  163.5 5.6 collective-permute-done.21
  170.1 8.6 shard_map.241
  182.6 8.6 shard_map.242
  192.2 10.1 collective-permute-done.26
  230.7 5.6 collective-permute-done.32
  282.5 5.9 collective-permute-done.39
  323.0 5.7 collective-permute-done.50
  345.6 8.6 shard_map.247
  357.3 8.6 shard_map.248
  368.1 8.1 collective-permute-done.56
  386.7 10.5 shard_map.249
  398.8 10.6 shard_map.250
  414.2 7.2 shard_map.252
  430.8 6.1 shard_map.253
  437.4 10.9 %collective-permute-done.64 = bf16[64,2048]{1,0:T(8,128)(2,1)S(1)} collective-permute-done((bf16[64,2048]{1,0:T(8,128)(2,1)}, bf16[64,2048]{1,0:T(8,128)(2,1)S(1)}, u32[]{:S(2)}, u32[]{:S(2)}) %collective-permute-start.64) | collective-permute-done | bytes 262176 | tf_op jit(solution)/shard_map/ppermute | solution.py:511
  461.8 10.1 shard_map.254
  472.2 11.2 %collective-permute-done.66 = bf16[64,2048]{1,0:T(8,128)(2,1)S(1)} collective-permute-done((bf16[64,2048]{1,0:T(8,128)(2,1)}, bf16[64,2048]{1,0:T(8,128)(2,1)S(1)}, u32[]{:S(2)}, u32[]{:S(2)}) %collective-permute-start.66) | collective-permute-done | bytes 262176 | tf_op jit(solution)/shard_map/ppermute | solution.py:511
  494.7 6.1 collective-permute-done.72
  508.6 7.0 shard_map.255
  518.1 7.9 shard_map.256
  533.5 8.8 collective-permute-done.73.refs_2_
  627.1 6.0 collective-permute-done.89
  638.6 5.7 collective-permute-done.93
  652.0 11.6 %shard_map.265 = (bf16[256,1536]{1,0:T(8,128)(2,1)S(1)}, bf16[256,1536]{1,0:T(8,128)(2,1)S(1)}, bf16[64,2048]{1,0:T(8,128)(2,1)S(1)}, bf16[64,2048]{1,0:T(8,128)...) custom-call(bf16[256,2048]{1,0:T(8,128)(2,1)} %pad_maximum_fusion.19.refs_0_.refs_2_, ...), custom_call_target="tpu_custom_call" | custom-call | flops 4831838208 | bytes 24117248 | tf_op jit(solution)/shard_map/pallas_call | solution.py:71
  666.4 11.3 %shard_map.266 = (bf16[256,1536]{1,0:T(8,128)(2,1)S(1)}, bf16[256,1536]{1,0:T(8,128)(2,1)S(1)}, bf16[64,2048]{1,0:T(8,128)(2,1)S(1)}, bf16[64,2048]{1,0:T(8,128)...) custom-call(bf16[256,2048]{1,0:T(8,128)(2,1)} %pad_maximum_fusion.20.refs_0_.refs_3_, ...), custom_call_target="tpu_custom_call" | custom-call | flops 4831838208 | bytes 24117248 | tf_op jit(solution)/shard_map/pallas_call | solution.py:71
  682.9 7.2 shard_map.268
  705.0 6.1 collective-permute-done.101
  712.4 6.1 shard_map.269
  735.3 9.9 shard_map.270
  757.2 6.7 collective-permute-done.107
  779.2 6.8 shard_map.271
  788.4 7.0 shard_map.272
  807.8 8.8 collective-permute-done.113.refs_2_
  819.2 19.2 %collective-permute-done.115.refs_4_ = bf16[256,512]{1,0:T(8,128)(2,1)S(1)} collective-permute-done((bf16[256,512]{1,0:T(8,128)(2,1)S(1)}, bf16[256,512]{1,0:T(8,128)(2,1)S(1)}, u32[]{:S(2)}, u32[]{:S(2)}) %collective-permute-start.115) | collective-permute-done | bytes 262176 | tf_op jit(solution)/shard_map/ppermute | solution.py:516
  868.9 6.1 collective-permute-done.110
  889.8 13.0 %collective-permute-done.134 = bf16[2,192,2048]{2,1,0:T(8,128)(2,1)S(1)} collective-permute-done((bf16[2,192,2048]{2,1,0:T(8,128)(2,1)S(1)}, bf16[2,192,2048]{2,1,0:T(8,128)(2,1)S(1)}, u32[]{:S(2)}, u32[]{:S(2)}) %collective-permute-start.134) | collective-permute-done | bytes 1572896 | tf_op jit(solution)/shard_map/ppermute | solution.py:782
  926.7 8.4 shard_map.281
  951.3 16.7 %collective-permute-done.143 = bf16[256,3072]{1,0:T(8,128)(2,1)S(1)} collective-permute-done((bf16[256,3072]{1,0:T(8,128)(2,1)S(1)}, bf16[256,3072]{1,0:T(8,128)(2,1)S(1)}, u32[]{:S(2)}, u32[]{:S(2)}) %collective-permute-start.143) | collective-permute-done | bytes 1572896 | tf_op jit(solution)/shard_map/ppermute | solution.py:782
  970.4 12.4 %collective-permute-done.153 = bf16[128,2048]{1,0:T(8,128)(2,1)S(1)} collective-permute-done((bf16[128,2048]{1,0:T(8,128)(2,1)S(1)}, bf16[128,2048]{1,0:T(8,128)(2,1)S(1)}, u32[]{:S(2)}, u32[]{:S(2)}) %collective-permute-start.153) | collective-permute-done | bytes 524320 | tf_op jit(solution)/shard_map/ppermute | solution.py:782
  989.0 5.9 collective-permute-start.150
  994.9 10.2 collective-permute-start.152
  1021.6 11.7 %collective-permute-done.160 = bf16[512,1024]{1,0:T(8,128)(2,1)S(1)} collective-permute-done((bf16[512,1024]{1,0:T(8,128)(2,1)S(1)}, bf16[512,1024]{1,0:T(8,128)(2,1)S(1)}, u32[]{:S(2)}, u32[]{:S(2)}) %collective-permute-start.160) | collective-permute-done | bytes 1048608 | tf_op jit(solution)/shard_map/ppermute | solution.py:782
  1038.7 15.7 %shard_map.283 = (f32[2048,1536]{1,0:T(8,128)}, f32[2048,1536]{1,0:T(8,128)}) custom-call(s32[1]{0:T(128)} %bitcast.26.place, bf16[1024,3072]{1,0:T(8,128)(2,1)} %pad_maximum_fusion.refs_0_, bf16[1024,3072]{1,0:T(8,128)(2,1)} %collective-permute-done.162.refs_1_, bf16[1024,3072]{1,0:T(8,128)(2,1)S(1)} %bitcast.95, ...), custom_call_target="tpu_custom_call" | custom-call | bytes 37748736 | tf_op jit(solution)/shard_map/pallas_call | solution.py:365
  (1268 shorter events, 593.9 us)
Async XLA Ops:
  7.2 51.5 %all-gather.11.cloned.1.call-start = ((), (), s32[]{:S(2)}) async-start(), calls=%async_computation.10 | async-start | bytes 2621440 | tf_op jit(solution)/shard_map/all_gather | solution.py:943
  9.4 126.3 %all-gather.13.cloned.1.call-start = ((), (), s32[]{:S(2)}) async-start(), calls=%async_computation.11 | async-start | bytes 2621440 | tf_op jit(solution)/shard_map/all_gather | solution.py:943
  9.4 49.4 %collective-permute-start.2 = (bf16[2048,1536]{1,0:T(8,128)(2,1)}, bf16[2048,1536]{1,0:T(8,128)(2,1)}, u32[]{:S(2)}, u32[]{:S(2)}) collective-permute-start(bf16[2048,1536]{1,0:T(8,128)(2,1)} %bitcast.100), channel_id=1, source_target_pairs={{0,16},{16,0},{1,17},{17,1},{2,18},{18,2},{3,19},{19,3},{4,20},{20... | collective-permute-start | bytes 18874376 | tf_op jit(solution)/shard_map/ppermute | solution.py:502
  9.9 48.8 %collective-permute-start.3 = (bf16[2048,1536]{1,0:T(8,128)(2,1)}, bf16[2048,1536]{1,0:T(8,128)(2,1)}, u32[]{:S(2)}, u32[]{:S(2)}) collective-permute-start(bf16[2048,1536]{1,0:T(8,128)(2,1)} %bitcast.109), channel_id=1, source_target_pairs={{0,16},{16,0},{1,17},{17,1},{2,18},{18,2},{3,19},{19,3},{4,20},{20... | collective-permute-start | bytes 18874376 | tf_op jit(solution)/shard_map/ppermute | solution.py:502
  10.0 48.8 %collective-permute-start.4 = (bf16[1536,2048]{1,0:T(8,128)(2,1)}, bf16[1536,2048]{1,0:T(8,128)(2,1)}, u32[]{:S(2)}, u32[]{:S(2)}) collective-permute-start(bf16[1536,2048]{1,0:T(8,128)(2,1)} %bitcast.118), channel_id=1, source_target_pairs={{0,16},{16,0},{1,17},{17,1},{2,18},{18,2},{3,19},{19,3},{4,20},{20... | collective-permute-start | bytes 18874376 | tf_op jit(solution)/shard_map/ppermute | solution.py:502
  14.2 44.6 %collective-permute-start = (bf16[2048,1024]{1,0:T(8,128)(2,1)}, bf16[2048,1024]{1,0:T(8,128)(2,1)}, u32[]{:S(2)}, u32[]{:S(2)}) collective-permute-start(bf16[2048,1024]{1,0:T(8,128)(2,1)} %pad_maximum_fusion.1.refs_3_.refs_8_), channel_id=1, source_target_pairs={{0,16},{16,0},{1,17},{17,1},{2,18},{18,2},{3,19},{19,3},{4,20},{20... | collective-permute-start | bytes 12582920 | tf_op jit(solution)/shard_map/ppermute | solution.py:502
  15.8 485.0 %reduce-scatter.5.cloned.1.call-start = ((), (), s32[]{:S(2)}) async-start(), calls=%async_computation.4 | async-start | bytes 3932160 | tf_op jit(solution)/shard_map/reduce_scatter | solution.py:474
  20.6 38.2 %collective-permute-start.1 = (bf16[512,2048]{1,0:T(8,128)(2,1)}, bf16[512,2048]{1,0:T(8,128)(2,1)}, u32[]{:S(2)}, u32[]{:S(2)}) collective-permute-start(bf16[512,2048]{1,0:T(8,128)(2,1)} %bitcast.127), channel_id=1, source_target_pairs={{0,16},{16,0},{1,17},{17,1},{2,18},{18,2},{3,19},{19,3},{4,20},{20... | collective-permute-start | bytes 6291464 | tf_op jit(solution)/shard_map/ppermute | solution.py:502
  421.4 40.4 %collective-permute-start.67 = (bf16[1024,3072]{1,0:T(8,128)(2,1)}, bf16[1024,3072]{1,0:T(8,128)(2,1)}, u32[]{:S(2)}, u32[]{:S(2)}) collective-permute-start(bf16[1024,3072]{1,0:T(8,128)(2,1)} %shard_map.252), channel_id=1, source_target_pairs={{0,16},{16,0},{1,17},{17,1},{2,18},{18,2},{3,19},{19,3},{4,20},{20... | collective-permute-start | bytes 18874376 | tf_op jit(solution)/shard_map/ppermute | solution.py:502
  437.0 159.5 %reduce-scatter.7.cloned.1.call-start = ((), (), s32[]{:S(2)}) async-start(), calls=%async_computation.5 | async-start | bytes 7864320 | tf_op jit(solution)/shard_map/reduce_scatter | solution.py:474
  472.0 161.1 %all-gather.7.cloned.1.call-start = ((), (), s32[]{:S(2)}) async-start(), calls=%async_computation.6 | async-start | bytes 3932160 | tf_op jit(solution)/shard_map/all_gather | solution.py:474
  505.9 241.9 %all-gather.9.cloned.1.call-start = ((), (), s32[]{:S(2)}) async-start(), calls=%async_computation.7 | async-start | bytes 7864320 | tf_op jit(solution)/shard_map/all_gather | solution.py:474
  529.1 33.8 %collective-permute-start.80 = (bf16[256,2048]{1,0:T(8,128)(2,1)}, bf16[256,2048]{1,0:T(8,128)(2,1)}, u32[]{:S(2)}, u32[]{:S(2)}) collective-permute-start(bf16[256,2048]{1,0:T(8,128)(2,1)} %shard_map.257), channel_id=1, source_target_pairs={{0,16},{16,0},{1,17},{17,1},{2,18},{18,2},{3,19},{19,3},{4,20},{20... | collective-permute-start | bytes 3145736 | tf_op jit(solution)/shard_map/ppermute | solution.py:502
  530.8 23.6 %collective-permute-start.75 = (bf16[256,512]{1,0:T(8,128)(2,1)S(1)}, bf16[256,512]{1,0:T(8,128)(2,1)S(1)}, u32[]{:S(2)}, u32[]{:S(2)}) collective-permute-start(bf16[256,512]{1,0:T(8,128)(2,1)S(1)} %get-tuple-element.534), channel_id=1, source_target_pairs={{0,12},{4,8},{8,4},{12,0},{1,13},{5,9},{9,5},{13,1},{2,14},{6,10},... | collective-permute-start | bytes 786440 | tf_op jit(solution)/shard_map/ppermute | solution.py:516
  532.7 35.7 %collective-permute-start.77 = (bf16[256,512]{1,0:T(8,128)(2,1)}, bf16[256,512]{1,0:T(8,128)(2,1)}, u32[]{:S(2)}, u32[]{:S(2)}) collective-permute-start(bf16[256,512]{1,0:T(8,128)(2,1)} %get-tuple-element.538), channel_id=1, source_target_pairs={{0,4},{4,0},{8,12},{12,8},{1,5},{5,1},{9,13},{13,9},{2,6},{6,2},{1... | collective-permute-start | bytes 786440 | tf_op jit(solution)/shard_map/ppermute | solution.py:516
  542.3 26.1 %collective-permute-start.78 = (bf16[256,512]{1,0:T(8,128)(2,1)}, bf16[256,512]{1,0:T(8,128)(2,1)}, u32[]{:S(2)}, u32[]{:S(2)}) collective-permute-start(bf16[256,512]{1,0:T(8,128)(2,1)} %get-tuple-element.550), channel_id=1, source_target_pairs={{0,8},{4,12},{8,0},{12,4},{1,9},{5,13},{9,1},{13,5},{2,10},{6,14},... | collective-permute-start | bytes 786440 | tf_op jit(solution)/shard_map/ppermute | solution.py:516
  544.9 27.7 %collective-permute-start.79 = (bf16[256,512]{1,0:T(8,128)(2,1)}, bf16[256,512]{1,0:T(8,128)(2,1)}, u32[]{:S(2)}, u32[]{:S(2)}) collective-permute-start(bf16[256,512]{1,0:T(8,128)(2,1)} %get-tuple-element.551), channel_id=1, source_target_pairs={{0,12},{4,8},{8,4},{12,0},{1,13},{5,9},{9,5},{13,1},{2,14},{6,10},... | collective-permute-start | bytes 786440 | tf_op jit(solution)/shard_map/ppermute | solution.py:516
  584.0 23.8 %collective-permute-start.82 = (bf16[1024,1024]{1,0:T(8,128)(2,1)}, bf16[1024,1024]{1,0:T(8,128)(2,1)}, u32[]{:S(2)}, u32[]{:S(2)}) collective-permute-start(bf16[1024,1024]{1,0:T(8,128)(2,1)} %shard_map.261), channel_id=1, source_target_pairs={{0,16},{16,0},{1,17},{17,1},{2,18},{18,2},{3,19},{19,3},{4,20},{20... | collective-permute-start | bytes 6291464 | tf_op jit(solution)/shard_map/ppermute | solution.py:502
  584.2 37.7 %collective-permute-start.91 = (bf16[128,2048]{1,0:T(8,128)(2,1)}, bf16[128,2048]{1,0:T(8,128)(2,1)}, u32[]{:S(2)}, u32[]{:S(2)}) collective-permute-start(bf16[128,2048]{1,0:T(8,128)(2,1)} %copy-done.141), channel_id=1, source_target_pairs={{0,4},{4,0},{8,12},{12,8},{16,24},{20,28},{24,16},{28,20},{1,5},{5... | collective-permute-start | bytes 1572872 | tf_op jit(solution)/shard_map/ppermute | solution.py:782
  607.8 190.4 %reduce-scatter.9.cloned.1.call-start = ((), (), s32[]{:S(2)}) async-start(), calls=%async_computation.8 | async-start | bytes 3932160 | tf_op jit(solution)/shard_map/reduce_scatter | solution.py:474
  690.1 45.1 %collective-permute-start.105 = (bf16[1024,3072]{1,0:T(8,128)(2,1)}, bf16[1024,3072]{1,0:T(8,128)(2,1)}, u32[]{:S(2)}, u32[]{:S(2)}) collective-permute-start(bf16[1024,3072]{1,0:T(8,128)(2,1)} %shard_map.268), channel_id=1, source_target_pairs={{0,16},{16,0},{1,17},{17,1},{2,18},{18,2},{3,19},{19,3},{4,20},{20... | collective-permute-start | bytes 18874376 | tf_op jit(solution)/shard_map/ppermute | solution.py:502
  690.7 31.5 %collective-permute-start.92 = (bf16[768,2048]{1,0:T(8,128)(2,1)}, bf16[768,2048]{1,0:T(8,128)(2,1)}, u32[]{:S(2)}, u32[]{:S(2)}) collective-permute-start(bf16[768,2048]{1,0:T(8,128)(2,1)} %all-gather.7.cloned.1.call-done.refs_2_), channel_id=1, source_target_pairs={{0,16},{1,17},{2,18},{3,19},{4,20},{5,21},{6,22},{7,23},{8,24},{9,... | collective-permute-start | bytes 9437192 | tf_op jit(solution)/shard_map/ppermute | solution.py:506
  694.4 28.5 %collective-permute-start.86 = (bf16[512,1024]{1,0:T(8,128)(2,1)}, bf16[512,1024]{1,0:T(8,128)(2,1)}, u32[]{:S(2)}, u32[]{:S(2)}) collective-permute-start(bf16[512,1024]{1,0:T(8,128)(2,1)} %copy-done.64), channel_id=1, source_target_pairs={{0,4},{4,0},{8,12},{12,8},{16,24},{20,28},{24,16},{28,20},{1,5},{5... | collective-permute-start | bytes 3145736 | tf_op jit(solution)/shard_map/ppermute | solution.py:782
  711.8 33.4 %collective-permute-start.108 = (bf16[64,2048]{1,0:T(8,128)(2,1)}, bf16[64,2048]{1,0:T(8,128)(2,1)}, u32[]{:S(2)}, u32[]{:S(2)}) collective-permute-start(bf16[64,2048]{1,0:T(8,128)(2,1)} %constant_dynamic-slice_fusion.3), channel_id=1, source_target_pairs={{0,8},{4,12},{8,0},{12,4},{16,20},{20,16},{24,28},{28,24},{1,9},{5... | collective-permute-start | bytes 786440 | tf_op jit(solution)/shard_map/ppermute | solution.py:782
  722.9 192.6 %reduce-scatter.11.cloned.1.call-start = ((), (), s32[]{:S(2)}) async-start(), calls=%async_computation.9 | async-start | bytes 7864320 | tf_op jit(solution)/shard_map/reduce_scatter | solution.py:474
  747.8 56.1 %collective-permute-start.117 = (bf16[1024,3072]{1,0:T(8,128)(2,1)}, bf16[1024,3072]{1,0:T(8,128)(2,1)}, u32[]{:S(2)}, u32[]{:S(2)}) collective-permute-start(bf16[1024,3072]{1,0:T(8,128)(2,1)} %all-gather.9.cloned.1.call-done.refs_2_), channel_id=1, source_target_pairs={{0,16},{1,17},{2,18},{3,19},{4,20},{5,21},{6,22},{7,23},{8,24},{9,... | collective-permute-start | bytes 18874376 | tf_op jit(solution)/shard_map/ppermute | solution.py:506
  769.5 32.4 %collective-permute-start.57 = (bf16[64,2048]{1,0:T(8,128)(2,1)}, bf16[64,2048]{1,0:T(8,128)(2,1)}, u32[]{:S(2)}, u32[]{:S(2)}) collective-permute-start(bf16[64,2048]{1,0:T(8,128)(2,1)} %add_convert_fusion.25), channel_id=1, source_target_pairs={{0,1},{1,2},{2,3},{3,0},{4,5},{5,6},{6,7},{7,4},{8,9},{9,10},{10,1... | collective-permute-start | bytes 786440 | tf_op jit(solution)/shard_map/ppermute | solution.py:511
  769.5 35.4 %collective-permute-start.116 = (bf16[64,2048]{1,0:T(8,128)(2,1)}, bf16[64,2048]{1,0:T(8,128)(2,1)}, u32[]{:S(2)}, u32[]{:S(2)}) collective-permute-start(bf16[64,2048]{1,0:T(8,128)(2,1)} %add_convert_fusion.11), channel_id=1, source_target_pairs={{0,8},{4,12},{8,0},{12,4},{16,20},{20,16},{24,28},{28,24},{1,9},{5... | collective-permute-start | bytes 786440 | tf_op jit(solution)/shard_map/ppermute | solution.py:782
  799.8 43.3 %collective-permute-start.123 = (bf16[256,2048]{1,0:T(8,128)(2,1)S(1)}, bf16[256,2048]{1,0:T(8,128)(2,1)S(1)}, u32[]{:S(2)}, u32[]{:S(2)}) collective-permute-start(bf16[256,2048]{1,0:T(8,128)(2,1)S(1)} %shard_map.273), channel_id=1, source_target_pairs={{0,16},{16,0},{1,17},{17,1},{2,18},{18,2},{3,19},{19,3},{4,20},{20... | collective-permute-start | bytes 3145736 | tf_op jit(solution)/shard_map/ppermute | solution.py:502
  802.3 46.6 %collective-permute-start.120 = (bf16[256,512]{1,0:T(8,128)(2,1)S(1)}, bf16[256,512]{1,0:T(8,128)(2,1)S(1)}, u32[]{:S(2)}, u32[]{:S(2)}) collective-permute-start(bf16[256,512]{1,0:T(8,128)(2,1)S(1)} %copy-done.201), channel_id=1, source_target_pairs={{0,4},{4,0},{8,12},{12,8},{1,5},{5,1},{9,13},{13,9},{2,6},{6,2},{1... | collective-permute-start | bytes 786440 | tf_op jit(solution)/shard_map/ppermute | solution.py:516
  804.9 33.5 %collective-permute-start.115 = (bf16[256,512]{1,0:T(8,128)(2,1)S(1)}, bf16[256,512]{1,0:T(8,128)(2,1)S(1)}, u32[]{:S(2)}, u32[]{:S(2)}) collective-permute-start(bf16[256,512]{1,0:T(8,128)(2,1)S(1)} %copy-done.203), channel_id=1, source_target_pairs={{0,12},{4,8},{8,4},{12,0},{1,13},{5,9},{9,5},{13,1},{2,14},{6,10},... | collective-permute-start | bytes 786440 | tf_op jit(solution)/shard_map/ppermute | solution.py:516
  816.6 32.7 %collective-permute-start.121 = (bf16[256,512]{1,0:T(8,128)(2,1)S(1)}, bf16[256,512]{1,0:T(8,128)(2,1)S(1)}, u32[]{:S(2)}, u32[]{:S(2)}) collective-permute-start(bf16[256,512]{1,0:T(8,128)(2,1)S(1)} %copy-done.199), channel_id=1, source_target_pairs={{0,8},{4,12},{8,0},{12,4},{1,9},{5,13},{9,1},{13,5},{2,10},{6,14},... | collective-permute-start | bytes 786440 | tf_op jit(solution)/shard_map/ppermute | solution.py:516
  818.3 32.4 %collective-permute-start.122 = (bf16[256,512]{1,0:T(8,128)(2,1)S(1)}, bf16[256,512]{1,0:T(8,128)(2,1)S(1)}, u32[]{:S(2)}, u32[]{:S(2)}) collective-permute-start(bf16[256,512]{1,0:T(8,128)(2,1)S(1)} %copy-done.197), channel_id=1, source_target_pairs={{0,12},{4,8},{8,4},{12,0},{1,13},{5,9},{9,5},{13,1},{2,14},{6,10},... | collective-permute-start | bytes 786440 | tf_op jit(solution)/shard_map/ppermute | solution.py:516
  838.4 25.6 %collective-permute-start.126 = (bf16[192,2048]{1,0:T(8,128)(2,1)S(1)}, bf16[192,2048]{1,0:T(8,128)(2,1)}, u32[]{:S(2)}, u32[]{:S(2)}) collective-permute-start(bf16[192,2048]{1,0:T(8,128)(2,1)S(1)} %copy-done.280), channel_id=1, source_target_pairs={{0,4},{4,0},{8,12},{12,8},{16,24},{20,28},{24,16},{28,20},{1,5},{5... | collective-permute-start | bytes 2359304 | tf_op jit(solution)/shard_map/ppermute | solution.py:782
  848.9 26.1 %collective-permute-start.110 = (bf16[256,1024]{1,0:T(8,128)(2,1)S(1)}, bf16[256,1024]{1,0:T(8,128)(2,1)S(1)}, u32[]{:S(2)}, u32[]{:S(2)}) collective-permute-start(bf16[256,1024]{1,0:T(8,128)(2,1)S(1)} %copy-done.260), channel_id=1, source_target_pairs={{0,8},{4,12},{8,0},{12,4},{16,20},{20,16},{24,28},{28,24},{1,9},{5... | collective-permute-start | bytes 1572872 | tf_op jit(solution)/shard_map/ppermute | solution.py:782
  849.3 30.2 %collective-permute-start.131 = (bf16[128,2048]{1,0:T(8,128)(2,1)S(1)}, bf16[128,2048]{1,0:T(8,128)(2,1)}, u32[]{:S(2)}, u32[]{:S(2)}) collective-permute-start(bf16[128,2048]{1,0:T(8,128)(2,1)S(1)} %shard_map.275), channel_id=1, source_target_pairs={{0,4},{4,0},{8,12},{12,8},{16,24},{20,28},{24,16},{28,20},{1,5},{5... | collective-permute-start | bytes 1572872 | tf_op jit(solution)/shard_map/ppermute | solution.py:782
  865.5 37.3 %collective-permute-start.134 = (bf16[2,192,2048]{2,1,0:T(8,128)(2,1)S(1)}, bf16[2,192,2048]{2,1,0:T(8,128)(2,1)S(1)}, u32[]{:S(2)}, u32[]{:S(2)}) collective-permute-start(bf16[2,192,2048]{2,1,0:T(8,128)(2,1)S(1)} %pad_maximum_fusion.6), channel_id=1, source_target_pairs={{0,8},{4,12},{8,0},{12,4},{16,20},{20,16},{24,28},{28,24},{1,9},{5... | collective-permute-start | bytes 4718600 | tf_op jit(solution)/shard_map/ppermute | solution.py:782
  875.7 27.7 %collective-permute-start.128 = (bf16[64,2048]{1,0:T(8,128)(2,1)S(1)}, bf16[64,2048]{1,0:T(8,128)(2,1)S(1)}, u32[]{:S(2)}, u32[]{:S(2)}) collective-permute-start(bf16[64,2048]{1,0:T(8,128)(2,1)S(1)} %add_convert_fusion.8), channel_id=1, source_target_pairs={{0,1},{1,2},{2,3},{3,0},{4,5},{5,6},{6,7},{7,4},{8,9},{9,10},{10,1... | collective-permute-start | bytes 786440 | tf_op jit(solution)/shard_map/ppermute | solution.py:511
  881.5 23.3 %collective-permute-start.132 = (bf16[64,2048]{1,0:T(8,128)(2,1)S(1)}, bf16[64,2048]{1,0:T(8,128)(2,1)S(1)}, u32[]{:S(2)}, u32[]{:S(2)}) collective-permute-start(bf16[64,2048]{1,0:T(8,128)(2,1)S(1)} %add_convert_fusion.7), channel_id=1, source_target_pairs={{0,1},{1,2},{2,3},{3,0},{4,5},{5,6},{6,7},{7,4},{8,9},{9,10},{10,1... | collective-permute-start | bytes 786440 | tf_op jit(solution)/shard_map/ppermute | solution.py:511
  882.8 35.5 %collective-permute-start.138 = (bf16[128,2048]{1,0:T(8,128)(2,1)}, bf16[128,2048]{1,0:T(8,128)(2,1)}, u32[]{:S(2)}, u32[]{:S(2)}) collective-permute-start(bf16[128,2048]{1,0:T(8,128)(2,1)} %pad_maximum_fusion.27), channel_id=1, source_target_pairs={{0,4},{4,0},{8,12},{12,8},{16,24},{20,28},{24,16},{28,20},{1,5},{5... | collective-permute-start | bytes 1572872 | tf_op jit(solution)/shard_map/ppermute | solution.py:782
  884.1 31.5 %collective-permute-start.133 = (bf16[64,2048]{1,0:T(8,128)(2,1)}, bf16[64,2048]{1,0:T(8,128)(2,1)}, u32[]{:S(2)}, u32[]{:S(2)}) collective-permute-start(bf16[64,2048]{1,0:T(8,128)(2,1)} %constant_dynamic-slice_fusion.1), channel_id=1, source_target_pairs={{0,8},{4,12},{8,0},{12,4},{16,20},{20,16},{24,28},{28,24},{1,9},{5... | collective-permute-start | bytes 786440 | tf_op jit(solution)/shard_map/ppermute | solution.py:782
  902.8 37.0 %collective-permute-start.127 = (bf16[512,1024]{1,0:T(8,128)(2,1)}, bf16[512,1024]{1,0:T(8,128)(2,1)}, u32[]{:S(2)}, u32[]{:S(2)}) collective-permute-start(bf16[512,1024]{1,0:T(8,128)(2,1)} %pad_maximum_fusion.23), channel_id=1, source_target_pairs={{0,4},{4,0},{8,12},{12,8},{16,24},{20,28},{24,16},{28,20},{1,5},{5... | collective-permute-start | bytes 3145736 | tf_op jit(solution)/shard_map/ppermute | solution.py:782
  903.4 31.7 %collective-permute-start.136 = (bf16[512,1024]{1,0:T(8,128)(2,1)}, bf16[512,1024]{1,0:T(8,128)(2,1)}, u32[]{:S(2)}, u32[]{:S(2)}) collective-permute-start(bf16[512,1024]{1,0:T(8,128)(2,1)} %shard_map.279), channel_id=1, source_target_pairs={{0,4},{4,0},{8,12},{12,8},{16,24},{20,28},{24,16},{28,20},{1,5},{5... | collective-permute-start | bytes 3145736 | tf_op jit(solution)/shard_map/ppermute | solution.py:782
  915.5 27.6 %collective-permute-start.145 = (bf16[64,2048]{1,0:T(8,128)(2,1)}, bf16[64,2048]{1,0:T(8,128)(2,1)S(1)}, u32[]{:S(2)}, u32[]{:S(2)}) collective-permute-start(bf16[64,2048]{1,0:T(8,128)(2,1)} %broadcast_select_fusion.27), channel_id=1, source_target_pairs={{0,0},{1,2},{2,1},{3,3},{4,4},{5,6},{6,5},{7,7},{8,8},{9,10},{10,9... | collective-permute-start | bytes 786440 | tf_op jit(solution)/shard_map/ppermute | solution.py:907
  939.1 28.8 %collective-permute-start.143 = (bf16[256,3072]{1,0:T(8,128)(2,1)S(1)}, bf16[256,3072]{1,0:T(8,128)(2,1)S(1)}, u32[]{:S(2)}, u32[]{:S(2)}) collective-permute-start(bf16[256,3072]{1,0:T(8,128)(2,1)S(1)} %copy-done.264), channel_id=1, source_target_pairs={{0,4},{4,0},{8,12},{12,8},{16,24},{20,28},{24,16},{28,20},{1,5},{5... | collective-permute-start | bytes 4718600 | tf_op jit(solution)/shard_map/ppermute | solution.py:782
  943.1 26.9 %collective-permute-start.140 = (bf16[256,2048]{1,0:T(8,128)(2,1)S(1)}, bf16[256,2048]{1,0:T(8,128)(2,1)S(1)}, u32[]{:S(2)}, u32[]{:S(2)}) collective-permute-start(bf16[256,2048]{1,0:T(8,128)(2,1)S(1)} %pad_maximum_fusion.24.refs_2_), channel_id=1, source_target_pairs={{0,16},{1,17},{2,18},{3,19},{4,20},{5,21},{6,22},{7,23},{8,24},{9,... | collective-permute-start | bytes 3145736 | tf_op jit(solution)/shard_map/ppermute | solution.py:506
  969.1 43.9 %collective-permute-start.158 = (bf16[2,256,3072]{2,1,0:T(8,128)(2,1)S(1)}, bf16[2,256,3072]{2,1,0:T(8,128)(2,1)S(1)}, u32[]{:S(2)}, u32[]{:S(2)}) collective-permute-start(bf16[2,256,3072]{2,1,0:T(8,128)(2,1)S(1)} %pad_maximum_fusion.3), channel_id=1, source_target_pairs={{0,8},{4,12},{8,0},{12,4},{16,20},{20,16},{24,28},{28,24},{1,9},{5... | collective-permute-start | bytes 9437192 | tf_op jit(solution)/shard_map/ppermute | solution.py:782
  987.8 25.1 %collective-permute-start.159 = (bf16[256,1024]{1,0:T(8,128)(2,1)S(1)}, bf16[256,1024]{1,0:T(8,128)(2,1)S(1)}, u32[]{:S(2)}, u32[]{:S(2)}) collective-permute-start(bf16[256,1024]{1,0:T(8,128)(2,1)S(1)} %add_convert_fusion.2), channel_id=1, source_target_pairs={{0,8},{4,12},{8,0},{12,4},{16,20},{20,16},{24,28},{28,24},{1,9},{5... | collective-permute-start | bytes 1572872 | tf_op jit(solution)/shard_map/ppermute | solution.py:782
  (479 other events, 6501.4 us)
Sparse Core Ops, SparseCore 0:
  10.2 48.5 all-gather.10
  60.9 56.7 all-gather.12
  437.1 42.2 reduce-scatter.4
  482.8 87.1 reduce-scatter.6
  571.7 48.8 all-gather.6
  622.3 70.1 all-gather.8
  723.0 49.8 reduce-scatter.8
  776.5 107.5 reduce-scatter.10

commit v4 on v3

--- a/solution.py
+++ b/solution.py
@@ -384,7 +384,7 @@
 START_COST = 0.9
 AHEAD = 10.0
 RING, LINKS, SWAP, SPARSE, NONE = range(5)
-RAW, TOP, OUTPUT, INPUT_GRAD, GAIN, GAINS, HALF, WHOLE, HOME, GATE_UP, DOWN, OUT, QKV = range(13)
+RAW, TOP, OUTPUT, INPUT_GRAD, GAIN, GAINS, HALF, WHOLE, HOME, LATE, GATE_UP, DOWN, OUT, QKV = range(14)
 CORES, CTX, MP = "section", "ctx", "mp"
 
 
@@ -847,6 +847,7 @@
     flag = core_bit(0, 2) == 0
     pair = jnp.stack([jnp.where(flag, share, got), jnp.where(flag, got, share)])
     driver.spend(1.5 + 2 * size)
+    driver.put((LATE, share.shape[1]), ())
     (got,) = yield Send(
         LINKS, [(joint_step(1, 2), pair)], 23.0 * size, 2.0 + 4 * size, slack + 6.0 * size
     )
@@ -883,7 +884,9 @@
     driver.put((HALF, name, layer), (half, other))
 
 
-def assemble_lane(driver, name, widths):
+def assemble_lane(driver, name, widths, after):
+    if after:
+        yield Need(after)
     first, second = yield Need((HALF, name, 0), (HALF, name, 1))
     core = lax.axis_index(CORES).astype(jnp.int32).reshape(1)
     whole = assemble(core, [*first, *second], widths)
@@ -1066,7 +1069,8 @@
             lane = matrix_lane(driver, name, layer, cost, way)
             driver.add(lane, 1 if urgent else 3, (name, layer), URGENT if urgent else 3.0)
     for name, _ in MATRICES:
-        driver.add(assemble_lane(driver, name, widths[name]), 2)
+        after = (LATE, 2 * ff) if name == DOWN and n_ctx == 4 else None
+        driver.add(assemble_lane(driver, name, widths[name], after), 2)
     driver.add(home_lane(driver, INPUT_GRAD), 1)
     driver.add(home_lane(driver, OUTPUT, ((HOME, INPUT_GRAD),)), 4)
     driver.add(gain_lane(driver), 2)

time: 1080 us -> 1090 us (level)
  starting transfers between devices: 121 us -> 132 us
    ppermute x20, waiting for transfers between devices: 61.9 us -> 74.9 us  [joint_step(): return lambda block: lax.ppermute(block, (CORES, CTX), route)]
    unnamed x712 -> x692, local copies, waits for them, and re-layouts: 37.9 us -> 35.8 us
  transfers between devices with their start and end apart: 171 -> 171, of which waited for: 87 -> 87; matrix products, arithmetic and copies ran while one was open for 11% -> 10% of each run, Pallas kernels for 24% -> 24%
where the time goes in v4:
time: 1090 us; the launch traced here: 1080 us
  waiting for transfers between devices  491 us (45%)
  Pallas kernels  278 us (26%)
  starting transfers between devices  132 us (12%)
  other arithmetic  110 us (10%)
  local copies, waits for them, and re-layouts  46.7 us (4%)
  between operations  22.3 us (2%)
    ppermute x84, waiting for transfers between devices, ring_step(): return lax.ppermute(block, MP, [(i, (i + 1) % count) for i in range(count)])  315 us
    pallas_call x24, Pallas kernels, kernel_call(): pl.pallas_call(whole, out_shape=out_shape, in_specs=[hbm] * (n_args + 2 *...  155 us
    pallas_call x20, Pallas kernels, piece_product(): pl.pallas_call(functools.partial(product_body, len(lefts), [len(group) fo...  91.6 us
    ppermute x20, waiting for transfers between devices, joint_step(): return lambda block: lax.ppermute(block, (CORES, CTX), route)  74.9 us
    ppermute x24, waiting for transfers between devices, across_ctx(): lax.ppermute(block, CTX, [(i, i ^ distance) for i in range(count)])  57.3 us
    unnamed x692, local copies, waits for them, and re-layouts  35.8 us
    all_gather x2, waiting for transfers between devices, gather_lane(): lax.all_gather(x, MP, axis=0, tiled=True)  35.7 us
    ppermute x24, starting transfers between devices, across_ctx(): lax.ppermute(block, CTX, [(i, i ^ distance) for i in range(count)])  35 us
  transfers between devices with their start and end apart: 171, of which 87 were waited for; matrix products, arithmetic and copies ran while one was open for 10% of the time, Pallas kernels for 24%

profile of v4, /device:TPU:0, one launch (start us, length us, event | category | flops | bytes accessed | tf_op | source)
XLA Modules:
  0.0 1080.0 jit_solution(13327227325229223719)
XLA Ops:
  23.0 35.7 %all-gather.11.cloned.1.call-done = bf16[1,512,2048]{2,1,0:T(8,128)(2,1)} async-done(((bf16[1,128,2048]{2,1,0:T(8,128)(2,1)}), bf16[1,512,2048]{2,1,0:T(8,128)(2,1)}) %all-gather.11.cloned.1.call-update) | async-done | bytes 2097168 | tf_op jit(solution)/shard_map/all_gather | solution.py:946
  97.0 10.0 collective-permute-done.9
  109.3 8.8 collective-permute-done.14
  118.2 5.7 collective-permute-done.13
  146.6 5.6 collective-permute-done.20
  157.9 5.6 collective-permute-done.22
  163.5 5.6 collective-permute-done.21
  170.1 8.6 shard_map.241
  182.6 8.6 shard_map.242
  192.3 10.1 collective-permute-done.26
  236.3 5.6 collective-permute-done.31
  241.9 5.6 collective-permute-done.34
  282.5 5.9 collective-permute-done.39
  322.9 5.7 collective-permute-done.50
  345.6 8.6 shard_map.247
  357.3 8.6 shard_map.248
  368.1 8.1 collective-permute-done.56
  386.6 10.5 shard_map.249
  398.8 10.6 shard_map.250
  414.2 7.2 shard_map.252
  430.8 6.1 shard_map.253
  437.4 10.9 %collective-permute-done.64 = bf16[64,2048]{1,0:T(8,128)(2,1)S(1)} collective-permute-done((bf16[64,2048]{1,0:T(8,128)(2,1)}, bf16[64,2048]{1,0:T(8,128)(2,1)S(1)}, u32[]{:S(2)}, u32[]{:S(2)}) %collective-permute-start.64) | collective-permute-done | bytes 262176 | tf_op jit(solution)/shard_map/ppermute | solution.py:511
  461.8 10.1 shard_map.254
  472.1 11.2 %collective-permute-done.66 = bf16[64,2048]{1,0:T(8,128)(2,1)S(1)} collective-permute-done((bf16[64,2048]{1,0:T(8,128)(2,1)}, bf16[64,2048]{1,0:T(8,128)(2,1)S(1)}, u32[]{:S(2)}, u32[]{:S(2)}) %collective-permute-start.66) | collective-permute-done | bytes 262176 | tf_op jit(solution)/shard_map/ppermute | solution.py:511
  494.6 6.1 collective-permute-done.72
  508.6 7.0 shard_map.255
  518.0 7.8 shard_map.256
  533.5 8.7 collective-permute-done.73.refs_2_
  627.0 6.0 collective-permute-done.89
  638.5 5.7 collective-permute-done.93
  651.9 11.6 %shard_map.265 = (bf16[256,1536]{1,0:T(8,128)(2,1)S(1)}, bf16[256,1536]{1,0:T(8,128)(2,1)S(1)}, bf16[64,2048]{1,0:T(8,128)(2,1)S(1)}, bf16[64,2048]{1,0:T(8,128)...) custom-call(bf16[256,2048]{1,0:T(8,128)(2,1)} %pad_maximum_fusion.19.refs_0_.refs_2_, ...), custom_call_target="tpu_custom_call" | custom-call | flops 4831838208 | bytes 24117248 | tf_op jit(solution)/shard_map/pallas_call | solution.py:71
  666.3 11.2 %shard_map.266 = (bf16[256,1536]{1,0:T(8,128)(2,1)S(1)}, bf16[256,1536]{1,0:T(8,128)(2,1)S(1)}, bf16[64,2048]{1,0:T(8,128)(2,1)S(1)}, bf16[64,2048]{1,0:T(8,128)...) custom-call(bf16[256,2048]{1,0:T(8,128)(2,1)} %pad_maximum_fusion.20.refs_0_.refs_3_, ...), custom_call_target="tpu_custom_call" | custom-call | flops 4831838208 | bytes 24117248 | tf_op jit(solution)/shard_map/pallas_call | solution.py:71
  682.8 7.2 shard_map.268
  704.9 6.1 collective-permute-done.101
  712.3 6.1 shard_map.269
  735.2 9.9 shard_map.270
  772.7 6.8 shard_map.271
  782.4 7.0 shard_map.272
  803.0 10.3 collective-permute-done.113.refs_2_
  836.7 7.5 collective-permute-done.121.refs_3_
  857.9 6.6 collective-permute-done.126
  871.9 14.1 %collective-permute-done.131 = bf16[128,2048]{1,0:T(8,128)(2,1)} collective-permute-done((bf16[128,2048]{1,0:T(8,128)(2,1)S(1)}, bf16[128,2048]{1,0:T(8,128)(2,1)}, u32[]{:S(2)}, u32[]{:S(2)}) %collective-permute-start.131) | collective-permute-done | bytes 524320 | tf_op jit(solution)/shard_map/ppermute | solution.py:782
  896.3 7.7 collective-permute-done.134
  952.2 17.4 %collective-permute-done.150 = bf16[256,3072]{1,0:T(8,128)(2,1)S(1)} collective-permute-done((bf16[256,3072]{1,0:T(8,128)(2,1)S(1)}, bf16[256,3072]{1,0:T(8,128)(2,1)S(1)}, u32[]{:S(2)}, u32[]{:S(2)}) %collective-permute-start.150) | collective-permute-done | bytes 1572896 | tf_op jit(solution)/shard_map/ppermute | solution.py:782
  973.0 8.2 shard_map.281
  988.8 26.4 %collective-permute-done.156 = bf16[256,1024]{1,0:T(8,128)(2,1)S(1)} collective-permute-done((bf16[256,1024]{1,0:T(8,128)(2,1)S(1)}, bf16[256,1024]{1,0:T(8,128)(2,1)S(1)}, u32[]{:S(2)}, u32[]{:S(2)}) %collective-permute-start.156) | collective-permute-done | bytes 524320 | tf_op jit(solution)/shard_map/ppermute | solution.py:782
  1033.0 8.4 collective-permute-start.154
  1052.6 15.7 %shard_map.283 = (f32[2048,1536]{1,0:T(8,128)}, f32[2048,1536]{1,0:T(8,128)}) custom-call(s32[1]{0:T(128)} %bitcast.26.place, bf16[1024,3072]{1,0:T(8,128)(2,1)} %pad_maximum_fusion.refs_0_, bf16[1024,3072]{1,0:T(8,128)(2,1)} %collective-permute-done.162.refs_1_, bf16[1024,3072]{1,0:T(8,128)(2,1)S(1)} %bitcast.95, ...), custom_call_target="tpu_custom_call" | custom-call | bytes 37748736 | tf_op jit(solution)/shard_map/pallas_call | solution.py:365
  (1248 shorter events, 609.0 us)
Async XLA Ops:
  7.2 51.5 %all-gather.11.cloned.1.call-start = ((), (), s32[]{:S(2)}) async-start(), calls=%async_computation.10 | async-start | bytes 2621440 | tf_op jit(solution)/shard_map/all_gather | solution.py:946
  9.4 126.3 %all-gather.13.cloned.1.call-start = ((), (), s32[]{:S(2)}) async-start(), calls=%async_computation.11 | async-start | bytes 2621440 | tf_op jit(solution)/shard_map/all_gather | solution.py:946
  9.4 49.4 %collective-permute-start.2 = (bf16[2048,1536]{1,0:T(8,128)(2,1)}, bf16[2048,1536]{1,0:T(8,128)(2,1)}, u32[]{:S(2)}, u32[]{:S(2)}) collective-permute-start(bf16[2048,1536]{1,0:T(8,128)(2,1)} %bitcast.100), channel_id=1, source_target_pairs={{0,16},{16,0},{1,17},{17,1},{2,18},{18,2},{3,19},{19,3},{4,20},{20... | collective-permute-start | bytes 18874376 | tf_op jit(solution)/shard_map/ppermute | solution.py:502
  9.9 48.8 %collective-permute-start.3 = (bf16[2048,1536]{1,0:T(8,128)(2,1)}, bf16[2048,1536]{1,0:T(8,128)(2,1)}, u32[]{:S(2)}, u32[]{:S(2)}) collective-permute-start(bf16[2048,1536]{1,0:T(8,128)(2,1)} %bitcast.109), channel_id=1, source_target_pairs={{0,16},{16,0},{1,17},{17,1},{2,18},{18,2},{3,19},{19,3},{4,20},{20... | collective-permute-start | bytes 18874376 | tf_op jit(solution)/shard_map/ppermute | solution.py:502
  10.0 48.8 %collective-permute-start.4 = (bf16[1536,2048]{1,0:T(8,128)(2,1)}, bf16[1536,2048]{1,0:T(8,128)(2,1)}, u32[]{:S(2)}, u32[]{:S(2)}) collective-permute-start(bf16[1536,2048]{1,0:T(8,128)(2,1)} %bitcast.118), channel_id=1, source_target_pairs={{0,16},{16,0},{1,17},{17,1},{2,18},{18,2},{3,19},{19,3},{4,20},{20... | collective-permute-start | bytes 18874376 | tf_op jit(solution)/shard_map/ppermute | solution.py:502
  14.2 44.6 %collective-permute-start = (bf16[2048,1024]{1,0:T(8,128)(2,1)}, bf16[2048,1024]{1,0:T(8,128)(2,1)}, u32[]{:S(2)}, u32[]{:S(2)}) collective-permute-start(bf16[2048,1024]{1,0:T(8,128)(2,1)} %pad_maximum_fusion.1.refs_3_.refs_8_), channel_id=1, source_target_pairs={{0,16},{16,0},{1,17},{17,1},{2,18},{18,2},{3,19},{19,3},{4,20},{20... | collective-permute-start | bytes 12582920 | tf_op jit(solution)/shard_map/ppermute | solution.py:502
  15.8 485.0 %reduce-scatter.5.cloned.1.call-start = ((), (), s32[]{:S(2)}) async-start(), calls=%async_computation.4 | async-start | bytes 3932160 | tf_op jit(solution)/shard_map/reduce_scatter | solution.py:474
  20.6 38.2 %collective-permute-start.1 = (bf16[512,2048]{1,0:T(8,128)(2,1)}, bf16[512,2048]{1,0:T(8,128)(2,1)}, u32[]{:S(2)}, u32[]{:S(2)}) collective-permute-start(bf16[512,2048]{1,0:T(8,128)(2,1)} %bitcast.127), channel_id=1, source_target_pairs={{0,16},{16,0},{1,17},{17,1},{2,18},{18,2},{3,19},{19,3},{4,20},{20... | collective-permute-start | bytes 6291464 | tf_op jit(solution)/shard_map/ppermute | solution.py:502
  421.4 40.3 %collective-permute-start.67 = (bf16[1024,3072]{1,0:T(8,128)(2,1)}, bf16[1024,3072]{1,0:T(8,128)(2,1)}, u32[]{:S(2)}, u32[]{:S(2)}) collective-permute-start(bf16[1024,3072]{1,0:T(8,128)(2,1)} %shard_map.252), channel_id=1, source_target_pairs={{0,16},{16,0},{1,17},{17,1},{2,18},{18,2},{3,19},{19,3},{4,20},{20... | collective-permute-start | bytes 18874376 | tf_op jit(solution)/shard_map/ppermute | solution.py:502
  436.9 159.4 %reduce-scatter.7.cloned.1.call-start = ((), (), s32[]{:S(2)}) async-start(), calls=%async_computation.5 | async-start | bytes 7864320 | tf_op jit(solution)/shard_map/reduce_scatter | solution.py:474
  471.9 161.1 %all-gather.7.cloned.1.call-start = ((), (), s32[]{:S(2)}) async-start(), calls=%async_computation.6 | async-start | bytes 3932160 | tf_op jit(solution)/shard_map/all_gather | solution.py:474
  505.8 241.8 %all-gather.9.cloned.1.call-start = ((), (), s32[]{:S(2)}) async-start(), calls=%async_computation.7 | async-start | bytes 7864320 | tf_op jit(solution)/shard_map/all_gather | solution.py:474
  529.0 33.7 %collective-permute-start.80 = (bf16[256,2048]{1,0:T(8,128)(2,1)}, bf16[256,2048]{1,0:T(8,128)(2,1)}, u32[]{:S(2)}, u32[]{:S(2)}) collective-permute-start(bf16[256,2048]{1,0:T(8,128)(2,1)} %shard_map.257), channel_id=1, source_target_pairs={{0,16},{16,0},{1,17},{17,1},{2,18},{18,2},{3,19},{19,3},{4,20},{20... | collective-permute-start | bytes 3145736 | tf_op jit(solution)/shard_map/ppermute | solution.py:502
  532.7 35.6 %collective-permute-start.77 = (bf16[256,512]{1,0:T(8,128)(2,1)}, bf16[256,512]{1,0:T(8,128)(2,1)}, u32[]{:S(2)}, u32[]{:S(2)}) collective-permute-start(bf16[256,512]{1,0:T(8,128)(2,1)} %get-tuple-element.538), channel_id=1, source_target_pairs={{0,4},{4,0},{8,12},{12,8},{1,5},{5,1},{9,13},{13,9},{2,6},{6,2},{1... | collective-permute-start | bytes 786440 | tf_op jit(solution)/shard_map/ppermute | solution.py:516
  542.2 26.0 %collective-permute-start.78 = (bf16[256,512]{1,0:T(8,128)(2,1)}, bf16[256,512]{1,0:T(8,128)(2,1)}, u32[]{:S(2)}, u32[]{:S(2)}) collective-permute-start(bf16[256,512]{1,0:T(8,128)(2,1)} %get-tuple-element.550), channel_id=1, source_target_pairs={{0,8},{4,12},{8,0},{12,4},{1,9},{5,13},{9,1},{13,5},{2,10},{6,14},... | collective-permute-start | bytes 786440 | tf_op jit(solution)/shard_map/ppermute | solution.py:516
  544.8 27.7 %collective-permute-start.79 = (bf16[256,512]{1,0:T(8,128)(2,1)}, bf16[256,512]{1,0:T(8,128)(2,1)}, u32[]{:S(2)}, u32[]{:S(2)}) collective-permute-start(bf16[256,512]{1,0:T(8,128)(2,1)} %get-tuple-element.551), channel_id=1, source_target_pairs={{0,12},{4,8},{8,4},{12,0},{1,13},{5,9},{9,5},{13,1},{2,14},{6,10},... | collective-permute-start | bytes 786440 | tf_op jit(solution)/shard_map/ppermute | solution.py:516
  583.9 23.8 %collective-permute-start.82 = (bf16[1024,1024]{1,0:T(8,128)(2,1)}, bf16[1024,1024]{1,0:T(8,128)(2,1)}, u32[]{:S(2)}, u32[]{:S(2)}) collective-permute-start(bf16[1024,1024]{1,0:T(8,128)(2,1)} %shard_map.261), channel_id=1, source_target_pairs={{0,16},{16,0},{1,17},{17,1},{2,18},{18,2},{3,19},{19,3},{4,20},{20... | collective-permute-start | bytes 6291464 | tf_op jit(solution)/shard_map/ppermute | solution.py:502
  584.2 37.7 %collective-permute-start.91 = (bf16[128,2048]{1,0:T(8,128)(2,1)}, bf16[128,2048]{1,0:T(8,128)(2,1)}, u32[]{:S(2)}, u32[]{:S(2)}) collective-permute-start(bf16[128,2048]{1,0:T(8,128)(2,1)} %copy-done.141), channel_id=1, source_target_pairs={{0,4},{4,0},{8,12},{12,8},{16,24},{20,28},{24,16},{28,20},{1,5},{5... | collective-permute-start | bytes 1572872 | tf_op jit(solution)/shard_map/ppermute | solution.py:782
  607.7 184.5 %reduce-scatter.9.cloned.1.call-start = ((), (), s32[]{:S(2)}) async-start(), calls=%async_computation.8 | async-start | bytes 3932160 | tf_op jit(solution)/shard_map/reduce_scatter | solution.py:474
  690.0 45.1 %collective-permute-start.105 = (bf16[1024,3072]{1,0:T(8,128)(2,1)}, bf16[1024,3072]{1,0:T(8,128)(2,1)}, u32[]{:S(2)}, u32[]{:S(2)}) collective-permute-start(bf16[1024,3072]{1,0:T(8,128)(2,1)} %shard_map.268), channel_id=1, source_target_pairs={{0,16},{16,0},{1,17},{17,1},{2,18},{18,2},{3,19},{19,3},{4,20},{20... | collective-permute-start | bytes 18874376 | tf_op jit(solution)/shard_map/ppermute | solution.py:502
  690.6 31.5 %collective-permute-start.92 = (bf16[768,2048]{1,0:T(8,128)(2,1)}, bf16[768,2048]{1,0:T(8,128)(2,1)}, u32[]{:S(2)}, u32[]{:S(2)}) collective-permute-start(bf16[768,2048]{1,0:T(8,128)(2,1)} %all-gather.7.cloned.1.call-done.refs_2_), channel_id=1, source_target_pairs={{0,16},{1,17},{2,18},{3,19},{4,20},{5,21},{6,22},{7,23},{8,24},{9,... | collective-permute-start | bytes 9437192 | tf_op jit(solution)/shard_map/ppermute | solution.py:506
  694.3 28.5 %collective-permute-start.86 = (bf16[512,1024]{1,0:T(8,128)(2,1)}, bf16[512,1024]{1,0:T(8,128)(2,1)}, u32[]{:S(2)}, u32[]{:S(2)}) collective-permute-start(bf16[512,1024]{1,0:T(8,128)(2,1)} %copy-done.64), channel_id=1, source_target_pairs={{0,4},{4,0},{8,12},{12,8},{16,24},{20,28},{24,16},{28,20},{1,5},{5... | collective-permute-start | bytes 3145736 | tf_op jit(solution)/shard_map/ppermute | solution.py:782
  711.7 33.4 %collective-permute-start.108 = (bf16[64,2048]{1,0:T(8,128)(2,1)}, bf16[64,2048]{1,0:T(8,128)(2,1)}, u32[]{:S(2)}, u32[]{:S(2)}) collective-permute-start(bf16[64,2048]{1,0:T(8,128)(2,1)} %constant_dynamic-slice_fusion.3), channel_id=1, source_target_pairs={{0,8},{4,12},{8,0},{12,4},{16,20},{20,16},{24,28},{28,24},{1,9},{5... | collective-permute-start | bytes 786440 | tf_op jit(solution)/shard_map/ppermute | solution.py:782
  722.8 193.8 %reduce-scatter.11.cloned.1.call-start = ((), (), s32[]{:S(2)}) async-start(), calls=%async_computation.9 | async-start | bytes 7864320 | tf_op jit(solution)/shard_map/reduce_scatter | solution.py:474
  747.6 52.7 %collective-permute-start.117 = (bf16[1024,3072]{1,0:T(8,128)(2,1)}, bf16[1024,3072]{1,0:T(8,128)(2,1)}, u32[]{:S(2)}, u32[]{:S(2)}) collective-permute-start(bf16[1024,3072]{1,0:T(8,128)(2,1)} %all-gather.9.cloned.1.call-done.refs_2_), channel_id=1, source_target_pairs={{0,16},{1,17},{2,18},{3,19},{4,20},{5,21},{6,22},{7,23},{8,24},{9,... | collective-permute-start | bytes 18874376 | tf_op jit(solution)/shard_map/ppermute | solution.py:506
  761.9 38.4 %collective-permute-start.116 = (bf16[64,2048]{1,0:T(8,128)(2,1)}, bf16[64,2048]{1,0:T(8,128)(2,1)}, u32[]{:S(2)}, u32[]{:S(2)}) collective-permute-start(bf16[64,2048]{1,0:T(8,128)(2,1)} %add_convert_fusion.11), channel_id=1, source_target_pairs={{0,8},{4,12},{8,0},{12,4},{16,20},{20,16},{24,28},{28,24},{1,9},{5... | collective-permute-start | bytes 786440 | tf_op jit(solution)/shard_map/ppermute | solution.py:782
  794.8 38.1 %collective-permute-start.123 = (bf16[256,2048]{1,0:T(8,128)(2,1)}, bf16[256,2048]{1,0:T(8,128)(2,1)}, u32[]{:S(2)}, u32[]{:S(2)}) collective-permute-start(bf16[256,2048]{1,0:T(8,128)(2,1)} %shard_map.273), channel_id=1, source_target_pairs={{0,16},{16,0},{1,17},{17,1},{2,18},{18,2},{3,19},{19,3},{4,20},{20... | collective-permute-start | bytes 3145736 | tf_op jit(solution)/shard_map/ppermute | solution.py:502
  794.9 31.0 %collective-permute-start.59 = (bf16[64,2048]{1,0:T(8,128)(2,1)}, bf16[64,2048]{1,0:T(8,128)(2,1)S(1)}, u32[]{:S(2)}, u32[]{:S(2)}) collective-permute-start(bf16[64,2048]{1,0:T(8,128)(2,1)} %add_convert_fusion.24), channel_id=1, source_target_pairs={{0,1},{1,2},{2,3},{3,0},{4,5},{5,6},{6,7},{7,4},{8,9},{9,10},{10,1... | collective-permute-start | bytes 786440 | tf_op jit(solution)/shard_map/ppermute | solution.py:511
  800.4 23.8 %collective-permute-start.115 = (bf16[256,512]{1,0:T(8,128)(2,1)}, bf16[256,512]{1,0:T(8,128)(2,1)S(1)}, u32[]{:S(2)}, u32[]{:S(2)}) collective-permute-start(bf16[256,512]{1,0:T(8,128)(2,1)} %copy-done.202), channel_id=1, source_target_pairs={{0,12},{4,8},{8,4},{12,0},{1,13},{5,9},{9,5},{13,1},{2,14},{6,10},... | collective-permute-start | bytes 786440 | tf_op jit(solution)/shard_map/ppermute | solution.py:516
  831.8 32.8 %collective-permute-start.126 = (bf16[192,2048]{1,0:T(8,128)(2,1)S(1)}, bf16[192,2048]{1,0:T(8,128)(2,1)S(1)}, u32[]{:S(2)}, u32[]{:S(2)}) collective-permute-start(bf16[192,2048]{1,0:T(8,128)(2,1)S(1)} %copy-done.274), channel_id=1, source_target_pairs={{0,4},{4,0},{8,12},{12,8},{16,24},{20,28},{24,16},{28,20},{1,5},{5... | collective-permute-start | bytes 2359304 | tf_op jit(solution)/shard_map/ppermute | solution.py:782
  835.8 32.3 %collective-permute-start.110 = (bf16[256,1024]{1,0:T(8,128)(2,1)S(1)}, bf16[256,1024]{1,0:T(8,128)(2,1)}, u32[]{:S(2)}, u32[]{:S(2)}) collective-permute-start(bf16[256,1024]{1,0:T(8,128)(2,1)S(1)} %copy-done.254), channel_id=1, source_target_pairs={{0,8},{4,12},{8,0},{12,4},{16,20},{20,16},{24,28},{28,24},{1,9},{5... | collective-permute-start | bytes 1572872 | tf_op jit(solution)/shard_map/ppermute | solution.py:782
  844.2 41.8 %collective-permute-start.131 = (bf16[128,2048]{1,0:T(8,128)(2,1)S(1)}, bf16[128,2048]{1,0:T(8,128)(2,1)}, u32[]{:S(2)}, u32[]{:S(2)}) collective-permute-start(bf16[128,2048]{1,0:T(8,128)(2,1)S(1)} %shard_map.275), channel_id=1, source_target_pairs={{0,4},{4,0},{8,12},{12,8},{16,24},{20,28},{24,16},{28,20},{1,5},{5... | collective-permute-start | bytes 1572872 | tf_op jit(solution)/shard_map/ppermute | solution.py:782
  864.6 25.8 %collective-permute-start.129 = (bf16[1024,1024]{1,0:T(8,128)(2,1)}, bf16[1024,1024]{1,0:T(8,128)(2,1)S(1)}, u32[]{:S(2)}, u32[]{:S(2)}) collective-permute-start(bf16[1024,1024]{1,0:T(8,128)(2,1)} %shard_map.277), channel_id=1, source_target_pairs={{0,16},{16,0},{1,17},{17,1},{2,18},{18,2},{3,19},{19,3},{4,20},{20... | collective-permute-start | bytes 6291464 | tf_op jit(solution)/shard_map/ppermute | solution.py:502
  864.9 39.1 %collective-permute-start.134 = (bf16[2,192,2048]{2,1,0:T(8,128)(2,1)S(1)}, bf16[2,192,2048]{2,1,0:T(8,128)(2,1)S(1)}, u32[]{:S(2)}, u32[]{:S(2)}) collective-permute-start(bf16[2,192,2048]{2,1,0:T(8,128)(2,1)S(1)} %pad_maximum_fusion.6), channel_id=1, source_target_pairs={{0,8},{4,12},{8,0},{12,4},{16,20},{20,16},{24,28},{28,24},{1,9},{5... | collective-permute-start | bytes 4718600 | tf_op jit(solution)/shard_map/ppermute | solution.py:782
  868.1 37.4 %collective-permute-start.128 = (bf16[64,2048]{1,0:T(8,128)(2,1)S(1)}, bf16[64,2048]{1,0:T(8,128)(2,1)S(1)}, u32[]{:S(2)}, u32[]{:S(2)}) collective-permute-start(bf16[64,2048]{1,0:T(8,128)(2,1)S(1)} %add_convert_fusion.8), channel_id=1, source_target_pairs={{0,1},{1,2},{2,3},{3,0},{4,5},{5,6},{6,7},{7,4},{8,9},{9,10},{10,1... | collective-permute-start | bytes 786440 | tf_op jit(solution)/shard_map/ppermute | solution.py:511
  889.7 29.8 %collective-permute-start.138 = (bf16[128,2048]{1,0:T(8,128)(2,1)}, bf16[128,2048]{1,0:T(8,128)(2,1)}, u32[]{:S(2)}, u32[]{:S(2)}) collective-permute-start(bf16[128,2048]{1,0:T(8,128)(2,1)} %pad_maximum_fusion.27), channel_id=1, source_target_pairs={{0,4},{4,0},{8,12},{12,8},{16,24},{20,28},{24,16},{28,20},{1,5},{5... | collective-permute-start | bytes 1572872 | tf_op jit(solution)/shard_map/ppermute | solution.py:782
  890.4 26.3 %collective-permute-start.133 = (bf16[64,2048]{1,0:T(8,128)(2,1)}, bf16[64,2048]{1,0:T(8,128)(2,1)}, u32[]{:S(2)}, u32[]{:S(2)}) collective-permute-start(bf16[64,2048]{1,0:T(8,128)(2,1)} %constant_dynamic-slice_fusion.1), channel_id=1, source_target_pairs={{0,8},{4,12},{8,0},{12,4},{16,20},{20,16},{24,28},{28,24},{1,9},{5... | collective-permute-start | bytes 786440 | tf_op jit(solution)/shard_map/ppermute | solution.py:782
  904.0 31.9 %collective-permute-start.127 = (bf16[512,1024]{1,0:T(8,128)(2,1)}, bf16[512,1024]{1,0:T(8,128)(2,1)}, u32[]{:S(2)}, u32[]{:S(2)}) collective-permute-start(bf16[512,1024]{1,0:T(8,128)(2,1)} %pad_maximum_fusion.23), channel_id=1, source_target_pairs={{0,4},{4,0},{8,12},{12,8},{16,24},{20,28},{24,16},{28,20},{1,5},{5... | collective-permute-start | bytes 3145736 | tf_op jit(solution)/shard_map/ppermute | solution.py:782
  905.5 24.9 %collective-permute-start.136 = (bf16[512,1024]{1,0:T(8,128)(2,1)}, bf16[512,1024]{1,0:T(8,128)(2,1)}, u32[]{:S(2)}, u32[]{:S(2)}) collective-permute-start(bf16[512,1024]{1,0:T(8,128)(2,1)} %shard_map.279), channel_id=1, source_target_pairs={{0,4},{4,0},{8,12},{12,8},{16,24},{20,28},{24,16},{28,20},{1,5},{5... | collective-permute-start | bytes 3145736 | tf_op jit(solution)/shard_map/ppermute | solution.py:782
  916.7 27.5 %collective-permute-start.141 = (bf16[64,2048]{1,0:T(8,128)(2,1)}, bf16[64,2048]{1,0:T(8,128)(2,1)S(1)}, u32[]{:S(2)}, u32[]{:S(2)}) collective-permute-start(bf16[64,2048]{1,0:T(8,128)(2,1)} %broadcast_select_fusion.27), channel_id=1, source_target_pairs={{0,0},{1,2},{2,1},{3,3},{4,4},{5,6},{6,5},{7,7},{8,8},{9,10},{10,9... | collective-permute-start | bytes 786440 | tf_op jit(solution)/shard_map/ppermute | solution.py:910
  942.7 27.0 %collective-permute-start.150 = (bf16[256,3072]{1,0:T(8,128)(2,1)S(1)}, bf16[256,3072]{1,0:T(8,128)(2,1)S(1)}, u32[]{:S(2)}, u32[]{:S(2)}) collective-permute-start(bf16[256,3072]{1,0:T(8,128)(2,1)S(1)} %copy-done.260), channel_id=1, source_target_pairs={{0,4},{4,0},{8,12},{12,8},{16,24},{20,28},{24,16},{28,20},{1,5},{5... | collective-permute-start | bytes 4718600 | tf_op jit(solution)/shard_map/ppermute | solution.py:782
  944.3 27.8 %collective-permute-start.149 = (bf16[256,1024]{1,0:T(8,128)(2,1)S(1)}, bf16[256,1024]{1,0:T(8,128)(2,1)S(1)}, u32[]{:S(2)}, u32[]{:S(2)}) collective-permute-start(bf16[256,1024]{1,0:T(8,128)(2,1)S(1)} %constant_dynamic-slice_fusion), channel_id=1, source_target_pairs={{0,8},{4,12},{8,0},{12,4},{16,20},{20,16},{24,28},{28,24},{1,9},{5... | collective-permute-start | bytes 1572872 | tf_op jit(solution)/shard_map/ppermute | solution.py:782
  945.1 40.2 %collective-permute-start.139 = (bf16[1024,1024]{1,0:T(8,128)(2,1)S(1)}, bf16[1024,1024]{1,0:T(8,128)(2,1)S(1)}, u32[]{:S(2)}, u32[]{:S(2)}) collective-permute-start(bf16[1024,1024]{1,0:T(8,128)(2,1)S(1)} %pad_maximum_fusion.4.refs_2_), channel_id=1, source_target_pairs={{0,16},{1,17},{2,18},{3,19},{4,20},{5,21},{6,22},{7,23},{8,24},{9,... | collective-permute-start | bytes 6291464 | tf_op jit(solution)/shard_map/ppermute | solution.py:506
  950.1 31.1 %collective-permute-start.147 = (bf16[128,2048]{1,0:T(8,128)(2,1)S(1)}, bf16[128,2048]{1,0:T(8,128)(2,1)S(1)}, u32[]{:S(2)}, u32[]{:S(2)}) collective-permute-start(bf16[128,2048]{1,0:T(8,128)(2,1)S(1)} %pad_maximum_fusion.28), channel_id=1, source_target_pairs={{0,4},{4,0},{8,12},{12,8},{16,24},{20,28},{24,16},{28,20},{1,5},{5... | collective-permute-start | bytes 1572872 | tf_op jit(solution)/shard_map/ppermute | solution.py:782
  970.2 45.1 %collective-permute-start.155 = (bf16[2,256,3072]{2,1,0:T(8,128)(2,1)S(1)}, bf16[2,256,3072]{2,1,0:T(8,128)(2,1)S(1)}, u32[]{:S(2)}, u32[]{:S(2)}) collective-permute-start(bf16[2,256,3072]{2,1,0:T(8,128)(2,1)S(1)} %pad_maximum_fusion.3), channel_id=1, source_target_pairs={{0,8},{4,12},{8,0},{12,4},{16,20},{20,16},{24,28},{28,24},{1,9},{5... | collective-permute-start | bytes 9437192 | tf_op jit(solution)/shard_map/ppermute | solution.py:782
  984.2 31.0 %collective-permute-start.156 = (bf16[256,1024]{1,0:T(8,128)(2,1)S(1)}, bf16[256,1024]{1,0:T(8,128)(2,1)S(1)}, u32[]{:S(2)}, u32[]{:S(2)}) collective-permute-start(bf16[256,1024]{1,0:T(8,128)(2,1)S(1)} %add_convert_fusion.2), channel_id=1, source_target_pairs={{0,8},{4,12},{8,0},{12,4},{16,20},{20,16},{24,28},{28,24},{1,9},{5... | collective-permute-start | bytes 1572872 | tf_op jit(solution)/shard_map/ppermute | solution.py:782
  1019.5 33.1 %collective-permute-start.162 = (bf16[1024,3072]{1,0:T(8,128)(2,1)}, bf16[1024,3072]{1,0:T(8,128)(2,1)}, u32[]{:S(2)}, u32[]{:S(2)}) collective-permute-start(bf16[1024,3072]{1,0:T(8,128)(2,1)} %pad_maximum_fusion.refs_0_), channel_id=1, source_target_pairs={{16,0},{17,1},{18,2},{19,3},{20,4},{21,5},{22,6},{23,7},{24,8},{25... | collective-permute-start | bytes 18874376 | tf_op jit(solution)/shard_map/ppermute | solution.py:506
  1021.8 25.4 %collective-permute-start.160 = (bf16[512,1024]{1,0:T(8,128)(2,1)S(1)}, bf16[512,1024]{1,0:T(8,128)(2,1)S(1)}, u32[]{:S(2)}, u32[]{:S(2)}) collective-permute-start(bf16[512,1024]{1,0:T(8,128)(2,1)S(1)} %pad_maximum_fusion.26), channel_id=1, source_target_pairs={{0,4},{4,0},{8,12},{12,8},{16,24},{20,28},{24,16},{28,20},{1,5},{5... | collective-permute-start | bytes 3145736 | tf_op jit(solution)/shard_map/ppermute | solution.py:782
  (469 other events, 6494.3 us)
Sparse Core Ops, SparseCore 0:
  10.2 48.5 all-gather.10
  60.9 56.8 all-gather.12
  437.0 42.2 reduce-scatter.4
  482.8 87.1 reduce-scatter.6
  571.7 48.7 all-gather.6
  622.2 70.1 all-gather.8
  722.9 52.6 reduce-scatter.8
  779.2 108.5 reduce-scatter.10
